TPU v7x, 128 devices: a whole 4x4x4 slice. The times are simulated.
128 devices in a mesh: dp: 8 (over z, core), tensor: 16 (over y, x).
Axes of the slice: x: 4, y: 4, z: 4, core: 2. Of those that a mesh axis runs over, the one named last changes fastest.
Arguments:
- h_in: bfloat16 [1024, 8192], P('dp'), may hold values from -6 to 6
- dout: bfloat16 [1024, 8192], P('dp'), may hold values from -6 to 6
- w_gate: bfloat16 [28672, 512], P('tensor'), may hold values from -0.25 to 0.25
- w_up: bfloat16 [28672, 512], P('tensor'), may hold values from -0.25 to 0.25
- w_down: bfloat16 [28672, 512], P('tensor'), may hold values from -0.125 to 0.125
- in_layout: int32 [224, 4], P('tensor'), may hold values from 0 to 63, all different within a row
- out_layout: int32 [224, 4], P('tensor'), may hold values from 0 to 63, all different within a row
Outputs:
- out: bfloat16 [1024, 8192], P('dp', 'tensor')
- dh: bfloat16 [1024, 8192], P('dp', 'tensor')
- grad_gate: float32 [224, 65536], P('tensor', 'dp')
- grad_up: float32 [224, 65536], P('tensor', 'dp')
- grad_down: float32 [224, 65536], P('tensor', 'dp')
Inputs may be any that keep to these rules, and one draw needn't show every extreme that they name: `in_layout`: each block row names 4 different blocks; every block is named by some block row. `out_layout`: each block row names 4 different blocks; every block is named by some block row.
All inputs are finite; a program needn't handle non-finite values.
Results may differ from a plain program's by a relative error of at most 0.018.
Values may be sent and summed in bfloat16 or wider, within the bound.
No kernel may reach another device: no remote copies, remote signals or barrier semaphores. Data moves between devices by JAX's collectives and lax.ppermute only.
A program may use at most 128 MiB of HBM per device.

v0:
```python
import jax
import jax.numpy as jnp
from jax import lax
from jax.sharding import PartitionSpec as P

D = 8192
BLK = 128
KB = 4


def block_sum(values, layout_flat, tokens, nblocks):
    empty = jnp.zeros((tokens, nblocks, BLK), jnp.float32)
    return empty.at[:, layout_flat].add(values).reshape(tokens, nblocks * BLK)


def shards(h_in, dout, w_gate, w_up, w_down, in_layout, out_layout):
    tokens = h_in.shape[0]
    rows_grp = in_layout.shape[0]
    nblocks = D // BLK
    lin_flat = in_layout.reshape(-1)
    lout_flat = out_layout.reshape(-1)
    wg = w_gate.reshape(rows_grp, BLK, KB * BLK)
    wu = w_up.reshape(rows_grp, BLK, KB * BLK)
    wd = w_down.reshape(rows_grp, BLK, KB * BLK)
    hx = jnp.take(h_in.reshape(tokens, nblocks, BLK), lin_flat, axis=1).reshape(
        tokens, rows_grp, KB * BLK
    )
    gate = jnp.einsum("trm,rim->tri", hx, wg, preferred_element_type=jnp.float32)
    up = jnp.einsum("trm,rim->tri", hx, wu, preferred_element_type=jnp.float32)
    sig = jax.nn.sigmoid(gate)
    act = gate * sig
    hidden = (act * up).astype(jnp.bfloat16)
    contrib = jnp.einsum("tri,rim->trm", hidden, wd, preferred_element_type=jnp.float32)
    partial_out = block_sum(contrib.reshape(tokens, rows_grp * KB, BLK), lout_flat, tokens, nblocks)
    partial_out = partial_out.astype(jnp.bfloat16).astype(jnp.float32)
    out = lax.psum_scatter(
        partial_out.astype(jnp.bfloat16), "tensor", scatter_dimension=1, tiled=True
    )
    dob = jnp.take(dout.reshape(tokens, nblocks, BLK), lout_flat, axis=1).reshape(
        tokens, rows_grp, KB * BLK
    )
    dhid = jnp.einsum("trm,rim->tri", dob, wd, preferred_element_type=jnp.float32)
    g_down = jnp.einsum("tri,trm->rim", hidden, dob, preferred_element_type=jnp.float32).reshape(
        rows_grp, -1
    )
    dgate = (dhid * up * sig * (1.0 + gate * (1.0 - sig))).astype(jnp.bfloat16)
    dup = (dhid * act).astype(jnp.bfloat16)
    g_gate = jnp.einsum("tri,trm->rim", dgate, hx, preferred_element_type=jnp.float32).reshape(
        rows_grp, -1
    )
    g_up = jnp.einsum("tri,trm->rim", dup, hx, preferred_element_type=jnp.float32).reshape(
        rows_grp, -1
    )
    summed_gate, summed_up, summed_down = (
        lax.psum(g_gate.astype(jnp.bfloat16), "dp").astype(jnp.float32),
        lax.psum(g_up.astype(jnp.bfloat16), "dp").astype(jnp.float32),
        lax.psum(g_down.astype(jnp.bfloat16), "dp").astype(jnp.float32),
    )
    share = summed_gate.shape[1] // lax.axis_size("dp")
    offset = lax.axis_index("dp") * share
    gate_part = lax.dynamic_slice_in_dim(summed_gate, offset, share, 1)
    up_part = lax.dynamic_slice_in_dim(summed_up, offset, share, 1)
    down_part = lax.dynamic_slice_in_dim(summed_down, offset, share, 1)
    dhx = jnp.einsum("tri,rim->trm", dgate, wg, preferred_element_type=jnp.float32)
    dhx = dhx + jnp.einsum("tri,rim->trm", dup, wu, preferred_element_type=jnp.float32)
    partial_dh = block_sum(dhx.reshape(tokens, rows_grp * KB, BLK), lin_flat, tokens, nblocks)
    partial_dh = partial_dh.astype(jnp.bfloat16).astype(jnp.float32)
    dh = lax.psum_scatter(
        partial_dh.astype(jnp.bfloat16), "tensor", scatter_dimension=1, tiled=True
    )
    return (out, dh, gate_part, up_part, down_part)


def solution(mesh):
    placed = (
        P("dp", None),
        P("dp", None),
        P("tensor", None),
        P("tensor", None),
        P("tensor", None),
        P("tensor", None),
        P("tensor", None),
    )
    return jax.shard_map(
        shards,
        mesh=mesh,
        in_specs=placed,
        out_specs=(
            P("dp", "tensor"),
            P("dp", "tensor"),
            P("tensor", "dp"),
            P("tensor", "dp"),
            P("tensor", "dp"),
        ),
        check_vma=False,
    )
```

profile of v0, /device:TPU:0, one launch (start us, length us, event | category | flops | bytes accessed | tf_op | source)
XLA Modules:
  0.0 268.9 jit_solution(1614522637076494654)
XLA Ops:
  9.9 4.1 %copy.44 = bf16[128,8192]{0,1:T(8,128)(2,1)} copy(bf16[128,8192]{1,0:T(8,128)(2,1)} %param.9) | data formatting | bytes 4194304 | tf_op args[0]
  14.0 4.1 %copy.45 = bf16[128,64,128]{2,0,1:T(8,128)(2,1)} copy(bf16[128,64,128]{0,2,1:T(8,128)(2,1)} %bitcast.76) | data formatting | bytes 4194304 | tf_op jit(solution)/shard_map/reshape | solution.py:25
  18.1 3.6 %gather_fusion = bf16[56,128,128]{2,1,0:T(8,128)(2,1)} fusion(bf16[128,64,128]{2,0,1:T(8,128)(2,1)} %copy.45, s32[1024]{0:T(1024)S(1)} %pad_clamp_fusion.1), kind=kCustom, calls=%fused_computation.clone | custom fusion | bytes 3670240 | tf_op jit(solution)/shard_map/jit(_take)/gather | solution.py:25
  21.7 3.0 %select_bitcast_fusion.1 = bf16[128,56,128]{2,0,1:T(8,128)(2,1)} fusion(bf16[56,128,128]{2,1,0:T(8,128)(2,1)} %gather_fusion, pred[56]{0:T(512)(128)(4,1)S(1)} %get-tuple-element.25), kind=kLoop, calls=%fused_computation.7 | loop fusion | flops 917504 | bytes 3670072 | tf_op jit(solution)/shard_map/jit(_take)/select_n | solution.py:25
  24.7 3.9 %copy.46 = bf16[128,56,128]{0,2,1:T(8,128)(2,1)} copy(bf16[128,56,128]{2,0,1:T(8,128)(2,1)} %select_bitcast_fusion.1) | data formatting | bytes 3670016 | tf_op jit(solution)/shard_map/jit(_take)/select_n | solution.py:25
  28.6 3.9 %convolution_bitcast_fusion.2 = f32[128,14,128]{2,0,1:T(8,128)} fusion(bf16[128,14,512]{0,2,1:T(8,128)(2,1)} %bitcast.62, bf16[14,128,512]{2,1,0:T(8,128)(2,1)} %bitcast.78), kind=kOutput, calls=%fused_computation.12 | convolution fusion | flops 234881024 | bytes 4587520 | tf_op jit(solution)/shard_map/trm,rim->tri/dot_general | solution.py:29
  34.2 4.1 %copy.54 = bf16[128,8192]{0,1:T(8,128)(2,1)} copy(bf16[128,8192]{1,0:T(8,128)(2,1)} %param.10) | data formatting | bytes 4194304 | tf_op args[1]
  38.3 4.1 %copy.55 = bf16[128,64,128]{2,0,1:T(8,128)(2,1)} copy(bf16[128,64,128]{0,2,1:T(8,128)(2,1)} %bitcast.77) | data formatting | bytes 4194304 | tf_op jit(solution)/shard_map/reshape | solution.py:39
  42.4 3.6 %gather_fusion.1 = bf16[56,128,128]{2,1,0:T(8,128)(2,1)} fusion(bf16[128,64,128]{2,0,1:T(8,128)(2,1)} %copy.55, s32[1024]{0:T(1024)S(1)} %pad_clamp_fusion), kind=kCustom, calls=%fused_computation.1.clone | custom fusion | bytes 3670240 | tf_op jit(solution)/shard_map/jit(_take)/gather | solution.py:39
  46.0 3.0 %select_bitcast_fusion = bf16[128,56,128]{2,0,1:T(8,128)(2,1)} fusion(bf16[56,128,128]{2,1,0:T(8,128)(2,1)} %gather_fusion.1, pred[56]{0:T(512)(128)(4,1)S(1)} %get-tuple-element.24), kind=kLoop, calls=%fused_computation.6 | loop fusion | flops 917504 | bytes 3670072 | tf_op jit(solution)/shard_map/jit(_take)/select_n | solution.py:39
  49.0 3.9 %copy.56 = bf16[128,56,128]{0,2,1:T(8,128)(2,1)} copy(bf16[128,56,128]{2,0,1:T(8,128)(2,1)} %select_bitcast_fusion) | data formatting | bytes 3670016 | tf_op jit(solution)/shard_map/jit(_take)/select_n | solution.py:39
  52.9 3.1 %multiply_convert_fusion = (bf16[128,14,128]{2,0,1:T(8,128)(2,1)S(1)}, bf16[128,14,128]{2,0,1:T(8,128)(2,1)S(1)}, bf16[128,14,128]{2,0,1:T(8,128)(2,1)S(1)}) fusion(f32[128,14,128]{2,0,1:T(8,128)} %convolution_bitcast_fusion.3, f32[128,14,128]{2,0,1:T(8,128)} %convolution_bitcast_fusion.2, bf16[128,14,512]{0,2,1:T(8,128)(2,1)} %bitcast.82, ...), kind=kOutput, calls=%fused_computation.14 | convolution fusion | flops 238321664 | bytes 6881280 | tf_op jit(solution)/shard_map/trm,rim->tri/dot_general | solution.py:42
  56.9 2.6 copy.78
  60.4 2.5 copy.79
  63.8 2.5 copy.80
  69.0 2.5 add_bitcast_fusion
  71.5 5.1 %copy.58 = f32[128,14,512]{0,2,1:T(8,128)} copy(f32[128,14,512]{2,0,1:T(8,128)} %add_bitcast_fusion) | data formatting | bytes 7340032 | tf_op jit(solution)/shard_map/add | solution.py:65
  76.6 5.5 %copy.59 = f32[56,128,128]{2,1,0:T(8,128)} copy(f32[56,128,128]{1,2,0:T(8,128)} %bitcast.66) | data formatting | bytes 7340032 | tf_op jit(solution)/shard_map/reshape | solution.py:66
  82.0 2.5 broadcast.43.clone.1
  84.5 13.4 %scatter_fusion.1 = f32[128,64,128]{2,0,1:T(8,128)} fusion(f32[128,64,128]{2,0,1:T(8,128)} %broadcast.43.clone.1, s32[56]{0:T(128)S(1)} %get-tuple-element.27, f32[56,128,128]{2,1,0:T(8,128)} %copy.59), kind=kCustom, calls=%fused_computation.3 | custom fusion | flops 917504 | bytes 11010272 | tf_op jit(solution)/shard_map/scatter-add | solution.py:13
  97.9 4.0 %convert_element_type.57 = bf16[128,64,128]{2,0,1:T(8,128)(2,1)} convert(f32[128,64,128]{2,0,1:T(8,128)} %scatter_fusion.1) | non-fusion elementwise | flops 1048576 | bytes 6291456 | tf_op jit(solution)/shard_map/convert_element_type | solution.py:67
  101.9 4.1 %copy.60 = bf16[128,64,128]{0,2,1:T(8,128)(2,1)} copy(bf16[128,64,128]{2,0,1:T(8,128)(2,1)} %convert_element_type.57) | data formatting | bytes 4194304 | tf_op jit(solution)/shard_map/convert_element_type | solution.py:67
  106.1 2.5 convolution_bitcast_fusion
  108.6 5.1 %copy.49 = f32[128,14,512]{0,2,1:T(8,128)} copy(f32[128,14,512]{2,0,1:T(8,128)} %convolution_bitcast_fusion) | data formatting | bytes 7340032 | tf_op jit(solution)/shard_map/tri,rim->trm/transpose | solution.py:33
  113.7 5.2 %copy.50 = f32[56,128,128]{2,1,0:T(8,128)} copy(f32[56,128,128]{1,2,0:T(8,128)} %bitcast.67) | data formatting | bytes 7340032 | tf_op jit(solution)/shard_map/reshape | solution.py:34
  118.9 2.5 broadcast.43.clone
  121.4 13.5 %scatter_fusion = f32[128,64,128]{2,0,1:T(8,128)} fusion(f32[128,64,128]{2,0,1:T(8,128)} %broadcast.43.clone, s32[56]{0:T(128)S(1)} %get-tuple-element.26, f32[56,128,128]{2,1,0:T(8,128)} %copy.50), kind=kCustom, calls=%fused_computation.2 | custom fusion | flops 917504 | bytes 11010272 | tf_op jit(solution)/shard_map/scatter-add | solution.py:13
  134.9 4.0 %convert_element_type.53 = bf16[128,64,128]{2,0,1:T(8,128)(2,1)} convert(f32[128,64,128]{2,0,1:T(8,128)} %scatter_fusion) | non-fusion elementwise | flops 1048576 | bytes 6291456 | tf_op jit(solution)/shard_map/convert_element_type | solution.py:35
  138.9 4.2 %copy.51 = bf16[128,64,128]{0,2,1:T(8,128)(2,1)} copy(bf16[128,64,128]{2,0,1:T(8,128)(2,1)} %convert_element_type.53) | data formatting | bytes 4194304 | tf_op jit(solution)/shard_map/convert_element_type | solution.py:35
  143.1 10.8 %all-reduce.3.cloned.1.call-done = (bf16[14,65536]{1,0:T(8,128)(2,1)}, bf16[14,65536]{1,0:T(8,128)(2,1)}, bf16[14,65536]{1,0:T(8,128)(2,1)}) async-done(((bf16[14,65536]{1,0:T(8,128)(2,1)}, bf16[14,65536]{1,0:T(8,128)(2,1)}, bf16[14,65536]{1,0:T(8,128)(2,1)}), (bf16[14,65536]{1,0:T(8,128)(2,1)}, bf16[14,65536]{1,0:T(8,128)(2,1)}, bf16[14,65536]{1,0:T(8,128)(2,1)})) %all-reduce.3.cloned.1.call-update) | async-done | bytes 5505040 | tf_op jit(solution)/shard_map/psum | solution.py:55
  159.2 23.5 %reduce-scatter.5.cloned.1.call-done = bf16[128,512]{0,1:T(8,128)(2,1)} async-done(((bf16[128,8192]{0,1:T(8,128)(2,1)}), bf16[128,512]{0,1:T(8,128)(2,1)}) %reduce-scatter.5.cloned.1.call-update) | async-done | bytes 131088 | tf_op jit(solution)/shard_map/reduce_scatter | solution.py:68
  184.4 75.4 %reduce-scatter.3.cloned.1.call-done = bf16[128,512]{0,1:T(8,128)(2,1)} async-done(((bf16[128,8192]{0,1:T(8,128)(2,1)}), bf16[128,512]{0,1:T(8,128)(2,1)}) %reduce-scatter.3.cloned.1.call-update) | async-done | bytes 131088 | tf_op jit(solution)/shard_map/reduce_scatter | solution.py:36
  (42 shorter events, 17.8 us)
Async XLA Ops:
  8.0 44.9 %copy-start = (bf16[1792,512]{1,0:T(8,128)(2,1)S(1)}, bf16[1792,512]{1,0:T(8,128)(2,1)}, u32[]{:S(2)}) copy-start(bf16[1792,512]{1,0:T(8,128)(2,1)} %param.13) | copy-start | bytes 5505028
  8.0 145.9 %all-reduce.3.cloned.1.call-start = ((), (), s32[]{:S(2)}) async-start(), calls=%async_computation.4 | async-start | bytes 12582912 | tf_op jit(solution)/shard_map/psum | solution.py:55
  28.6 3.9 %copy-start.1 = (bf16[128,56,128]{0,2,1:T(8,128)(2,1)S(1)}, bf16[128,56,128]{0,2,1:T(8,128)(2,1)}, u32[]{:S(2)}) copy-start(bf16[128,56,128]{0,2,1:T(8,128)(2,1)} %copy.46) | copy-start | bytes 5505028
  28.6 3.9 %copy-start.4 = (bf16[1792,512]{1,0:T(8,128)(2,1)S(1)}, bf16[1792,512]{1,0:T(8,128)(2,1)}, u32[]{:S(2)}) copy-start(bf16[1792,512]{1,0:T(8,128)(2,1)} %param.11) | copy-start | bytes 5505028
  52.8 3.1 %copy-start.2 = (bf16[128,56,128]{0,2,1:T(8,128)(2,1)S(1)}, bf16[128,56,128]{0,2,1:T(8,128)(2,1)}, u32[]{:S(2)}) copy-start(bf16[128,56,128]{0,2,1:T(8,128)(2,1)} %copy.46) | copy-start | bytes 5505028
  60.4 2.5 copy-start.5
  66.3 116.4 %reduce-scatter.5.cloned.1.call-start = ((), (), s32[]{:S(2)}) async-start(), calls=%async_computation.3 | async-start | bytes 2228224 | tf_op jit(solution)/shard_map/reduce_scatter | solution.py:68
  66.7 2.3 copy-start.3
  106.0 153.7 %reduce-scatter.3.cloned.1.call-start = ((), (), s32[]{:S(2)}) async-start(), calls=%async_computation.2 | async-start | bytes 2228224 | tf_op jit(solution)/shard_map/reduce_scatter | solution.py:36
Sparse Core Ops, SparseCore 0:
  66.4 87.4 all-reduce.2
Sparse Core Ops, SparseCore 1:
  106.1 76.5 reduce-scatter.4
  186.2 73.5 reduce-scatter.2
where the time goes:
time: 270 us; the launch traced here: 269 us
  waiting for transfers between devices  110 us (41%)
  local copies, waits for them, and re-layouts  79.1 us (29%)
  other arithmetic  46.2 us (17%)
  matrix products  18 us (7%)
  between operations  15.6 us (6%)
    reduce_scatter x1, waiting for transfers between devices, shards(): lax.psum_scatter(partial_out.astype(jnp.bfloat16), 'tensor', scatter_dime...  75.4 us
    scatter-add x2, other arithmetic, block_sum(): return empty.at[:, layout_flat].add(values).reshape(tokens, nblocks * BLK)  27 us
    reduce_scatter x1, waiting for transfers between devices, shards(): lax.psum_scatter(partial_dh.astype(jnp.bfloat16), 'tensor', scatter_dimen...  23.5 us
    unnamed x24, local copies, waits for them, and re-layouts  21.4 us
    psum x1, waiting for transfers between devices, shards(): lax.psum(g_gate.astype(jnp.bfloat16), 'dp').astype(jnp.float32)  10.8 us
    reshape x1, local copies, waits for them, and re-layouts, shards(): dhx.reshape(tokens, rows_grp * KB, BLK)  5.46 us
  transfers between devices with their start and end apart: 3, of which 3 were waited for; matrix products, arithmetic and copies ran while one was open for 31% of the time, Pallas kernels for 0%

commit v1 on v0

v1 whole, which is shorter than its diff:
```python
import jax
import jax.numpy as jnp
from jax import lax
from jax.experimental import pallas as pl
from jax.experimental.pallas import tpu as pltpu
from jax.sharding import PartitionSpec as P

D = 8192
BLK = 128
KB = 4
W = KB * BLK
NBLK = D // BLK
ROWS = 14
TOK = 128
AXES = ("dp", "tensor")
F32 = jnp.float32
BF16 = jnp.bfloat16
NT = (((1,), (1,)), ((), ()))


def pairs(axis, step):
    out = []
    for d in range(128):
        dp, t = divmod(d, 16)
        z, c = divmod(dp, 2)
        y, x = divmod(t, 4)
        m = 1 if (c == 0) == (step == 0) else 3
        if axis == "x":
            x ^= m
        elif axis == "y":
            y ^= m
        elif axis == "z":
            z ^= m
        else:
            c ^= 1
        out.append((d, (z * 2 + c) * 16 + y * 4 + x))
    return out


def send(a, axis, step=0):
    return lax.ppermute(a, AXES, pairs(axis, step))


def ring_order(me, core):
    first = 1 + 2 * core
    return (me ^ first, me ^ 2, me, me ^ (first ^ 2))


def dot(a, b, dims=None):
    if dims is None:
        return jnp.dot(a, b, preferred_element_type=F32)
    return lax.dot_general(a, b, dims, preferred_element_type=F32)


def gather_cols(ref, lay, r):
    return jnp.concatenate(
        [ref[:, pl.ds(pl.multiple_of(lay[r, k] * BLK, BLK), BLK)] for k in range(KB)], axis=1
    )


def split_units(pos, act, tmp, keep, give, a, wide):
    z, c = pos[0], pos[1]
    tmp[...] = act.T.reshape(8, 16, TOK)
    for q, own in enumerate(ring_order(z, c)):
        keep[a, 0, q] = tmp[own * 2 + c]
    for q, own in enumerate(ring_order(z, 1 - c)):
        give[a, 0, q] = tmp[own * 2 + 1 - c]


def emit_chunks(acc, outer, inner, transposed, sent, kept):
    for p in range(4):
        dst = sent if p < 2 else kept
        for q in range(4):
            y, x = (inner[q], outer[p]) if transposed else (outer[p], inner[q])
            base = (y * 4 + x) * 4
            for j in range(4):
                dst[p % 2, q, :, j * BLK : (j + 1) * BLK] = acc[base + j].astype(BF16)


def forward_kernel(pos, lin, lout, h, wg, wu, wd, a_out, b_out, keep, give, sent, kept, acc, tmp):
    r = pl.program_id(0)

    @pl.when(r == 0)
    def _():
        acc[...] = jnp.zeros_like(acc)

    hx = gather_cols(h, lin, r)
    gate = dot(hx, wg[...], NT)
    up = dot(hx, wu[...], NT)
    sig = jax.nn.sigmoid(gate)
    silu = gate * sig
    hidden = (silu * up).astype(BF16)
    a_out[0] = up * sig * (1.0 + gate * (1.0 - sig))
    b_out[0] = silu
    part = dot(hidden, wd[...])
    for k in range(KB):
        acc[lout[r, k]] += part[:, k * BLK : (k + 1) * BLK]
    split_units(pos, hidden, tmp, keep, give, 0, 1)

    @pl.when(r == ROWS - 1)
    def _():
        xs, ys = ring_order(pos[3], pos[1]), ring_order(pos[2], pos[1])
        emit_chunks(acc, xs, ys, True, sent, kept)


def backward_kernel(pos, lin, lout, dout, wg, wu, wd, a_in, b_in, keep, give, sent, kept, acc, tmp):
    r = pl.program_id(0)

    @pl.when(r == 0)
    def _():
        acc[...] = jnp.zeros_like(acc)

    dob = gather_cols(dout, lout, r)
    dhid = dot(dob, wd[...], NT)
    dgate = (dhid * a_in[0]).astype(BF16)
    dup = (dhid * b_in[0]).astype(BF16)
    part = dot(dgate, wg[...]) + dot(dup, wu[...])
    for k in range(KB):
        acc[lin[r, k]] += part[:, k * BLK : (k + 1) * BLK]
    split_units(pos, dgate, tmp, keep, give, 0, 2)
    split_units(pos, dup, tmp, keep, give, 1, 2)

    @pl.when(r == ROWS - 1)
    def _():
        xs, ys = ring_order(pos[3], pos[1]), ring_order(pos[2], pos[1])
        emit_chunks(acc, ys, xs, False, sent, kept)


def grads_kernel(lin, lout, h0, h1, d0, d1, hid0, hid1, dg0, dg1, sent, kept):
    r = pl.program_id(0)
    hx = jnp.concatenate([gather_cols(h0, lin, r), gather_cols(h1, lin, r)], axis=0)
    dob = jnp.concatenate([gather_cols(d0, lout, r), gather_cols(d1, lout, r)], axis=0)
    hid = jnp.concatenate([hid0[...].reshape(64, TOK), hid1[...].reshape(64, TOK)], axis=1)
    dgu = jnp.concatenate([dg0[...].reshape(128, TOK), dg1[...].reshape(128, TOK)], axis=1)
    g_in = dot(dgu, hx).astype(BF16).reshape(2, 4, 16, W)
    g_down = dot(hid, dob).astype(BF16).reshape(4, 16, W)
    for q in range(4):
        dst = sent if q < 2 else kept
        dst[q % 2, 0, 0] = g_in[0, q]
        dst[q % 2, 1, 0] = g_in[1, q]
        dst[q % 2, 2, 0] = g_down[q]


def finish_kernel(own, r1, r2, gate, up, down, tmp):
    for g, out in enumerate((gate, up, down)):
        total = own[0, g].astype(F32) + r1[0, g].astype(F32) + r2[g].astype(F32)
        total = total.reshape(ROWS * 16, W)
        for k in range(KB):
            tmp[k] = total[:, k * BLK : (k + 1) * BLK]
        for i in range(16):
            for k in range(KB):
                at = i * W + k * BLK
                out[:, at : at + BLK] = tmp[k, pl.ds(i, ROWS, stride=16), :]


def const(*shape):
    return pl.BlockSpec(shape, lambda r, *_: (0,) * len(shape))


def per_row(*shape, at=0):
    return pl.BlockSpec(shape, lambda r, *_: tuple(r if d == at else 0 for d in range(len(shape))))


PARAMS = pltpu.CompilerParams(vmem_limit_bytes=48 * 2**20, dimension_semantics=("arbitrary",))


def pass_call(kernel, n_act, tokens, ops, args, extra_in, extra_out):
    act = jax.ShapeDtypeStruct((n_act, ROWS, 4, 16, TOK), BF16)
    chunks = jax.ShapeDtypeStruct((2, 4, TOK, W), BF16)
    act_spec = per_row(n_act, 1, 4, 16, TOK, at=1)
    return pl.pallas_call(
        kernel,
        grid_spec=pltpu.PrefetchScalarGridSpec(
            num_scalar_prefetch=3,
            grid=(ROWS,),
            in_specs=[const(TOK, D)] + [per_row(BLK, W)] * 3 + [per_row(1, BLK, BLK)] * extra_in,
            out_specs=[per_row(1, TOK, BLK)] * extra_out
            + [act_spec, act_spec, const(2, 4, TOK, W), const(2, 4, TOK, W)],
            scratch_shapes=[pltpu.VMEM((NBLK, TOK, BLK), F32), pltpu.VMEM((8, 16, TOK), BF16)],
        ),
        out_shape=[jax.ShapeDtypeStruct((ROWS, TOK, BLK), F32)] * extra_out + [act, act, chunks, chunks],
        compiler_params=PARAMS,
        cost_estimate=pl.CostEstimate(
            flops=3 * 2 * TOK * ROWS * BLK * W, bytes_accessed=16 * 2**20, transcendentals=0
        ),
    )(*args)


def grads_call(lin, lout, h0, h1, d0, d1, hid0, hid1, dg0, dg1):
    out = jax.ShapeDtypeStruct((2, 3, ROWS, 16, W), BF16)
    return pl.pallas_call(
        grads_kernel,
        grid_spec=pltpu.PrefetchScalarGridSpec(
            num_scalar_prefetch=2,
            grid=(ROWS,),
            in_specs=[const(TOK, D)] * 4
            + [per_row(1, 1, 4, 16, TOK, at=1)] * 2
            + [per_row(2, 1, 4, 16, TOK, at=1)] * 2,
            out_specs=[per_row(2, 3, 1, 16, W, at=2)] * 2,
        ),
        out_shape=[out, out],
        compiler_params=PARAMS,
        cost_estimate=pl.CostEstimate(
            flops=3 * 2 * TOK * ROWS * BLK * W, bytes_accessed=16 * 2**20, transcendentals=0
        ),
    )(lin, lout, h0, h1, d0, d1, hid0, hid1, dg0, dg1)


def finish_call(own, r1, r2):
    out = jax.ShapeDtypeStruct((ROWS, 16 * W), F32)
    first = pl.BlockSpec((1, 3, ROWS, 16, W), lambda i: (0, 0, 0, 0, 0))
    return pl.pallas_call(
        finish_kernel,
        grid=(1,),
        in_specs=[first, first, pl.BlockSpec((3, ROWS, 16, W), lambda i: (0, 0, 0, 0))],
        out_specs=[pl.BlockSpec((ROWS, 16 * W), lambda i: (0, 0))] * 3,
        out_shape=[out] * 3,
        scratch_shapes=[pltpu.VMEM((KB, ROWS * 16, BLK), F32)],
        compiler_params=PARAMS,
    )(own, r1, r2)


def add(*terms):
    return sum(t.astype(F32) for t in terms).astype(BF16)


def ring_pair(sent, kept, first, second):
    r1 = send(sent, first, 0)
    r2 = send(add(kept[1], r1[1]), first, 1)
    mid = add(kept[0], r1[0], r2)
    r3 = send(mid[0:2], second, 0)
    r4 = send(add(mid[3], r3[1]), second, 1)
    return add(mid[2], r3[0], r4)


def shards(h_in, dout, w_gate, w_up, w_down, in_layout, out_layout):
    dp, t = lax.axis_index("dp"), lax.axis_index("tensor")
    pos = jnp.stack([dp // 2, dp % 2, t // 4, t % 4]).astype(jnp.int32)
    h_other = send(h_in, "core")
    d_other = send(dout, "core")
    a, b, hid_keep, hid_give, p_sent, p_kept = pass_call(
        forward_kernel, 1, TOK, None, (pos, in_layout, out_layout, h_in, w_gate, w_up, w_down), 0, 2
    )
    dg_keep, dg_give, q_sent, q_kept = pass_call(
        backward_kernel, 2, TOK, None, (pos, in_layout, out_layout, dout, w_gate, w_up, w_down, a, b), 2, 0
    )
    hid_other = send(hid_give, "core")
    dg_other = send(dg_give, "core")
    g_sent, g_kept = grads_call(
        in_layout, out_layout, h_in, h_other, dout, d_other, hid_keep, hid_other, dg_keep, dg_other
    )
    g1 = send(g_sent, "z", 0)
    g2 = send(add(g_kept[1], g1[1]), "z", 1)
    g_gate, g_up, g_down = finish_call(g_kept, g1, g2)
    out = ring_pair(p_sent, p_kept, "x", "y")
    dh = ring_pair(q_sent, q_kept, "y", "x")
    return (out, dh, g_gate, g_up, g_down)


def solution(mesh):
    rows = P("tensor", None)
    return jax.shard_map(
        shards,
        mesh=mesh,
        in_specs=(P("dp", None), P("dp", None), rows, rows, rows, rows, rows),
        out_specs=(P("dp", "tensor"), P("dp", "tensor")) + (P("tensor", "dp"),) * 3,
        check_vma=False,
    )
```

time: 270 us -> 82.6 us (0.31)
  waiting for transfers between devices: 110 us -> 21.9 us
  local copies, waits for them, and re-layouts: 79.1 us -> 2.91 us
  other arithmetic: 46.2 us -> 2.5 us
  Pallas kernels: 0 us -> 37 us
  matrix products: 18 us -> 0 us
  starting transfers between devices: 0.31 us -> 16.9 us
  between operations: 15.6 us -> 0.74 us
    reduce_scatter x2 -> x0, waiting for transfers between devices: 98.9 us -> none  [the longest x1 75.4 us: shards(): lax.psum_scatter(partial_out.astype(jnp.bfloat16), 'tensor', scatter_dime...]
    pallas_call x0 -> x4, Pallas kernels: none -> 37 us  [the longest x2 26.1 us: pass_call(): pl.pallas_call(kernel, grid_spec=pltpu.PrefetchScalarGridSpec(num_scalar_...]
    scatter-add x2 -> x0, other arithmetic: 27 us -> none  [block_sum(): return empty.at[:, layout_flat].add(values).reshape(tokens, nblocks * BLK)]
    ppermute x0 -> x14, waiting for transfers between devices: none -> 21.9 us  [send(): return lax.ppermute(a, AXES, pairs(axis, step))]
    reshape x8 -> x0, local copies, waits for them, and re-layouts: 19.2 us -> none  [the longest x1 5.46 us: shards(): dhx.reshape(tokens, rows_grp * KB, BLK)]
    unnamed x24 -> x4, local copies, waits for them, and re-layouts: 21.4 us -> 2.87 us
    dot_general x9 -> x0, matrix products: 18 us -> none  [the longest x1 3.91 us: shards(): up = jnp.einsum('trm,rim->tri', hx, wu, preferred_element_type=jnp.float32)]
    ppermute x0 -> x14, starting transfers between devices: none -> 16.9 us  [send(): return lax.ppermute(a, AXES, pairs(axis, step))]
  transfers between devices with their start and end apart: 3 -> 14, of which waited for: 3 -> 8; matrix products, arithmetic and copies ran while one was open for 31% -> 5% of each run, Pallas kernels for 0% -> 43%
where the time goes in v1:
time: 82.6 us; the launch traced here: 82 us
  Pallas kernels  37 us (45%)
  waiting for transfers between devices  21.9 us (27%)
  starting transfers between devices  16.9 us (20%)
  local copies, waits for them, and re-layouts  2.91 us (4%)
  other arithmetic  2.5 us (3%)
    pallas_call x2, Pallas kernels, pass_call(): pl.pallas_call(kernel, grid_spec=pltpu.PrefetchScalarGridSpec(num_scalar_...  26.1 us
    ppermute x14, waiting for transfers between devices, send(): return lax.ppermute(a, AXES, pairs(axis, step))  21.9 us
    ppermute x14, starting transfers between devices, send(): return lax.ppermute(a, AXES, pairs(axis, step))  16.9 us
    pallas_call x1, Pallas kernels, grads_call(): pl.pallas_call(grads_kernel, grid_spec=pltpu.PrefetchScalarGridSpec(num_s...  9.14 us
    unnamed x4, local copies, waits for them, and re-layouts  2.87 us
    convert_element_type x9, other arithmetic, add(): return sum((t.astype(F32) for t in terms)).astype(BF16)  2.42 us
    pallas_call x1, Pallas kernels, finish_call(): pl.pallas_call(finish_kernel, grid=(1,), in_specs=[first, first, pl.Block...  1.78 us
  transfers between devices with their start and end apart: 14, of which 8 were waited for; matrix products, arithmetic and copies ran while one was open for 5% of the time, Pallas kernels for 43%

profile of v1, /device:TPU:0, one launch (start us, length us, event | category | flops | bytes accessed | tf_op | source)
XLA Modules:
  0.0 82.0 jit_solution(9694752155994049349)
XLA Ops:
  0.7 0.5 collective-permute-start.9
  1.2 0.8 copy.12.lin
  2.0 0.8 copy.13.lout
  2.8 12.8 %shard_map.110 = (f32[14,128,128]{2,1,0:T(8,128)S(1)}, f32[14,128,128]{2,1,0:T(8,128)S(1)}, bf16[1,14,4,16,128]{4,3,2,1,0:T(8,128)(2,1)S(1)}, bf16[1,14,4,16,128...) custom-call(s32[4]{0:T(128)S(1)} %pad_add_fusion.pos, ...), custom_call_target="tpu_custom_call" | custom-call | flops 704643072 | bytes 16777216 | tf_op jit(solution)/shard_map/pallas_call | solution.py:171
  15.7 1.7 %collective-permute-start = (bf16[2,4,128,512]{3,2,1,0:T(8,128)(2,1)S(1)}, bf16[2,4,128,512]{3,2,1,0:T(8,128)(2,1)S(1)}, u32[]{:S(2)}, u32[]{:S(2)}) collective-permute-start(bf16[2,4,128,512]{3,2,1,0:T(8,128)(2,1)S(1)} %get-tuple-element.21), channel_id=1, source_target_pairs={{0,1},{1,0},{2,3},{3,2},{4,5},{5,4},{6,7},{7,6},{8,9},{9,8},{10,11... | collective-permute-start | bytes 3145736 | tf_op jit(solution)/shard_map/ppermute | solution.py:41
  17.3 13.3 %shard_map.111 = (bf16[2,14,4,16,128]{4,3,2,1,0:T(8,128)(2,1)S(1)}, bf16[2,14,4,16,128]{4,3,2,1,0:T(8,128)(2,1)S(1)}, bf16[2,4,128,512]{3,2,1,0:T(8,128)(2,1)S(1)}, bf16[2,4,128,512]{3,2,1,0:T(8,128)(2,1)S(1)}) custom-call(s32[4]{0:T(128)S(1)} %pad_add_fusion.pos, s32[14,4]{1,0:T(8,128)S(1)} %copy.12.lin, s32[14,4]{1,0:T(8,128)S(1)} %copy.13.lout, ...), custom_call_target="tpu_custom_call" | custom-call | flops 704643072 | bytes 16777216 | tf_op jit(solution)/shard_map/pallas_call | solution.py:171
  30.6 1.7 %collective-permute-start.4 = (bf16[2,4,128,512]{3,2,1,0:T(8,128)(2,1)S(1)}, bf16[2,4,128,512]{3,2,1,0:T(8,128)(2,1)S(1)}, u32[]{:S(2)}, u32[]{:S(2)}) collective-permute-start(bf16[2,4,128,512]{3,2,1,0:T(8,128)(2,1)S(1)} %get-tuple-element.25), channel_id=1, source_target_pairs={{0,4},{1,5},{2,6},{3,7},{4,0},{5,1},{6,2},{7,3},{8,12},{9,13},{10,... | collective-permute-start | bytes 3145736 | tf_op jit(solution)/shard_map/ppermute | solution.py:41
  32.3 2.2 %collective-permute-start.10 = (bf16[1,14,4,16,128]{4,3,2,1,0:T(8,128)(2,1)S(1)}, bf16[1,14,4,16,128]{4,3,2,1,0:T(8,128)(2,1)S(1)}, u32[]{:S(2)}, u32[]{:S(2)}) collective-permute-start(bf16[1,14,4,16,128]{4,3,2,1,0:T(8,128)(2,1)S(1)} %get-tuple-element.27), channel_id=1, source_target_pairs={{0,16},{1,17},{2,18},{3,19},{4,20},{5,21},{6,22},{7,23},{8,24},{9,... | collective-permute-start | bytes 688136 | tf_op jit(solution)/shard_map/ppermute | solution.py:41
  34.5 1.1 %collective-permute-done.10.hid1 = bf16[1,14,4,16,128]{4,3,2,1,0:T(8,128)(2,1)S(1)} collective-permute-done((bf16[1,14,4,16,128]{4,3,2,1,0:T(8,128)(2,1)S(1)}, bf16[1,14,4,16,128]{4,3,2,1,0:T(8,128)(2,1)S(1)}, u32[]{:S(2)}, u32[]{:S(2)}) %collective-permute-start.10) | collective-permute-done | bytes 229408 | tf_op jit(solution)/shard_map/ppermute | solution.py:41
  35.6 0.4 collective-permute-start.11
  36.0 1.4 %collective-permute-done.11.dg1 = bf16[2,14,4,16,128]{4,3,2,1,0:T(8,128)(2,1)S(1)} collective-permute-done((bf16[2,14,4,16,128]{4,3,2,1,0:T(8,128)(2,1)S(1)}, bf16[2,14,4,16,128]{4,3,2,1,0:T(8,128)(2,1)S(1)}, u32[]{:S(2)}, u32[]{:S(2)}) %collective-permute-start.11) | collective-permute-done | bytes 458784 | tf_op jit(solution)/shard_map/ppermute | solution.py:41
  37.5 1.3 %copy-done = bf16[128,8192]{1,0:T(8,128)(2,1)} copy-done((bf16[128,8192]{1,0:T(8,128)(2,1)}, bf16[128,8192]{1,0:T(8,128)(2,1)S(1)}, u32[]{:S(2)}) %copy-start) | copy-done | bytes 2097176
  38.8 9.1 %shard_map.112 = (bf16[2,3,14,16,512]{4,3,2,1,0:T(8,128)(2,1)S(1)}, bf16[2,3,14,16,512]{4,3,2,1,0:T(8,128)(2,1)S(1)}) custom-call(s32[14,4]{1,0:T(8,128)S(1)} %copy.12.lin, s32[14,4]{1,0:T(8,128)S(1)} %copy.13.lout, bf16[128,8192]{1,0:T(8,128)(2,1)} %h0.1, bf16[128,8192]{1,0:T(8,128)(2,1)} %copy-done, bf16[128,8192]{1,0:T(8,128)(2,1)} %d0.1, ...), custom_call_target="tpu_custom_call" | custom-call | flops 704643072 | bytes 16777216 | tf_op jit(solution)/shard_map/pallas_call | solution.py:191
  47.9 2.0 %collective-permute-start.12 = (bf16[2,3,14,16,512]{4,3,2,1,0:T(8,128)(2,1)S(1)}, bf16[2,3,14,16,512]{4,3,2,1,0:T(8,128)(2,1)S(1)}, u32[]{:S(2)}, u32[]{:S(2)}) collective-permute-start(bf16[2,3,14,16,512]{4,3,2,1,0:T(8,128)(2,1)S(1)} %get-tuple-element.31), channel_id=1, source_target_pairs={{0,32},{1,33},{2,34},{3,35},{4,36},{5,37},{6,38},{7,39},{8,40},{9,... | collective-permute-start | bytes 4128776 | tf_op jit(solution)/shard_map/ppermute | solution.py:41
  50.1 0.6 collective-permute-start.1
  50.8 2.0 %collective-permute-start.5 = (bf16[4,128,512]{2,1,0:T(8,128)(2,1)S(1)}, bf16[4,128,512]{2,1,0:T(8,128)(2,1)S(1)}, u32[]{:S(2)}, u32[]{:S(2)}) collective-permute-start(bf16[4,128,512]{2,1,0:T(8,128)(2,1)S(1)} %fusion.4), channel_id=1, source_target_pairs={{0,12},{1,13},{2,14},{3,15},{4,8},{5,9},{6,10},{7,11},{8,4},{9,5},... | collective-permute-start | bytes 1572872 | tf_op jit(solution)/shard_map/ppermute | solution.py:41
  52.8 7.8 %collective-permute-done.1 = bf16[4,128,512]{2,1,0:T(8,128)(2,1)S(1)} collective-permute-done((bf16[4,128,512]{2,1,0:T(8,128)(2,1)S(1)}, bf16[4,128,512]{2,1,0:T(8,128)(2,1)S(1)}, u32[]{:S(2)}, u32[]{:S(2)}) %collective-permute-start.1) | collective-permute-done | bytes 524320 | tf_op jit(solution)/shard_map/ppermute | solution.py:41
  60.8 0.2 collective-permute-start.2
  61.0 0.2 collective-permute-done.5
  61.3 0.2 fusion
  61.5 0.4 collective-permute-start.6
  61.9 5.3 %collective-permute-done.2 = bf16[2,128,512]{2,1,0:T(8,128)(2,1)S(1)} collective-permute-done((bf16[2,128,512]{2,1,0:T(8,128)(2,1)S(1)}, bf16[2,128,512]{2,1,0:T(8,128)(2,1)S(1)}, u32[]{:S(2)}, u32[]{:S(2)}) %collective-permute-start.2) | collective-permute-done | bytes 262176 | tf_op jit(solution)/shard_map/ppermute | solution.py:41
  67.3 0.4 collective-permute-start.3
  67.7 0.3 fusion.2
  68.0 2.7 %collective-permute-start.13 = (bf16[3,14,16,512]{3,2,1,0:T(8,128)(2,1)S(1)}, bf16[3,14,16,512]{3,2,1,0:T(8,128)(2,1)S(1)}, u32[]{:S(2)}, u32[]{:S(2)}) collective-permute-start(bf16[3,14,16,512]{3,2,1,0:T(8,128)(2,1)S(1)} %fusion.2), channel_id=1, source_target_pairs={{0,96},{1,97},{2,98},{3,99},{4,100},{5,101},{6,102},{7,103},{8,104... | collective-permute-start | bytes 2064392 | tf_op jit(solution)/shard_map/ppermute | solution.py:41
  70.8 2.0 %collective-permute-start.7 = (bf16[128,512]{1,0:T(8,128)(2,1)S(1)}, bf16[128,512]{1,0:T(8,128)(2,1)S(1)}, u32[]{:S(2)}, u32[]{:S(2)}) collective-permute-start(bf16[128,512]{1,0:T(8,128)(2,1)S(1)} %fusion.8), channel_id=1, source_target_pairs={{0,3},{1,2},{2,1},{3,0},{4,7},{5,6},{6,5},{7,4},{8,11},{9,10},{10,... | collective-permute-start | bytes 393224 | tf_op jit(solution)/shard_map/ppermute | solution.py:41
  72.8 0.8 collective-permute-done.3
  73.5 0.7 fusion.6
  74.2 2.8 %collective-permute-done.7 = bf16[128,512]{1,0:T(8,128)(2,1)S(1)} collective-permute-done((bf16[128,512]{1,0:T(8,128)(2,1)S(1)}, bf16[128,512]{1,0:T(8,128)(2,1)S(1)}, u32[]{:S(2)}, u32[]{:S(2)}) %collective-permute-start.7) | collective-permute-done | bytes 131104 | tf_op jit(solution)/shard_map/ppermute | solution.py:41
  77.0 0.7 fusion.5
  77.7 2.5 %collective-permute-done.13.r2 = bf16[3,14,16,512]{3,2,1,0:T(8,128)(2,1)S(1)} collective-permute-done((bf16[3,14,16,512]{3,2,1,0:T(8,128)(2,1)S(1)}, bf16[3,14,16,512]{3,2,1,0:T(8,128)(2,1)S(1)}, u32[]{:S(2)}, u32[]{:S(2)}) %collective-permute-start.13) | collective-permute-done | bytes 688160 | tf_op jit(solution)/shard_map/ppermute | solution.py:41
  80.2 1.8 %shard_map.113 = (f32[14,8192]{1,0:T(8,128)}, f32[14,8192]{1,0:T(8,128)}, f32[14,8192]{1,0:T(8,128)}) custom-call(bf16[2,3,14,16,512]{4,3,2,1,0:T(8,128)(2,1)S(1)} %get-tuple-element.30.own, bf16[2,3,14,16,512]{4,3,2,1,0:T(8,128)(2,1)S(1)} %collective-permute-done.12.r1, bf16[3,14,16,512]{3,2,1,0:T(8,128)(2,1)S(1)} %collective-permute-done.13.r2), custom_call_target="tpu_custom_call" | custom-call | tf_op jit(solution)/shard_map/pallas_call | solution.py:212
  (16 shorter events, 0.8 us)
Async XLA Ops:
  0.6 36.8 %collective-permute-start.8 = (bf16[128,8192]{1,0:T(8,128)(2,1)}, bf16[128,8192]{1,0:T(8,128)(2,1)S(1)}, u32[]{:S(2)}, u32[]{:S(2)}) collective-permute-start(bf16[128,8192]{1,0:T(8,128)(2,1)} %h0.1), channel_id=1, source_target_pairs={{0,16},{1,17},{2,18},{3,19},{4,20},{5,21},{6,22},{7,23},{8,24},{9,... | collective-permute-start | bytes 6291464 | tf_op jit(solution)/shard_map/ppermute | solution.py:41
  0.7 36.7 %collective-permute-start.9 = (bf16[128,8192]{1,0:T(8,128)(2,1)}, bf16[128,8192]{1,0:T(8,128)(2,1)}, u32[]{:S(2)}, u32[]{:S(2)}) collective-permute-start(bf16[128,8192]{1,0:T(8,128)(2,1)} %d0.1), channel_id=1, source_target_pairs={{0,16},{1,17},{2,18},{3,19},{4,20},{5,21},{6,22},{7,23},{8,24},{9,... | collective-permute-start | bytes 6291464 | tf_op jit(solution)/shard_map/ppermute | solution.py:41
  15.7 34.3 %collective-permute-start = (bf16[2,4,128,512]{3,2,1,0:T(8,128)(2,1)S(1)}, bf16[2,4,128,512]{3,2,1,0:T(8,128)(2,1)S(1)}, u32[]{:S(2)}, u32[]{:S(2)}) collective-permute-start(bf16[2,4,128,512]{3,2,1,0:T(8,128)(2,1)S(1)} %get-tuple-element.21), channel_id=1, source_target_pairs={{0,1},{1,0},{2,3},{3,2},{4,5},{5,4},{6,7},{7,6},{8,9},{9,8},{10,11... | collective-permute-start | bytes 3145736 | tf_op jit(solution)/shard_map/ppermute | solution.py:41
  30.6 20.0 %collective-permute-start.4 = (bf16[2,4,128,512]{3,2,1,0:T(8,128)(2,1)S(1)}, bf16[2,4,128,512]{3,2,1,0:T(8,128)(2,1)S(1)}, u32[]{:S(2)}, u32[]{:S(2)}) collective-permute-start(bf16[2,4,128,512]{3,2,1,0:T(8,128)(2,1)S(1)} %get-tuple-element.25), channel_id=1, source_target_pairs={{0,4},{1,5},{2,6},{3,7},{4,0},{5,1},{6,2},{7,3},{8,12},{9,13},{10,... | collective-permute-start | bytes 3145736 | tf_op jit(solution)/shard_map/ppermute | solution.py:41
  32.3 3.4 %collective-permute-start.10 = (bf16[1,14,4,16,128]{4,3,2,1,0:T(8,128)(2,1)S(1)}, bf16[1,14,4,16,128]{4,3,2,1,0:T(8,128)(2,1)S(1)}, u32[]{:S(2)}, u32[]{:S(2)}) collective-permute-start(bf16[1,14,4,16,128]{4,3,2,1,0:T(8,128)(2,1)S(1)} %get-tuple-element.27), channel_id=1, source_target_pairs={{0,16},{1,17},{2,18},{3,19},{4,20},{5,21},{6,22},{7,23},{8,24},{9,... | collective-permute-start | bytes 688136 | tf_op jit(solution)/shard_map/ppermute | solution.py:41
  35.6 1.8 %collective-permute-start.11 = (bf16[2,14,4,16,128]{4,3,2,1,0:T(8,128)(2,1)S(1)}, bf16[2,14,4,16,128]{4,3,2,1,0:T(8,128)(2,1)S(1)}, u32[]{:S(2)}, u32[]{:S(2)}) collective-permute-start(bf16[2,14,4,16,128]{4,3,2,1,0:T(8,128)(2,1)S(1)} %get-tuple-element.29), channel_id=1, source_target_pairs={{0,16},{1,17},{2,18},{3,19},{4,20},{5,21},{6,22},{7,23},{8,24},{9,... | collective-permute-start | bytes 1376264 | tf_op jit(solution)/shard_map/ppermute | solution.py:41
  37.4 1.3 %copy-start = (bf16[128,8192]{1,0:T(8,128)(2,1)}, bf16[128,8192]{1,0:T(8,128)(2,1)S(1)}, u32[]{:S(2)}) copy-start(bf16[128,8192]{1,0:T(8,128)(2,1)S(1)} %collective-permute-done.8.h1) | copy-start | bytes 6291460
  47.9 19.8 %collective-permute-start.12 = (bf16[2,3,14,16,512]{4,3,2,1,0:T(8,128)(2,1)S(1)}, bf16[2,3,14,16,512]{4,3,2,1,0:T(8,128)(2,1)S(1)}, u32[]{:S(2)}, u32[]{:S(2)}) collective-permute-start(bf16[2,3,14,16,512]{4,3,2,1,0:T(8,128)(2,1)S(1)} %get-tuple-element.31), channel_id=1, source_target_pairs={{0,32},{1,33},{2,34},{3,35},{4,36},{5,37},{6,38},{7,39},{8,40},{9,... | collective-permute-start | bytes 4128776 | tf_op jit(solution)/shard_map/ppermute | solution.py:41
  50.1 10.5 %collective-permute-start.1 = (bf16[4,128,512]{2,1,0:T(8,128)(2,1)S(1)}, bf16[4,128,512]{2,1,0:T(8,128)(2,1)S(1)}, u32[]{:S(2)}, u32[]{:S(2)}) collective-permute-start(bf16[4,128,512]{2,1,0:T(8,128)(2,1)S(1)} %fusion.3), channel_id=1, source_target_pairs={{0,3},{1,2},{2,1},{3,0},{4,7},{5,6},{6,5},{7,4},{8,11},{9,10},{10,... | collective-permute-start | bytes 1572872 | tf_op jit(solution)/shard_map/ppermute | solution.py:41
  50.8 10.5 %collective-permute-start.5 = (bf16[4,128,512]{2,1,0:T(8,128)(2,1)S(1)}, bf16[4,128,512]{2,1,0:T(8,128)(2,1)S(1)}, u32[]{:S(2)}, u32[]{:S(2)}) collective-permute-start(bf16[4,128,512]{2,1,0:T(8,128)(2,1)S(1)} %fusion.4), channel_id=1, source_target_pairs={{0,12},{1,13},{2,14},{3,15},{4,8},{5,9},{6,10},{7,11},{8,4},{9,5},... | collective-permute-start | bytes 1572872 | tf_op jit(solution)/shard_map/ppermute | solution.py:41
  60.8 6.5 %collective-permute-start.2 = (bf16[2,128,512]{2,1,0:T(8,128)(2,1)S(1)}, bf16[2,128,512]{2,1,0:T(8,128)(2,1)S(1)}, u32[]{:S(2)}, u32[]{:S(2)}) collective-permute-start(bf16[2,128,512]{2,1,0:T(8,128)(2,1)S(1)} %slice.83), channel_id=1, source_target_pairs={{0,4},{1,5},{2,6},{3,7},{4,0},{5,1},{6,2},{7,3},{8,12},{9,13},{10,... | collective-permute-start | bytes 786440 | tf_op jit(solution)/shard_map/ppermute | solution.py:41
  61.5 9.2 %collective-permute-start.6 = (bf16[2,128,512]{2,1,0:T(8,128)(2,1)S(1)}, bf16[2,128,512]{2,1,0:T(8,128)(2,1)S(1)}, u32[]{:S(2)}, u32[]{:S(2)}) collective-permute-start(bf16[2,128,512]{2,1,0:T(8,128)(2,1)S(1)} %slice.90), channel_id=1, source_target_pairs={{0,1},{1,0},{2,3},{3,2},{4,5},{5,4},{6,7},{7,6},{8,9},{9,8},{10,11... | collective-permute-start | bytes 786440 | tf_op jit(solution)/shard_map/ppermute | solution.py:41
  67.3 6.3 %collective-permute-start.3 = (bf16[128,512]{1,0:T(8,128)(2,1)S(1)}, bf16[128,512]{1,0:T(8,128)(2,1)S(1)}, u32[]{:S(2)}, u32[]{:S(2)}) collective-permute-start(bf16[128,512]{1,0:T(8,128)(2,1)S(1)} %fusion.7), channel_id=1, source_target_pairs={{0,12},{1,13},{2,14},{3,15},{4,8},{5,9},{6,10},{7,11},{8,4},{9,5},... | collective-permute-start | bytes 393224 | tf_op jit(solution)/shard_map/ppermute | solution.py:41
  68.0 12.2 %collective-permute-start.13 = (bf16[3,14,16,512]{3,2,1,0:T(8,128)(2,1)S(1)}, bf16[3,14,16,512]{3,2,1,0:T(8,128)(2,1)S(1)}, u32[]{:S(2)}, u32[]{:S(2)}) collective-permute-start(bf16[3,14,16,512]{3,2,1,0:T(8,128)(2,1)S(1)} %fusion.2), channel_id=1, source_target_pairs={{0,96},{1,97},{2,98},{3,99},{4,100},{5,101},{6,102},{7,103},{8,104... | collective-permute-start | bytes 2064392 | tf_op jit(solution)/shard_map/ppermute | solution.py:41
  70.8 6.3 %collective-permute-start.7 = (bf16[128,512]{1,0:T(8,128)(2,1)S(1)}, bf16[128,512]{1,0:T(8,128)(2,1)S(1)}, u32[]{:S(2)}, u32[]{:S(2)}) collective-permute-start(bf16[128,512]{1,0:T(8,128)(2,1)S(1)} %fusion.8), channel_id=1, source_target_pairs={{0,3},{1,2},{2,1},{3,0},{4,7},{5,6},{6,5},{7,4},{8,11},{9,10},{10,... | collective-permute-start | bytes 393224 | tf_op jit(solution)/shard_map/ppermute | solution.py:41

commit v2 on v1

v2 whole, which is shorter than its diff:
```python
import jax
import jax.numpy as jnp
from jax import lax
from jax.experimental import pallas as pl
from jax.experimental.pallas import tpu as pltpu
from jax.sharding import PartitionSpec as P

D = 8192
BLK = 128
KB = 4
W = KB * BLK
NBLK = D // BLK
ROWS = 14
TOK = 128
AXES = ("dp", "tensor")
F32 = jnp.float32
BF16 = jnp.bfloat16
NT = (((1,), (1,)), ((), ()))


def pairs(axis, step):
    out = []
    for d in range(128):
        dp, t = divmod(d, 16)
        z, c = divmod(dp, 2)
        y, x = divmod(t, 4)
        m = 1 if (c == 0) == (step == 0) else 3
        if axis == "x":
            x ^= m
        elif axis == "y":
            y ^= m
        elif axis == "z":
            z ^= m
        else:
            c ^= 1
        out.append((d, (z * 2 + c) * 16 + y * 4 + x))
    return out


def send(a, axis, step=0):
    return lax.ppermute(a, AXES, pairs(axis, step))


def ring_order(me, core):
    first = 1 + 2 * core
    return (me ^ first, me ^ 2, me, me ^ (first ^ 2))


def dot(a, b, dims=None):
    if dims is None:
        return jnp.dot(a, b, preferred_element_type=F32)
    return lax.dot_general(a, b, dims, preferred_element_type=F32)


def gather_cols(ref, lay, r):
    return jnp.concatenate(
        [ref[:, pl.ds(pl.multiple_of(lay[r, k] * BLK, BLK), BLK)] for k in range(KB)], axis=1
    )


def emit_chunks(acc, outer, inner, transposed, sent, kept):
    for p in range(4):
        dst = sent if p < 2 else kept
        for q in range(4):
            y, x = (inner[q], outer[p]) if transposed else (outer[p], inner[q])
            base = (y * 4 + x) * 4
            for j in range(4):
                dst[p % 2, q, :, j * BLK : (j + 1) * BLK] = acc[base + j].astype(BF16)


def main_kernel(
    pos, lin_hbm, lout_hbm, h_hbm, d_hbm, wg_hbm, wu_hbm, wd_hbm,
    keep, give, p_sent, p_kept, q_sent, q_kept, h, d,
    wg, wu, wd, acc_p, acc_q, hid, dgu, turned, lin, lout, sem, w_sem,
):
    small = [
        pltpu.make_async_copy(lin_hbm, lin, sem.at[0]),
        pltpu.make_async_copy(lout_hbm, lout, sem.at[1]),
        pltpu.make_async_copy(h_hbm, h, sem.at[2]),
        pltpu.make_async_copy(d_hbm, d, sem.at[3]),
    ]

    def weights(start, n):
        rows = pl.ds(start * BLK, n * BLK)
        both = ((wg_hbm, wg), (wu_hbm, wu), (wd_hbm, wd))
        return [
            pltpu.make_async_copy(src.at[rows], dst.at[rows], w_sem.at[i, 0 if start == 0 else 1])
            for i, (src, dst) in enumerate(both)
        ]

    early, late = weights(0, EARLY), weights(EARLY, ROWS - EARLY)
    for c in small + early + late:
        c.start()
    acc_p[...] = jnp.zeros_like(acc_p)
    acc_q[...] = jnp.zeros_like(acc_q)
    for c in small + early:
        c.wait()
    z, core = pos[0], pos[1]
    mine = [o * 2 + core for o in ring_order(z, core)]
    others = [o * 2 + 1 - core for o in ring_order(z, 1 - core)]

    def rows_of(r):
        at = r * BLK if isinstance(r, int) else pl.multiple_of(r * BLK, BLK)
        return pl.ds(at, BLK)

    def units(s):
        for i in range(UNROLL):
            r = s * UNROLL + i
            sl = rows_of(r)
            hx, dob = gather_cols(h, lin, r), gather_cols(d, lout, r)
            gate, up, dhid = dot(hx, wg[sl], NT), dot(hx, wu[sl], NT), dot(dob, wd[sl], NT)
            sig = jax.nn.sigmoid(gate)
            silu = gate * sig
            hidden = (silu * up).astype(BF16)
            dgate = (dhid * up * sig * (1.0 + gate * (1.0 - sig))).astype(BF16)
            dup = (dhid * silu).astype(BF16)
            hid[r] = hidden
            dgu[r, :, :BLK] = dgate
            dgu[r, :, BLK:] = dup
            for a, v in enumerate((hidden, dgate, dup)):
                turned[r, a] = v.T.reshape(8, 16, TOK)

    def features(s):
        for i in range(UNROLL):
            r = s * UNROLL + i
            sl = rows_of(r)
            part = dot(hid[r], wd[sl])
            dhx = dot(dgu[r], jnp.concatenate([wg[sl], wu[sl]], axis=0))
            for k in range(KB):
                acc_p[lout[r, k]] += part[:, k * BLK : (k + 1) * BLK]
            for k in range(KB):
                acc_q[lin[r, k]] += dhx[:, k * BLK : (k + 1) * BLK]
            for a in range(3):
                for q in range(4):
                    keep[a, r, q] = turned[r, a, mine[q]]
                    give[a, r, q] = turned[r, a, others[q]]

    def both(s):
        features(s - 1)
        units(s)

    units(0)
    pl.loop(1, EARLY // UNROLL)(both)
    for c in late:
        c.wait()
    pl.loop(EARLY // UNROLL, ROWS // UNROLL)(both)
    features(ROWS // UNROLL - 1)
    xs, ys = ring_order(pos[3], core), ring_order(pos[2], core)
    emit_chunks(acc_p, xs, ys, True, p_sent, p_kept)
    emit_chunks(acc_q, ys, xs, False, q_sent, q_kept)


def grads_kernel(lin, lout, h0, h1, d0, d1, act0, act1, sent, kept):
    @pl.loop(0, ROWS // UNROLL)
    def _(s):
        for i in range(UNROLL):
            r = s * UNROLL + i
            hx = jnp.concatenate([gather_cols(h0, lin, r), gather_cols(h1, lin, r)], axis=0)
            dob = jnp.concatenate([gather_cols(d0, lout, r), gather_cols(d1, lout, r)], axis=0)
            act = [
                jnp.concatenate([act0[a, r].reshape(64, TOK), act1[a, r].reshape(64, TOK)], axis=1)
                for a in range(3)
            ]
            g_in = dot(jnp.concatenate(act[1:], axis=0), hx).astype(BF16).reshape(2, 4, 16, W)
            g_down = dot(act[0], dob).astype(BF16).reshape(4, 16, W)
            for q in range(4):
                dst = sent if q < 2 else kept
                dst[q % 2, 0, r] = g_in[0, q]
                dst[q % 2, 1, r] = g_in[1, q]
                dst[q % 2, 2, r] = g_down[q]


def finish_kernel(own, r1, r2, gate, up, down, tmp):
    for g, out in enumerate((gate, up, down)):
        total = own[0, g].astype(F32) + r1[0, g].astype(F32) + r2[g].astype(F32)
        total = total.reshape(ROWS * 16, W)
        for k in range(KB):
            tmp[k] = total[:, k * BLK : (k + 1) * BLK]
        for i in range(16):
            for k in range(KB):
                at = i * W + k * BLK
                out[:, at : at + BLK] = tmp[k, pl.ds(i, ROWS, stride=16), :]


V = pltpu.VMEM
IN_SMEM = pl.BlockSpec(memory_space=pltpu.SMEM)
IN_VMEM = pl.BlockSpec(memory_space=pltpu.VMEM)
ANYWHERE = pl.BlockSpec(memory_space=pl.ANY)
UNROLL = 2
EARLY = 4


def in_hbm(*arrays):
    return [pltpu.with_memory_space_constraint(a, pltpu.HBM) for a in arrays]


def in_vmem(*arrays):
    return [pltpu.with_memory_space_constraint(a, pltpu.VMEM) for a in arrays]


def cost(mib):
    return pl.CostEstimate(flops=10**9, bytes_accessed=mib * 2**20, transcendentals=0)


def main_call(pos, *arrays):
    act = V((3, ROWS, 4, 16, TOK), BF16)
    chunks = V((2, 4, TOK, W), BF16)
    weight = V((ROWS * BLK, W), BF16)
    total = V((NBLK, TOK, BLK), F32)
    layout = pltpu.SMEM((ROWS, KB), jnp.int32)
    return pl.pallas_call(
        main_kernel,
        in_specs=[IN_SMEM] + [ANYWHERE] * 7,
        out_specs=[IN_VMEM] * 8,
        out_shape=[act, act, chunks, chunks, chunks, chunks, V((TOK, D), BF16), V((TOK, D), BF16)],
        scratch_shapes=[
            weight, weight, weight, total, total,
            V((ROWS, TOK, BLK), BF16), V((ROWS, TOK, 2 * BLK), BF16), V((ROWS, 3, 8, 16, TOK), BF16),
            layout, layout, pltpu.SemaphoreType.DMA((4,)), pltpu.SemaphoreType.DMA((3, 2)),
        ],
        compiler_params=pltpu.CompilerParams(vmem_limit_bytes=24 * 2**20),
        cost_estimate=cost(24),
    )(pos, *in_hbm(*arrays))


def grads_call(lin, lout, *arrays):
    out = V((2, 3, ROWS, 16, W), BF16)
    return pl.pallas_call(
        grads_kernel,
        in_specs=[IN_SMEM] * 2 + [IN_VMEM] * 6,
        out_specs=[IN_VMEM] * 2,
        out_shape=[out, out],
        compiler_params=pltpu.CompilerParams(vmem_limit_bytes=4 * 2**20),
        cost_estimate=cost(12),
    )(lin, lout, *in_vmem(*arrays))


def finish_call(*arrays):
    out = jax.ShapeDtypeStruct((ROWS, 16 * W), F32)
    return pl.pallas_call(
        finish_kernel,
        in_specs=[IN_VMEM] * 3,
        out_specs=[IN_VMEM] * 3,
        out_shape=[out] * 3,
        scratch_shapes=[V((KB, ROWS * 16, BLK), F32)],
        compiler_params=pltpu.CompilerParams(vmem_limit_bytes=8 * 2**20),
        cost_estimate=cost(6),
    )(*in_vmem(*arrays))


def add(*terms):
    return sum(t.astype(F32) for t in terms).astype(BF16)


def ring_pair(sent, kept, first, second):
    r1 = send(sent, first, 0)
    r2 = send(add(kept[1], r1[1]), first, 1)
    mid = add(kept[0], r1[0], r2)
    r3 = send(mid[0:2], second, 0)
    r4 = send(add(mid[3], r3[1]), second, 1)
    return add(mid[2], r3[0], r4)


def shards(h_in, dout, w_gate, w_up, w_down, in_layout, out_layout):
    dp, t = lax.axis_index("dp"), lax.axis_index("tensor")
    pos = jnp.stack([dp // 2, dp % 2, t // 4, t % 4]).astype(jnp.int32)
    h_other = send(h_in, "core")
    d_other = send(dout, "core")
    keep, give, p_sent, p_kept, q_sent, q_kept, h_own, d_own = main_call(
        pos, in_layout, out_layout, h_in, dout, w_gate, w_up, w_down
    )
    taken = send(give, "core")
    g_sent, g_kept = grads_call(in_layout, out_layout, h_own, h_other, d_own, d_other, keep, taken)
    g1 = send(g_sent, "z", 0)
    g2 = send(add(g_kept[1], g1[1]), "z", 1)
    g_gate, g_up, g_down = finish_call(g_kept, g1, g2)
    out = ring_pair(p_sent, p_kept, "x", "y")
    dh = ring_pair(q_sent, q_kept, "y", "x")
    return (out, dh, g_gate, g_up, g_down)


def solution(mesh):
    rows = P("tensor", None)
    return jax.shard_map(
        shards,
        mesh=mesh,
        in_specs=(P("dp", None), P("dp", None), rows, rows, rows, rows, rows),
        out_specs=(P("dp", "tensor"), P("dp", "tensor")) + (P("tensor", "dp"),) * 3,
        check_vma=False,
    )
```

time: 82.6 us -> 63.9 us (0.77)
  Pallas kernels: 37 us -> 15.9 us
  starting transfers between devices: 16.9 us -> 24.9 us
  waiting for transfers between devices: 21.9 us -> 16.8 us
    pallas_call x4 -> x3, Pallas kernels: 37 us -> 15.9 us  [the longest x1 9.15 us: main_call(): pl.pallas_call(main_kernel, in_specs=[IN_SMEM] + [ANYWHERE] * 7, out_spec...]
    ppermute x14 -> x13, starting transfers between devices: 16.9 us -> 24.9 us  [send(): return lax.ppermute(a, AXES, pairs(axis, step))]
    ppermute x14 -> x13, waiting for transfers between devices: 21.9 us -> 16.8 us  [send(): return lax.ppermute(a, AXES, pairs(axis, step))]
    unnamed x4 -> x6, local copies, waits for them, and re-layouts: 2.87 us -> 2.73 us
  transfers between devices with their start and end apart: 14 -> 13, of which waited for: 8 -> 7; matrix products, arithmetic and copies ran while one was open for 5% -> 8% of each run, Pallas kernels for 43% -> 22%
where the time goes in v2:
time: 63.9 us; the launch traced here: 63.7 us
  starting transfers between devices  24.9 us (39%)
  waiting for transfers between devices  16.8 us (26%)
  Pallas kernels  15.9 us (25%)
  local copies, waits for them, and re-layouts  2.77 us (4%)
  other arithmetic  2.51 us (4%)
  between operations  0.73 us (1%)
    ppermute x13, starting transfers between devices, send(): return lax.ppermute(a, AXES, pairs(axis, step))  24.9 us
    ppermute x13, waiting for transfers between devices, send(): return lax.ppermute(a, AXES, pairs(axis, step))  16.8 us
    pallas_call x1, Pallas kernels, main_call(): pl.pallas_call(main_kernel, in_specs=[IN_SMEM] + [ANYWHERE] * 7, out_spec...  9.15 us
    pallas_call x1, Pallas kernels, grads_call(): pl.pallas_call(grads_kernel, in_specs=[IN_SMEM] * 2 + [IN_VMEM] * 6, out_...  4.96 us
    unnamed x6, local copies, waits for them, and re-layouts  2.73 us
    convert_element_type x9, other arithmetic, add(): return sum((t.astype(F32) for t in terms)).astype(BF16)  2.43 us
    pallas_call x1, Pallas kernels, finish_call(): pl.pallas_call(finish_kernel, in_specs=[IN_VMEM] * 3, out_specs=[IN_VMEM]...  1.79 us
  transfers between devices with their start and end apart: 13, of which 7 were waited for; matrix products, arithmetic and copies ran while one was open for 8% of the time, Pallas kernels for 22%

profile of v2, /device:TPU:0, one launch (start us, length us, event | category | flops | bytes accessed | tf_op | source)
XLA Modules:
  0.0 63.7 jit_solution(5745643730742123544)
XLA Ops:
  0.6 0.1 collective-permute-start.8
  0.7 0.5 collective-permute-start.9
  1.2 1.4 %copy.12.lin_hbm.lin = s32[14,4]{1,0:T(8,128)} copy(s32[14,4]{0,1:T(4,128)} %param.12) | data formatting | bytes 448 | tf_op args[5]
  2.6 1.4 %copy.13.lout_hbm.lout = s32[14,4]{1,0:T(8,128)} copy(s32[14,4]{0,1:T(4,128)} %param.13) | data formatting | bytes 448 | tf_op args[6]
  4.0 9.1 %shard_map.110 = (bf16[3,14,4,16,128]{4,3,2,1,0:T(8,128)(2,1)S(1)}, bf16[3,14,4,16,128]{4,3,2,1,0:T(8,128)(2,1)S(1)}, bf16[2,4,128,512]{3,2,1,0:T(8,128)(2,1)S(1...) custom-call(s32[4]{0:T(128)S(1)} %pad_add_fusion.pos, ...), custom_call_target="tpu_custom_call" | custom-call | flops 1000000000 | bytes 25165824 | tf_op jit(solution)/shard_map/pallas_call | solution.py:211
  13.2 1.6 %collective-permute-start = (bf16[2,4,128,512]{3,2,1,0:T(8,128)(2,1)S(1)}, bf16[2,4,128,512]{3,2,1,0:T(8,128)(2,1)S(1)}, u32[]{:S(2)}, u32[]{:S(2)}) collective-permute-start(bf16[2,4,128,512]{3,2,1,0:T(8,128)(2,1)S(1)} %get-tuple-element.19), channel_id=1, source_target_pairs={{0,1},{1,0},{2,3},{3,2},{4,5},{5,4},{6,7},{7,6},{8,9},{9,8},{10,11... | collective-permute-start | bytes 3145736 | tf_op jit(solution)/shard_map/ppermute | solution.py:41
  14.8 1.1 %collective-permute-start.10 = (bf16[3,14,4,16,128]{4,3,2,1,0:T(8,128)(2,1)S(1)}, bf16[3,14,4,16,128]{4,3,2,1,0:T(8,128)(2,1)S(1)}, u32[]{:S(2)}, u32[]{:S(2)}) collective-permute-start(bf16[3,14,4,16,128]{4,3,2,1,0:T(8,128)(2,1)S(1)} %get-tuple-element.25), channel_id=1, source_target_pairs={{0,16},{1,17},{2,18},{3,19},{4,20},{5,21},{6,22},{7,23},{8,24},{9,... | collective-permute-start | bytes 2064392 | tf_op jit(solution)/shard_map/ppermute | solution.py:41
  15.9 1.6 %collective-permute-start.4 = (bf16[2,4,128,512]{3,2,1,0:T(8,128)(2,1)S(1)}, bf16[2,4,128,512]{3,2,1,0:T(8,128)(2,1)S(1)}, u32[]{:S(2)}, u32[]{:S(2)}) collective-permute-start(bf16[2,4,128,512]{3,2,1,0:T(8,128)(2,1)S(1)} %get-tuple-element.21), channel_id=1, source_target_pairs={{0,4},{1,5},{2,6},{3,7},{4,0},{5,1},{6,2},{7,3},{8,12},{9,13},{10,... | collective-permute-start | bytes 3145736 | tf_op jit(solution)/shard_map/ppermute | solution.py:41
  17.5 0.2 collective-permute-done.10.act1
  17.7 5.0 %shard_map.111 = (bf16[2,3,14,16,512]{4,3,2,1,0:T(8,128)(2,1)S(1)}, bf16[2,3,14,16,512]{4,3,2,1,0:T(8,128)(2,1)S(1)}) custom-call(s32[14,4]{1,0:T(8,128)S(1)} %copy-done, s32[14,4]{1,0:T(8,128)S(1)} %copy-done.1, bf16[128,8192]{1,0:T(8,128)(2,1)S(1)} %get-tuple-element.22.h0, bf16[128,8192]{1,0:T(8,128)(2,1)S(1)} %collective-permute-done.8.h1, ...), custom_call_target="tpu_custom_call" | custom-call | flops 1000000000 | bytes 12582912 | tf_op jit(solution)/shard_map/pallas_call | solution.py:228
  22.7 2.0 %collective-permute-start.11 = (bf16[2,3,14,16,512]{4,3,2,1,0:T(8,128)(2,1)S(1)}, bf16[2,3,14,16,512]{4,3,2,1,0:T(8,128)(2,1)S(1)}, u32[]{:S(2)}, u32[]{:S(2)}) collective-permute-start(bf16[2,3,14,16,512]{4,3,2,1,0:T(8,128)(2,1)S(1)} %get-tuple-element.27), channel_id=1, source_target_pairs={{0,32},{1,33},{2,34},{3,35},{4,36},{5,37},{6,38},{7,39},{8,40},{9,... | collective-permute-start | bytes 4128776 | tf_op jit(solution)/shard_map/ppermute | solution.py:41
  24.7 3.4 %collective-permute-done = bf16[2,4,128,512]{3,2,1,0:T(8,128)(2,1)S(1)} collective-permute-done((bf16[2,4,128,512]{3,2,1,0:T(8,128)(2,1)S(1)}, bf16[2,4,128,512]{3,2,1,0:T(8,128)(2,1)S(1)}, u32[]{:S(2)}, u32[]{:S(2)}) %collective-permute-start) | collective-permute-done | bytes 1048608 | tf_op jit(solution)/shard_map/ppermute | solution.py:41
  28.1 0.1 fusion.3
  28.2 2.9 %collective-permute-start.1 = (bf16[4,128,512]{2,1,0:T(8,128)(2,1)S(1)}, bf16[4,128,512]{2,1,0:T(8,128)(2,1)S(1)}, u32[]{:S(2)}, u32[]{:S(2)}) collective-permute-start(bf16[4,128,512]{2,1,0:T(8,128)(2,1)S(1)} %fusion.3), channel_id=1, source_target_pairs={{0,3},{1,2},{2,1},{3,0},{4,7},{5,6},{6,5},{7,4},{8,11},{9,10},{10,... | collective-permute-start | bytes 1572872 | tf_op jit(solution)/shard_map/ppermute | solution.py:41
  31.1 0.1 fusion.4
  31.3 3.1 %collective-permute-start.5 = (bf16[4,128,512]{2,1,0:T(8,128)(2,1)S(1)}, bf16[4,128,512]{2,1,0:T(8,128)(2,1)S(1)}, u32[]{:S(2)}, u32[]{:S(2)}) collective-permute-start(bf16[4,128,512]{2,1,0:T(8,128)(2,1)S(1)} %fusion.4), channel_id=1, source_target_pairs={{0,12},{1,13},{2,14},{3,15},{4,8},{5,9},{6,10},{7,11},{8,4},{9,5},... | collective-permute-start | bytes 1572872 | tf_op jit(solution)/shard_map/ppermute | solution.py:41
  34.4 4.3 %collective-permute-done.1 = bf16[4,128,512]{2,1,0:T(8,128)(2,1)S(1)} collective-permute-done((bf16[4,128,512]{2,1,0:T(8,128)(2,1)S(1)}, bf16[4,128,512]{2,1,0:T(8,128)(2,1)S(1)}, u32[]{:S(2)}, u32[]{:S(2)}) %collective-permute-start.1) | collective-permute-done | bytes 524320 | tf_op jit(solution)/shard_map/ppermute | solution.py:41
  38.7 0.2 fusion.1
  38.9 1.7 %collective-permute-start.2 = (bf16[2,128,512]{2,1,0:T(8,128)(2,1)S(1)}, bf16[2,128,512]{2,1,0:T(8,128)(2,1)S(1)}, u32[]{:S(2)}, u32[]{:S(2)}) collective-permute-start(bf16[2,128,512]{2,1,0:T(8,128)(2,1)S(1)} %slice.83), channel_id=1, source_target_pairs={{0,4},{1,5},{2,6},{3,7},{4,0},{5,1},{6,2},{7,3},{8,12},{9,13},{10,... | collective-permute-start | bytes 786440 | tf_op jit(solution)/shard_map/ppermute | solution.py:41
  40.7 1.7 %collective-permute-done.5 = bf16[4,128,512]{2,1,0:T(8,128)(2,1)S(1)} collective-permute-done((bf16[4,128,512]{2,1,0:T(8,128)(2,1)S(1)}, bf16[4,128,512]{2,1,0:T(8,128)(2,1)S(1)}, u32[]{:S(2)}, u32[]{:S(2)}) %collective-permute-start.5) | collective-permute-done | bytes 524320 | tf_op jit(solution)/shard_map/ppermute | solution.py:41
  42.4 0.2 fusion
  42.6 0.1 collective-permute-start.6
  42.7 2.6 %collective-permute-done.2 = bf16[2,128,512]{2,1,0:T(8,128)(2,1)S(1)} collective-permute-done((bf16[2,128,512]{2,1,0:T(8,128)(2,1)S(1)}, bf16[2,128,512]{2,1,0:T(8,128)(2,1)S(1)}, u32[]{:S(2)}, u32[]{:S(2)}) %collective-permute-start.2) | collective-permute-done | bytes 262176 | tf_op jit(solution)/shard_map/ppermute | solution.py:41
  45.4 3.2 %collective-permute-start.3 = (bf16[128,512]{1,0:T(8,128)(2,1)S(1)}, bf16[128,512]{1,0:T(8,128)(2,1)S(1)}, u32[]{:S(2)}, u32[]{:S(2)}) collective-permute-start(bf16[128,512]{1,0:T(8,128)(2,1)S(1)} %fusion.7), channel_id=1, source_target_pairs={{0,12},{1,13},{2,14},{3,15},{4,8},{5,9},{6,10},{7,11},{8,4},{9,5},... | collective-permute-start | bytes 393224 | tf_op jit(solution)/shard_map/ppermute | solution.py:41
  48.6 0.3 fusion.2
  48.8 4.1 %collective-permute-start.12 = (bf16[3,14,16,512]{3,2,1,0:T(8,128)(2,1)S(1)}, bf16[3,14,16,512]{3,2,1,0:T(8,128)(2,1)S(1)}, u32[]{:S(2)}, u32[]{:S(2)}) collective-permute-start(bf16[3,14,16,512]{3,2,1,0:T(8,128)(2,1)S(1)} %fusion.2), channel_id=1, source_target_pairs={{0,96},{1,97},{2,98},{3,99},{4,100},{5,101},{6,102},{7,103},{8,104... | collective-permute-start | bytes 2064392 | tf_op jit(solution)/shard_map/ppermute | solution.py:41
  53.0 2.9 %collective-permute-start.7 = (bf16[128,512]{1,0:T(8,128)(2,1)S(1)}, bf16[128,512]{1,0:T(8,128)(2,1)S(1)}, u32[]{:S(2)}, u32[]{:S(2)}) collective-permute-start(bf16[128,512]{1,0:T(8,128)(2,1)S(1)} %fusion.8), channel_id=1, source_target_pairs={{0,3},{1,2},{2,1},{3,0},{4,7},{5,6},{6,5},{7,4},{8,11},{9,10},{10,... | collective-permute-start | bytes 393224 | tf_op jit(solution)/shard_map/ppermute | solution.py:41
  55.9 0.7 %fusion.6 = bf16[128,512]{1,0:T(8,128)(2,1)} fusion(bf16[128,512]{1,0:T(8,128)(2,1)S(1)} %collective-permute-done.3, bf16[2,128,512]{2,1,0:T(8,128)(2,1)S(1)} %collective-permute-done.2, bf16[4,128,512]{2,1,0:T(8,128)(2,1)S(1)} %fusion.1), kind=kLoop, calls=%fused_computation.13 | loop fusion | flops 393216 | bytes 524288 | tf_op jit(solution)/shard_map/convert_element_type | solution.py:252
  56.6 2.7 %collective-permute-done.7 = bf16[128,512]{1,0:T(8,128)(2,1)S(1)} collective-permute-done((bf16[128,512]{1,0:T(8,128)(2,1)S(1)}, bf16[128,512]{1,0:T(8,128)(2,1)S(1)}, u32[]{:S(2)}, u32[]{:S(2)}) %collective-permute-start.7) | collective-permute-done | bytes 131104 | tf_op jit(solution)/shard_map/ppermute | solution.py:41
  59.2 0.7 %fusion.5 = bf16[128,512]{1,0:T(8,128)(2,1)} fusion(bf16[128,512]{1,0:T(8,128)(2,1)S(1)} %collective-permute-done.7, bf16[2,128,512]{2,1,0:T(8,128)(2,1)S(1)} %collective-permute-done.6, bf16[4,128,512]{2,1,0:T(8,128)(2,1)S(1)} %fusion), kind=kLoop, calls=%fused_computation.11 | loop fusion | flops 393216 | bytes 524288 | tf_op jit(solution)/shard_map/convert_element_type | solution.py:252
  60.0 1.9 %collective-permute-done.12.r2 = bf16[3,14,16,512]{3,2,1,0:T(8,128)(2,1)S(1)} collective-permute-done((bf16[3,14,16,512]{3,2,1,0:T(8,128)(2,1)S(1)}, bf16[3,14,16,512]{3,2,1,0:T(8,128)(2,1)S(1)}, u32[]{:S(2)}, u32[]{:S(2)}) %collective-permute-start.12) | collective-permute-done | bytes 688160 | tf_op jit(solution)/shard_map/ppermute | solution.py:41
  61.9 1.8 %shard_map.112 = (f32[14,8192]{1,0:T(8,128)}, f32[14,8192]{1,0:T(8,128)}, f32[14,8192]{1,0:T(8,128)}) custom-call(bf16[2,3,14,16,512]{4,3,2,1,0:T(8,128)(2,1)S(1)} %get-tuple-element.26.own, bf16[2,3,14,16,512]{4,3,2,1,0:T(8,128)(2,1)S(1)} %collective-permute-done.11.r1, bf16[3,14,16,512]{3,2,1,0:T(8,128)(2,1)S(1)} %collective-permute-done.12.r2), custom_call_target="tpu_custom_call" | custom-call | flops 1000000000 | bytes 6291456 | tf_op jit(solution)/shard_map/pallas_call | solution.py:240
  (15 shorter events, 0.2 us)
Async XLA Ops:
  0.6 17.1 %collective-permute-start.8 = (bf16[128,8192]{1,0:T(8,128)(2,1)}, bf16[128,8192]{1,0:T(8,128)(2,1)S(1)}, u32[]{:S(2)}, u32[]{:S(2)}) collective-permute-start(bf16[128,8192]{1,0:T(8,128)(2,1)} %h_hbm.1), channel_id=1, source_target_pairs={{0,16},{1,17},{2,18},{3,19},{4,20},{5,21},{6,22},{7,23},{8,24},{9,... | collective-permute-start | bytes 6291464 | tf_op jit(solution)/shard_map/ppermute | solution.py:41
  0.7 17.0 %collective-permute-start.9 = (bf16[128,8192]{1,0:T(8,128)(2,1)}, bf16[128,8192]{1,0:T(8,128)(2,1)}, u32[]{:S(2)}, u32[]{:S(2)}) collective-permute-start(bf16[128,8192]{1,0:T(8,128)(2,1)} %d_hbm.1), channel_id=1, source_target_pairs={{0,16},{1,17},{2,18},{3,19},{4,20},{5,21},{6,22},{7,23},{8,24},{9,... | collective-permute-start | bytes 6291464 | tf_op jit(solution)/shard_map/ppermute | solution.py:41
  4.0 13.7 %copy-start = (s32[14,4]{1,0:T(8,128)S(1)}, s32[14,4]{1,0:T(8,128)}, u32[]{:S(2)}) copy-start(s32[14,4]{1,0:T(8,128)} %copy.12.lin_hbm.lin) | copy-start | bytes 676
  4.0 13.7 %copy-start.1 = (s32[14,4]{1,0:T(8,128)S(1)}, s32[14,4]{1,0:T(8,128)}, u32[]{:S(2)}) copy-start(s32[14,4]{1,0:T(8,128)} %copy.13.lout_hbm.lout) | copy-start | bytes 676
  13.2 14.9 %collective-permute-start = (bf16[2,4,128,512]{3,2,1,0:T(8,128)(2,1)S(1)}, bf16[2,4,128,512]{3,2,1,0:T(8,128)(2,1)S(1)}, u32[]{:S(2)}, u32[]{:S(2)}) collective-permute-start(bf16[2,4,128,512]{3,2,1,0:T(8,128)(2,1)S(1)} %get-tuple-element.19), channel_id=1, source_target_pairs={{0,1},{1,0},{2,3},{3,2},{4,5},{5,4},{6,7},{7,6},{8,9},{9,8},{10,11... | collective-permute-start | bytes 3145736 | tf_op jit(solution)/shard_map/ppermute | solution.py:41
  14.8 2.9 %collective-permute-start.10 = (bf16[3,14,4,16,128]{4,3,2,1,0:T(8,128)(2,1)S(1)}, bf16[3,14,4,16,128]{4,3,2,1,0:T(8,128)(2,1)S(1)}, u32[]{:S(2)}, u32[]{:S(2)}) collective-permute-start(bf16[3,14,4,16,128]{4,3,2,1,0:T(8,128)(2,1)S(1)} %get-tuple-element.25), channel_id=1, source_target_pairs={{0,16},{1,17},{2,18},{3,19},{4,20},{5,21},{6,22},{7,23},{8,24},{9,... | collective-permute-start | bytes 2064392 | tf_op jit(solution)/shard_map/ppermute | solution.py:41
  15.9 15.2 %collective-permute-start.4 = (bf16[2,4,128,512]{3,2,1,0:T(8,128)(2,1)S(1)}, bf16[2,4,128,512]{3,2,1,0:T(8,128)(2,1)S(1)}, u32[]{:S(2)}, u32[]{:S(2)}) collective-permute-start(bf16[2,4,128,512]{3,2,1,0:T(8,128)(2,1)S(1)} %get-tuple-element.21), channel_id=1, source_target_pairs={{0,4},{1,5},{2,6},{3,7},{4,0},{5,1},{6,2},{7,3},{8,12},{9,13},{10,... | collective-permute-start | bytes 3145736 | tf_op jit(solution)/shard_map/ppermute | solution.py:41
  22.7 25.9 %collective-permute-start.11 = (bf16[2,3,14,16,512]{4,3,2,1,0:T(8,128)(2,1)S(1)}, bf16[2,3,14,16,512]{4,3,2,1,0:T(8,128)(2,1)S(1)}, u32[]{:S(2)}, u32[]{:S(2)}) collective-permute-start(bf16[2,3,14,16,512]{4,3,2,1,0:T(8,128)(2,1)S(1)} %get-tuple-element.27), channel_id=1, source_target_pairs={{0,32},{1,33},{2,34},{3,35},{4,36},{5,37},{6,38},{7,39},{8,40},{9,... | collective-permute-start | bytes 4128776 | tf_op jit(solution)/shard_map/ppermute | solution.py:41
  28.2 10.5 %collective-permute-start.1 = (bf16[4,128,512]{2,1,0:T(8,128)(2,1)S(1)}, bf16[4,128,512]{2,1,0:T(8,128)(2,1)S(1)}, u32[]{:S(2)}, u32[]{:S(2)}) collective-permute-start(bf16[4,128,512]{2,1,0:T(8,128)(2,1)S(1)} %fusion.3), channel_id=1, source_target_pairs={{0,3},{1,2},{2,1},{3,0},{4,7},{5,6},{6,5},{7,4},{8,11},{9,10},{10,... | collective-permute-start | bytes 1572872 | tf_op jit(solution)/shard_map/ppermute | solution.py:41
  31.3 11.1 %collective-permute-start.5 = (bf16[4,128,512]{2,1,0:T(8,128)(2,1)S(1)}, bf16[4,128,512]{2,1,0:T(8,128)(2,1)S(1)}, u32[]{:S(2)}, u32[]{:S(2)}) collective-permute-start(bf16[4,128,512]{2,1,0:T(8,128)(2,1)S(1)} %fusion.4), channel_id=1, source_target_pairs={{0,12},{1,13},{2,14},{3,15},{4,8},{5,9},{6,10},{7,11},{8,4},{9,5},... | collective-permute-start | bytes 1572872 | tf_op jit(solution)/shard_map/ppermute | solution.py:41
  38.9 6.5 %collective-permute-start.2 = (bf16[2,128,512]{2,1,0:T(8,128)(2,1)S(1)}, bf16[2,128,512]{2,1,0:T(8,128)(2,1)S(1)}, u32[]{:S(2)}, u32[]{:S(2)}) collective-permute-start(bf16[2,128,512]{2,1,0:T(8,128)(2,1)S(1)} %slice.83), channel_id=1, source_target_pairs={{0,4},{1,5},{2,6},{3,7},{4,0},{5,1},{6,2},{7,3},{8,12},{9,13},{10,... | collective-permute-start | bytes 786440 | tf_op jit(solution)/shard_map/ppermute | solution.py:41
  42.6 10.3 %collective-permute-start.6 = (bf16[2,128,512]{2,1,0:T(8,128)(2,1)S(1)}, bf16[2,128,512]{2,1,0:T(8,128)(2,1)S(1)}, u32[]{:S(2)}, u32[]{:S(2)}) collective-permute-start(bf16[2,128,512]{2,1,0:T(8,128)(2,1)S(1)} %slice.90), channel_id=1, source_target_pairs={{0,1},{1,0},{2,3},{3,2},{4,5},{5,4},{6,7},{7,6},{8,9},{9,8},{10,11... | collective-permute-start | bytes 786440 | tf_op jit(solution)/shard_map/ppermute | solution.py:41
  45.4 10.5 %collective-permute-start.3 = (bf16[128,512]{1,0:T(8,128)(2,1)S(1)}, bf16[128,512]{1,0:T(8,128)(2,1)S(1)}, u32[]{:S(2)}, u32[]{:S(2)}) collective-permute-start(bf16[128,512]{1,0:T(8,128)(2,1)S(1)} %fusion.7), channel_id=1, source_target_pairs={{0,12},{1,13},{2,14},{3,15},{4,8},{5,9},{6,10},{7,11},{8,4},{9,5},... | collective-permute-start | bytes 393224 | tf_op jit(solution)/shard_map/ppermute | solution.py:41
  48.8 13.0 %collective-permute-start.12 = (bf16[3,14,16,512]{3,2,1,0:T(8,128)(2,1)S(1)}, bf16[3,14,16,512]{3,2,1,0:T(8,128)(2,1)S(1)}, u32[]{:S(2)}, u32[]{:S(2)}) collective-permute-start(bf16[3,14,16,512]{3,2,1,0:T(8,128)(2,1)S(1)} %fusion.2), channel_id=1, source_target_pairs={{0,96},{1,97},{2,98},{3,99},{4,100},{5,101},{6,102},{7,103},{8,104... | collective-permute-start | bytes 2064392 | tf_op jit(solution)/shard_map/ppermute | solution.py:41
  53.0 6.3 %collective-permute-start.7 = (bf16[128,512]{1,0:T(8,128)(2,1)S(1)}, bf16[128,512]{1,0:T(8,128)(2,1)S(1)}, u32[]{:S(2)}, u32[]{:S(2)}) collective-permute-start(bf16[128,512]{1,0:T(8,128)(2,1)S(1)} %fusion.8), channel_id=1, source_target_pairs={{0,3},{1,2},{2,1},{3,0},{4,7},{5,6},{6,5},{7,4},{8,11},{9,10},{10,... | collective-permute-start | bytes 393224 | tf_op jit(solution)/shard_map/ppermute | solution.py:41

commit v3 on v2

--- a/solution.py
+++ b/solution.py
@@ -54,7 +54,7 @@
 
 def gather_cols(ref, lay, r):
     return jnp.concatenate(
-        [ref[:, pl.ds(pl.multiple_of(lay[r, k] * BLK, BLK), BLK)] for k in range(KB)], axis=1
+        [ref[:, pl.ds(pl.multiple_of(lay[k, r] * BLK, BLK), BLK)] for k in range(KB)], axis=1
     )
 
 
@@ -127,9 +127,9 @@
             part = dot(hid[r], wd[sl])
             dhx = dot(dgu[r], jnp.concatenate([wg[sl], wu[sl]], axis=0))
             for k in range(KB):
-                acc_p[lout[r, k]] += part[:, k * BLK : (k + 1) * BLK]
+                acc_p[lout[k, r]] += part[:, k * BLK : (k + 1) * BLK]
             for k in range(KB):
-                acc_q[lin[r, k]] += dhx[:, k * BLK : (k + 1) * BLK]
+                acc_q[lin[k, r]] += dhx[:, k * BLK : (k + 1) * BLK]
             for a in range(3):
                 for q in range(4):
                     keep[a, r, q] = turned[r, a, mine[q]]
@@ -207,7 +207,7 @@
     chunks = V((2, 4, TOK, W), BF16)
     weight = V((ROWS * BLK, W), BF16)
     total = V((NBLK, TOK, BLK), F32)
-    layout = pltpu.SMEM((ROWS, KB), jnp.int32)
+    layout = pltpu.SMEM((KB, ROWS), jnp.int32)
     return pl.pallas_call(
         main_kernel,
         in_specs=[IN_SMEM] + [ANYWHERE] * 7,
@@ -252,16 +252,12 @@
     return sum(t.astype(F32) for t in terms).astype(BF16)
 
 
-def ring_pair(sent, kept, first, second):
-    r1 = send(sent, first, 0)
-    r2 = send(add(kept[1], r1[1]), first, 1)
-    mid = add(kept[0], r1[0], r2)
-    r3 = send(mid[0:2], second, 0)
-    r4 = send(add(mid[3], r3[1]), second, 1)
-    return add(mid[2], r3[0], r4)
+def after(value, other):
+    return lax.optimization_barrier((value, other))[0]
 
 
 def shards(h_in, dout, w_gate, w_up, w_down, in_layout, out_layout):
+    in_layout, out_layout = in_layout.T, out_layout.T
     dp, t = lax.axis_index("dp"), lax.axis_index("tensor")
     pos = jnp.stack([dp // 2, dp % 2, t // 4, t % 4]).astype(jnp.int32)
     h_other = send(h_in, "core")
@@ -271,11 +267,21 @@
     )
     taken = send(give, "core")
     g_sent, g_kept = grads_call(in_layout, out_layout, h_own, h_other, d_own, d_other, keep, taken)
+    p1, q1 = send(p_sent, "x", 0), send(q_sent, "y", 0)
     g1 = send(g_sent, "z", 0)
-    g2 = send(add(g_kept[1], g1[1]), "z", 1)
+    p2 = send(add(p_kept[1], p1[1]), "x", 1)
+    q2 = send(add(q_kept[1], q1[1]), "y", 1)
+    p_mid = add(p_kept[0], p1[0], p2)
+    p3 = send(p_mid[0:2], "y", 0)
+    g_half = add(g_kept[1], after(g1, p_mid)[1])
+    g2 = send(g_half, "z", 1)
+    q_mid = add(q_kept[0], q1[0], after(q2, g_half))
+    q3 = send(q_mid[0:2], "x", 0)
+    p4 = send(add(p_mid[3], p3[1]), "y", 1)
+    q4 = send(add(q_mid[3], q3[1]), "x", 1)
     g_gate, g_up, g_down = finish_call(g_kept, g1, g2)
-    out = ring_pair(p_sent, p_kept, "x", "y")
-    dh = ring_pair(q_sent, q_kept, "y", "x")
+    out = add(p_mid[2], p3[0], after(p4, g_gate))
+    dh = add(q_mid[2], q3[0], after(q4, g_gate))
     return (out, dh, g_gate, g_up, g_down)
 
 

time: 63.9 us -> 57.8 us (0.905); the launches traced: 63.7 us -> 56.8 us
  waiting for transfers between devices: 16.8 us -> 13.7 us
  local copies, waits for them, and re-layouts: 2.77 us -> 0.05 us
  starting transfers between devices: 24.9 us -> 23.9 us
    ppermute x13, waiting for transfers between devices: 16.8 us -> 13.7 us  [send(): return lax.ppermute(a, AXES, pairs(axis, step))]
    unnamed x6 -> x4, local copies, waits for them, and re-layouts: 2.73 us -> 0.01 us
    ppermute x13, starting transfers between devices: 24.9 us -> 23.9 us  [send(): return lax.ppermute(a, AXES, pairs(axis, step))]
  transfers between devices with their start and end apart: 13 -> 13, of which waited for: 7 -> 4; matrix products, arithmetic and copies ran while one was open for 8% -> 2% of each run, Pallas kernels for 22% -> 28%
where the time goes in v3:
time: 57.8 us; the launch traced here: 56.8 us
  starting transfers between devices  23.9 us (41%)
  Pallas kernels  15.9 us (28%)
  waiting for transfers between devices  13.7 us (24%)
  other arithmetic  2.51 us (4%)
  between operations  0.73 us (1%)
    ppermute x13, starting transfers between devices, send(): return lax.ppermute(a, AXES, pairs(axis, step))  23.9 us
    ppermute x13, waiting for transfers between devices, send(): return lax.ppermute(a, AXES, pairs(axis, step))  13.7 us
    pallas_call x1, Pallas kernels, main_call(): pl.pallas_call(main_kernel, in_specs=[IN_SMEM] + [ANYWHERE] * 7, out_spec...  9.18 us
    pallas_call x1, Pallas kernels, grads_call(): pl.pallas_call(grads_kernel, in_specs=[IN_SMEM] * 2 + [IN_VMEM] * 6, out_...  4.97 us
    convert_element_type x9, other arithmetic, add(): return sum((t.astype(F32) for t in terms)).astype(BF16)  2.43 us
    pallas_call x1, Pallas kernels, finish_call(): pl.pallas_call(finish_kernel, in_specs=[IN_VMEM] * 3, out_specs=[IN_VMEM]...  1.8 us
  transfers between devices with their start and end apart: 13, of which 4 were waited for; matrix products, arithmetic and copies ran while one was open for 2% of the time, Pallas kernels for 28%

profile of v3, /device:TPU:0, one launch (start us, length us, event | category | flops | bytes accessed | tf_op | source)
XLA Modules:
  0.0 56.8 jit_solution(2278576881552182102)
XLA Ops:
  0.6 0.1 collective-permute-start.4
  0.7 0.5 collective-permute-start.5
  1.2 0.1 pad_add_fusion.pos
  1.3 9.2 %shard_map.110 = (bf16[3,14,4,16,128]{4,3,2,1,0:T(8,128)(2,1)S(1)}, bf16[3,14,4,16,128]{4,3,2,1,0:T(8,128)(2,1)S(1)}, bf16[2,4,128,512]{3,2,1,0:T(8,128)(2,1)S(1...) custom-call(s32[4]{0:T(128)S(1)} %pad_add_fusion.pos, ...), custom_call_target="tpu_custom_call" | custom-call | flops 1000000000 | bytes 25165824 | tf_op jit(solution)/shard_map/pallas_call | solution.py:211
  10.5 0.2 collective-permute-start.6
  10.7 1.6 %collective-permute-start = (bf16[2,4,128,512]{3,2,1,0:T(8,128)(2,1)S(1)}, bf16[2,4,128,512]{3,2,1,0:T(8,128)(2,1)S(1)}, u32[]{:S(2)}, u32[]{:S(2)}) collective-permute-start(bf16[2,4,128,512]{3,2,1,0:T(8,128)(2,1)S(1)} %get-tuple-element.23), channel_id=1, source_target_pairs={{0,1},{1,0},{2,3},{3,2},{4,5},{5,4},{6,7},{7,6},{8,9},{9,8},{10,11... | collective-permute-start | bytes 3145736 | tf_op jit(solution)/shard_map/ppermute | solution.py:41
  12.2 1.6 %collective-permute-start.9 = (bf16[2,4,128,512]{3,2,1,0:T(8,128)(2,1)S(1)}, bf16[2,4,128,512]{3,2,1,0:T(8,128)(2,1)S(1)}, u32[]{:S(2)}, u32[]{:S(2)}) collective-permute-start(bf16[2,4,128,512]{3,2,1,0:T(8,128)(2,1)S(1)} %get-tuple-element.34), channel_id=1, source_target_pairs={{0,4},{1,5},{2,6},{3,7},{4,0},{5,1},{6,2},{7,3},{8,12},{9,13},{10,... | collective-permute-start | bytes 3145736 | tf_op jit(solution)/shard_map/ppermute | solution.py:41
  13.8 5.0 %shard_map.111 = (bf16[2,3,14,16,512]{4,3,2,1,0:T(8,128)(2,1)S(1)}, bf16[2,3,14,16,512]{4,3,2,1,0:T(8,128)(2,1)S(1)}) custom-call(s32[4,14]{1,0:T(4,128)S(1)} %bitcast.33, s32[4,14]{1,0:T(4,128)S(1)} %bitcast.35, bf16[128,8192]{1,0:T(8,128)(2,1)S(1)} %get-tuple-element.24.h0, bf16[128,8192]{1,0:T(8,128)(2,1)S(1)} %collective-permute-done.4.h1, ...), custom_call_target="tpu_custom_call" | custom-call | flops 1000000000 | bytes 12582912 | tf_op jit(solution)/shard_map/pallas_call | solution.py:228
  18.8 2.0 %collective-permute-start.7 = (bf16[2,3,14,16,512]{4,3,2,1,0:T(8,128)(2,1)S(1)}, bf16[2,3,14,16,512]{4,3,2,1,0:T(8,128)(2,1)S(1)}, u32[]{:S(2)}, u32[]{:S(2)}) collective-permute-start(bf16[2,3,14,16,512]{4,3,2,1,0:T(8,128)(2,1)S(1)} %get-tuple-element.29), channel_id=1, source_target_pairs={{0,32},{1,33},{2,34},{3,35},{4,36},{5,37},{6,38},{7,39},{8,40},{9,... | collective-permute-start | bytes 4128776 | tf_op jit(solution)/shard_map/ppermute | solution.py:41
  20.8 4.7 %collective-permute-done = bf16[2,4,128,512]{3,2,1,0:T(8,128)(2,1)S(1)} collective-permute-done((bf16[2,4,128,512]{3,2,1,0:T(8,128)(2,1)S(1)}, bf16[2,4,128,512]{3,2,1,0:T(8,128)(2,1)S(1)}, u32[]{:S(2)}, u32[]{:S(2)}) %collective-permute-start) | collective-permute-done | bytes 1048608 | tf_op jit(solution)/shard_map/ppermute | solution.py:41
  25.5 0.1 fusion.3
  25.6 2.9 %collective-permute-start.1 = (bf16[4,128,512]{2,1,0:T(8,128)(2,1)S(1)}, bf16[4,128,512]{2,1,0:T(8,128)(2,1)S(1)}, u32[]{:S(2)}, u32[]{:S(2)}) collective-permute-start(bf16[4,128,512]{2,1,0:T(8,128)(2,1)S(1)} %fusion.3), channel_id=1, source_target_pairs={{0,3},{1,2},{2,1},{3,0},{4,7},{5,6},{6,5},{7,4},{8,11},{9,10},{10,... | collective-permute-start | bytes 1572872 | tf_op jit(solution)/shard_map/ppermute | solution.py:41
  28.5 0.0 collective-permute-done.9
  28.5 0.1 fusion.4
  28.6 3.1 %collective-permute-start.10 = (bf16[4,128,512]{2,1,0:T(8,128)(2,1)S(1)}, bf16[4,128,512]{2,1,0:T(8,128)(2,1)S(1)}, u32[]{:S(2)}, u32[]{:S(2)}) collective-permute-start(bf16[4,128,512]{2,1,0:T(8,128)(2,1)S(1)} %fusion.4), channel_id=1, source_target_pairs={{0,12},{1,13},{2,14},{3,15},{4,8},{5,9},{6,10},{7,11},{8,4},{9,5},... | collective-permute-start | bytes 1572872 | tf_op jit(solution)/shard_map/ppermute | solution.py:41
  31.8 4.3 %collective-permute-done.1 = bf16[4,128,512]{2,1,0:T(8,128)(2,1)S(1)} collective-permute-done((bf16[4,128,512]{2,1,0:T(8,128)(2,1)S(1)}, bf16[4,128,512]{2,1,0:T(8,128)(2,1)S(1)}, u32[]{:S(2)}, u32[]{:S(2)}) %collective-permute-start.1) | collective-permute-done | bytes 524320 | tf_op jit(solution)/shard_map/ppermute | solution.py:41
  36.1 0.2 fusion.1
  36.3 1.7 %collective-permute-start.2 = (bf16[2,128,512]{2,1,0:T(8,128)(2,1)S(1)}, bf16[2,128,512]{2,1,0:T(8,128)(2,1)S(1)}, u32[]{:S(2)}, u32[]{:S(2)}) collective-permute-start(bf16[2,128,512]{2,1,0:T(8,128)(2,1)S(1)} %slice.83), channel_id=1, source_target_pairs={{0,4},{1,5},{2,6},{3,7},{4,0},{5,1},{6,2},{7,3},{8,12},{9,13},{10,... | collective-permute-start | bytes 786440 | tf_op jit(solution)/shard_map/ppermute | solution.py:41
  38.0 0.0 collective-permute-done.7.r1
  38.0 0.3 fusion.2
  38.3 4.1 %collective-permute-start.8 = (bf16[3,14,16,512]{3,2,1,0:T(8,128)(2,1)S(1)}, bf16[3,14,16,512]{3,2,1,0:T(8,128)(2,1)S(1)}, u32[]{:S(2)}, u32[]{:S(2)}) collective-permute-start(bf16[3,14,16,512]{3,2,1,0:T(8,128)(2,1)S(1)} %fusion.2), channel_id=1, source_target_pairs={{0,96},{1,97},{2,98},{3,99},{4,100},{5,101},{6,102},{7,103},{8,104... | collective-permute-start | bytes 2064392 | tf_op jit(solution)/shard_map/ppermute | solution.py:41
  42.4 0.0 collective-permute-done.10
  42.4 0.2 fusion
  42.7 0.4 collective-permute-start.11
  43.1 2.9 %collective-permute-start.3 = (bf16[128,512]{1,0:T(8,128)(2,1)S(1)}, bf16[128,512]{1,0:T(8,128)(2,1)S(1)}, u32[]{:S(2)}, u32[]{:S(2)}) collective-permute-start(bf16[128,512]{1,0:T(8,128)(2,1)S(1)} %fusion.7), channel_id=1, source_target_pairs={{0,12},{1,13},{2,14},{3,15},{4,8},{5,9},{6,10},{7,11},{8,4},{9,5},... | collective-permute-start | bytes 393224 | tf_op jit(solution)/shard_map/ppermute | solution.py:41
  46.0 3.1 %collective-permute-done.11 = bf16[2,128,512]{2,1,0:T(8,128)(2,1)S(1)} collective-permute-done((bf16[2,128,512]{2,1,0:T(8,128)(2,1)S(1)}, bf16[2,128,512]{2,1,0:T(8,128)(2,1)S(1)}, u32[]{:S(2)}, u32[]{:S(2)}) %collective-permute-start.11) | collective-permute-done | bytes 262176 | tf_op jit(solution)/shard_map/ppermute | solution.py:41
  49.1 2.9 %collective-permute-start.12 = (bf16[128,512]{1,0:T(8,128)(2,1)S(1)}, bf16[128,512]{1,0:T(8,128)(2,1)S(1)}, u32[]{:S(2)}, u32[]{:S(2)}) collective-permute-start(bf16[128,512]{1,0:T(8,128)(2,1)S(1)} %fusion.8), channel_id=1, source_target_pairs={{0,3},{1,2},{2,1},{3,0},{4,7},{5,6},{6,5},{7,4},{8,11},{9,10},{10,... | collective-permute-start | bytes 393224 | tf_op jit(solution)/shard_map/ppermute | solution.py:41
  52.0 1.8 %shard_map.112 = (f32[14,8192]{1,0:T(8,128)}, f32[14,8192]{1,0:T(8,128)}, f32[14,8192]{1,0:T(8,128)}) custom-call(bf16[2,3,14,16,512]{4,3,2,1,0:T(8,128)(2,1)S(1)} %get-tuple-element.28.own, bf16[2,3,14,16,512]{4,3,2,1,0:T(8,128)(2,1)S(1)} %collective-permute-done.7.r1, bf16[3,14,16,512]{3,2,1,0:T(8,128)(2,1)S(1)} %collective-permute-done.8.r2), custom_call_target="tpu_custom_call" | custom-call | flops 1000000000 | bytes 6291456 | tf_op jit(solution)/shard_map/pallas_call | solution.py:240
  53.8 0.0 collective-permute-done.3
  53.8 1.6 %collective-permute-done.12 = bf16[128,512]{1,0:T(8,128)(2,1)S(1)} collective-permute-done((bf16[128,512]{1,0:T(8,128)(2,1)S(1)}, bf16[128,512]{1,0:T(8,128)(2,1)S(1)}, u32[]{:S(2)}, u32[]{:S(2)}) %collective-permute-start.12) | collective-permute-done | bytes 131104 | tf_op jit(solution)/shard_map/ppermute | solution.py:41
  55.4 0.7 %fusion.6 = bf16[128,512]{1,0:T(8,128)(2,1)} fusion(bf16[128,512]{1,0:T(8,128)(2,1)S(1)} %collective-permute-done.3, bf16[2,128,512]{2,1,0:T(8,128)(2,1)S(1)} %collective-permute-done.2, bf16[4,128,512]{2,1,0:T(8,128)(2,1)S(1)} %fusion.1), kind=kLoop, calls=%fused_computation.13 | loop fusion | flops 393216 | bytes 524288 | tf_op jit(solution)/shard_map/convert_element_type | solution.py:252
  56.1 0.7 %fusion.5 = bf16[128,512]{1,0:T(8,128)(2,1)} fusion(bf16[128,512]{1,0:T(8,128)(2,1)S(1)} %collective-permute-done.12, bf16[2,128,512]{2,1,0:T(8,128)(2,1)S(1)} %collective-permute-done.11, bf16[4,128,512]{2,1,0:T(8,128)(2,1)S(1)} %fusion), kind=kLoop, calls=%fused_computation.11 | loop fusion | flops 393216 | bytes 524288 | tf_op jit(solution)/shard_map/convert_element_type | solution.py:252
  (13 shorter events, 0.1 us)
Async XLA Ops:
  0.6 13.2 %collective-permute-start.4 = (bf16[128,8192]{1,0:T(8,128)(2,1)}, bf16[128,8192]{1,0:T(8,128)(2,1)S(1)}, u32[]{:S(2)}, u32[]{:S(2)}) collective-permute-start(bf16[128,8192]{1,0:T(8,128)(2,1)} %h_hbm.1), channel_id=1, source_target_pairs={{0,16},{1,17},{2,18},{3,19},{4,20},{5,21},{6,22},{7,23},{8,24},{9,... | collective-permute-start | bytes 6291464 | tf_op jit(solution)/shard_map/ppermute | solution.py:41
  0.7 13.1 %collective-permute-start.5 = (bf16[128,8192]{1,0:T(8,128)(2,1)}, bf16[128,8192]{1,0:T(8,128)(2,1)}, u32[]{:S(2)}, u32[]{:S(2)}) collective-permute-start(bf16[128,8192]{1,0:T(8,128)(2,1)} %d_hbm.1), channel_id=1, source_target_pairs={{0,16},{1,17},{2,18},{3,19},{4,20},{5,21},{6,22},{7,23},{8,24},{9,... | collective-permute-start | bytes 6291464 | tf_op jit(solution)/shard_map/ppermute | solution.py:41
  1.3 12.5 %copy-start = (s32[14,4]{0,1:T(4,128)S(1)}, s32[14,4]{0,1:T(4,128)}, u32[]{:S(2)}) copy-start(s32[14,4]{0,1:T(4,128)} %param.12) | copy-start | bytes 676
  1.3 12.5 %copy-start.1 = (s32[14,4]{0,1:T(4,128)S(1)}, s32[14,4]{0,1:T(4,128)}, u32[]{:S(2)}) copy-start(s32[14,4]{0,1:T(4,128)} %param.13) | copy-start | bytes 676
  10.5 3.3 %collective-permute-start.6 = (bf16[3,14,4,16,128]{4,3,2,1,0:T(8,128)(2,1)S(1)}, bf16[3,14,4,16,128]{4,3,2,1,0:T(8,128)(2,1)S(1)}, u32[]{:S(2)}, u32[]{:S(2)}) collective-permute-start(bf16[3,14,4,16,128]{4,3,2,1,0:T(8,128)(2,1)S(1)} %get-tuple-element.27), channel_id=1, source_target_pairs={{0,16},{1,17},{2,18},{3,19},{4,20},{5,21},{6,22},{7,23},{8,24},{9,... | collective-permute-start | bytes 2064392 | tf_op jit(solution)/shard_map/ppermute | solution.py:41
  10.7 14.8 %collective-permute-start = (bf16[2,4,128,512]{3,2,1,0:T(8,128)(2,1)S(1)}, bf16[2,4,128,512]{3,2,1,0:T(8,128)(2,1)S(1)}, u32[]{:S(2)}, u32[]{:S(2)}) collective-permute-start(bf16[2,4,128,512]{3,2,1,0:T(8,128)(2,1)S(1)} %get-tuple-element.23), channel_id=1, source_target_pairs={{0,1},{1,0},{2,3},{3,2},{4,5},{5,4},{6,7},{7,6},{8,9},{9,8},{10,11... | collective-permute-start | bytes 3145736 | tf_op jit(solution)/shard_map/ppermute | solution.py:41
  12.2 16.3 %collective-permute-start.9 = (bf16[2,4,128,512]{3,2,1,0:T(8,128)(2,1)S(1)}, bf16[2,4,128,512]{3,2,1,0:T(8,128)(2,1)S(1)}, u32[]{:S(2)}, u32[]{:S(2)}) collective-permute-start(bf16[2,4,128,512]{3,2,1,0:T(8,128)(2,1)S(1)} %get-tuple-element.34), channel_id=1, source_target_pairs={{0,4},{1,5},{2,6},{3,7},{4,0},{5,1},{6,2},{7,3},{8,12},{9,13},{10,... | collective-permute-start | bytes 3145736 | tf_op jit(solution)/shard_map/ppermute | solution.py:41
  18.8 19.2 %collective-permute-start.7 = (bf16[2,3,14,16,512]{4,3,2,1,0:T(8,128)(2,1)S(1)}, bf16[2,3,14,16,512]{4,3,2,1,0:T(8,128)(2,1)S(1)}, u32[]{:S(2)}, u32[]{:S(2)}) collective-permute-start(bf16[2,3,14,16,512]{4,3,2,1,0:T(8,128)(2,1)S(1)} %get-tuple-element.29), channel_id=1, source_target_pairs={{0,32},{1,33},{2,34},{3,35},{4,36},{5,37},{6,38},{7,39},{8,40},{9,... | collective-permute-start | bytes 4128776 | tf_op jit(solution)/shard_map/ppermute | solution.py:41
  25.6 10.5 %collective-permute-start.1 = (bf16[4,128,512]{2,1,0:T(8,128)(2,1)S(1)}, bf16[4,128,512]{2,1,0:T(8,128)(2,1)S(1)}, u32[]{:S(2)}, u32[]{:S(2)}) collective-permute-start(bf16[4,128,512]{2,1,0:T(8,128)(2,1)S(1)} %fusion.3), channel_id=1, source_target_pairs={{0,3},{1,2},{2,1},{3,0},{4,7},{5,6},{6,5},{7,4},{8,11},{9,10},{10,... | collective-permute-start | bytes 1572872 | tf_op jit(solution)/shard_map/ppermute | solution.py:41
  28.6 13.8 %collective-permute-start.10 = (bf16[4,128,512]{2,1,0:T(8,128)(2,1)S(1)}, bf16[4,128,512]{2,1,0:T(8,128)(2,1)S(1)}, u32[]{:S(2)}, u32[]{:S(2)}) collective-permute-start(bf16[4,128,512]{2,1,0:T(8,128)(2,1)S(1)} %fusion.4), channel_id=1, source_target_pairs={{0,12},{1,13},{2,14},{3,15},{4,8},{5,9},{6,10},{7,11},{8,4},{9,5},... | collective-permute-start | bytes 1572872 | tf_op jit(solution)/shard_map/ppermute | solution.py:41
  36.3 6.7 %collective-permute-start.2 = (bf16[2,128,512]{2,1,0:T(8,128)(2,1)S(1)}, bf16[2,128,512]{2,1,0:T(8,128)(2,1)S(1)}, u32[]{:S(2)}, u32[]{:S(2)}) collective-permute-start(bf16[2,128,512]{2,1,0:T(8,128)(2,1)S(1)} %slice.83), channel_id=1, source_target_pairs={{0,4},{1,5},{2,6},{3,7},{4,0},{5,1},{6,2},{7,3},{8,12},{9,13},{10,... | collective-permute-start | bytes 786440 | tf_op jit(solution)/shard_map/ppermute | solution.py:41
  38.3 13.7 %collective-permute-start.8 = (bf16[3,14,16,512]{3,2,1,0:T(8,128)(2,1)S(1)}, bf16[3,14,16,512]{3,2,1,0:T(8,128)(2,1)S(1)}, u32[]{:S(2)}, u32[]{:S(2)}) collective-permute-start(bf16[3,14,16,512]{3,2,1,0:T(8,128)(2,1)S(1)} %fusion.2), channel_id=1, source_target_pairs={{0,96},{1,97},{2,98},{3,99},{4,100},{5,101},{6,102},{7,103},{8,104... | collective-permute-start | bytes 2064392 | tf_op jit(solution)/shard_map/ppermute | solution.py:41
  42.7 6.5 %collective-permute-start.11 = (bf16[2,128,512]{2,1,0:T(8,128)(2,1)S(1)}, bf16[2,128,512]{2,1,0:T(8,128)(2,1)S(1)}, u32[]{:S(2)}, u32[]{:S(2)}) collective-permute-start(bf16[2,128,512]{2,1,0:T(8,128)(2,1)S(1)} %slice.90), channel_id=1, source_target_pairs={{0,1},{1,0},{2,3},{3,2},{4,5},{5,4},{6,7},{7,6},{8,9},{9,8},{10,11... | collective-permute-start | bytes 786440 | tf_op jit(solution)/shard_map/ppermute | solution.py:41
  43.1 10.8 %collective-permute-start.3 = (bf16[128,512]{1,0:T(8,128)(2,1)S(1)}, bf16[128,512]{1,0:T(8,128)(2,1)S(1)}, u32[]{:S(2)}, u32[]{:S(2)}) collective-permute-start(bf16[128,512]{1,0:T(8,128)(2,1)S(1)} %fusion.7), channel_id=1, source_target_pairs={{0,12},{1,13},{2,14},{3,15},{4,8},{5,9},{6,10},{7,11},{8,4},{9,5},... | collective-permute-start | bytes 393224 | tf_op jit(solution)/shard_map/ppermute | solution.py:41
  49.1 6.3 %collective-permute-start.12 = (bf16[128,512]{1,0:T(8,128)(2,1)S(1)}, bf16[128,512]{1,0:T(8,128)(2,1)S(1)}, u32[]{:S(2)}, u32[]{:S(2)}) collective-permute-start(bf16[128,512]{1,0:T(8,128)(2,1)S(1)} %fusion.8), channel_id=1, source_target_pairs={{0,3},{1,2},{2,1},{3,0},{4,7},{5,6},{6,5},{7,4},{8,11},{9,10},{10,... | collective-permute-start | bytes 393224 | tf_op jit(solution)/shard_map/ppermute | solution.py:41

commit v4 on v3

--- a/solution.py
+++ b/solution.py
@@ -58,9 +58,9 @@
     )
 
 
-def emit_chunks(acc, outer, inner, transposed, sent, kept):
+def emit_chunks(acc, outer, inner, transposed, sent, stay):
     for p in range(4):
-        dst = sent if p < 2 else kept
+        dst = sent if p < 2 else stay
         for q in range(4):
             y, x = (inner[q], outer[p]) if transposed else (outer[p], inner[q])
             base = (y * 4 + x) * 4
@@ -70,7 +70,7 @@
 
 def main_kernel(
     pos, lin_hbm, lout_hbm, h_hbm, d_hbm, wg_hbm, wu_hbm, wd_hbm,
-    keep, give, p_sent, p_kept, q_sent, q_kept, h, d,
+    keep, give, p_sent, p_stay, q_sent, q_stay, h, d,
     wg, wu, wd, acc_p, acc_q, hid, dgu, turned, lin, lout, sem, w_sem,
 ):
     small = [
@@ -135,44 +135,51 @@
                     keep[a, r, q] = turned[r, a, mine[q]]
                     give[a, r, q] = turned[r, a, others[q]]
 
-    def both(s):
+    units(0)
+    for c in late:
+        c.wait()
+    for s in range(1, ROWS // UNROLL):
         features(s - 1)
         units(s)
-
-    units(0)
-    pl.loop(1, EARLY // UNROLL)(both)
-    for c in late:
-        c.wait()
-    pl.loop(EARLY // UNROLL, ROWS // UNROLL)(both)
     features(ROWS // UNROLL - 1)
     xs, ys = ring_order(pos[3], core), ring_order(pos[2], core)
-    emit_chunks(acc_p, xs, ys, True, p_sent, p_kept)
-    emit_chunks(acc_q, ys, xs, False, q_sent, q_kept)
-
-
-def grads_kernel(lin, lout, h0, h1, d0, d1, act0, act1, sent, kept):
-    @pl.loop(0, ROWS // UNROLL)
-    def _(s):
-        for i in range(UNROLL):
-            r = s * UNROLL + i
-            hx = jnp.concatenate([gather_cols(h0, lin, r), gather_cols(h1, lin, r)], axis=0)
-            dob = jnp.concatenate([gather_cols(d0, lout, r), gather_cols(d1, lout, r)], axis=0)
-            act = [
-                jnp.concatenate([act0[a, r].reshape(64, TOK), act1[a, r].reshape(64, TOK)], axis=1)
-                for a in range(3)
-            ]
-            g_in = dot(jnp.concatenate(act[1:], axis=0), hx).astype(BF16).reshape(2, 4, 16, W)
-            g_down = dot(act[0], dob).astype(BF16).reshape(4, 16, W)
-            for q in range(4):
-                dst = sent if q < 2 else kept
-                dst[q % 2, 0, r] = g_in[0, q]
-                dst[q % 2, 1, r] = g_in[1, q]
-                dst[q % 2, 2, r] = g_down[q]
+    emit_chunks(acc_p, xs, ys, True, p_sent, p_stay)
+    emit_chunks(acc_q, ys, xs, False, q_sent, q_stay)
+
+
+def pair_rows(a, b):
+    return jnp.concatenate([a, b], axis=0)
+
+
+def units_of(act0, act1, a, r):
+    return jnp.concatenate([act0[a, r].reshape(64, TOK), act1[a, r].reshape(64, TOK)], axis=1)
+
+
+def grads_kernel(lin, lout, h0, h1, d0, act0, act1, d1_in, keeps, passes, own, after_next, d1, sem):
+    copy = pltpu.make_async_copy(d1_in, d1, sem)
+    copy.start()
+
+    def put(g, r, rows):
+        for q, dst in enumerate((keeps, passes, own, after_next)):
+            dst[g, r] = rows[q * 16 : (q + 1) * 16]
+
+    for r in range(ROWS):
+        hx = pair_rows(gather_cols(h0, lin, r), gather_cols(h1, lin, r))
+        dgu = pair_rows(units_of(act0, act1, 1, r), units_of(act0, act1, 2, r))
+        g = dot(dgu, hx).astype(BF16)
+        put(0, r, g[:64])
+        put(1, r, g[64:])
+
+    copy.wait()
+
+    for r in range(ROWS):
+        dob = pair_rows(gather_cols(d0, lout, r), gather_cols(d1, lout, r))
+        put(2, r, dot(units_of(act0, act1, 0, r), dob).astype(BF16))
 
 
 def finish_kernel(own, r1, r2, gate, up, down, tmp):
     for g, out in enumerate((gate, up, down)):
-        total = own[0, g].astype(F32) + r1[0, g].astype(F32) + r2[g].astype(F32)
+        total = own[g].astype(F32) + r1[g].astype(F32) + r2[g].astype(F32)
         total = total.reshape(ROWS * 16, W)
         for k in range(KB):
             tmp[k] = total[:, k * BLK : (k + 1) * BLK]
@@ -186,8 +193,8 @@
 IN_SMEM = pl.BlockSpec(memory_space=pltpu.SMEM)
 IN_VMEM = pl.BlockSpec(memory_space=pltpu.VMEM)
 ANYWHERE = pl.BlockSpec(memory_space=pl.ANY)
-UNROLL = 2
-EARLY = 4
+UNROLL = 7
+EARLY = 7
 
 
 def in_hbm(*arrays):
@@ -199,7 +206,7 @@
 
 
 def cost(mib):
-    return pl.CostEstimate(flops=10**9, bytes_accessed=mib * 2**20, transcendentals=0)
+    return pl.CostEstimate(flops=0, bytes_accessed=mib * 2**10, transcendentals=0)
 
 
 def main_call(pos, *arrays):
@@ -212,7 +219,7 @@
         main_kernel,
         in_specs=[IN_SMEM] + [ANYWHERE] * 7,
         out_specs=[IN_VMEM] * 8,
-        out_shape=[act, act, chunks, chunks, chunks, chunks, V((TOK, D), BF16), V((TOK, D), BF16)],
+        out_shape=[act, act] + [chunks] * 4 + [V((TOK, D), BF16)] * 2,
         scratch_shapes=[
             weight, weight, weight, total, total,
             V((ROWS, TOK, BLK), BF16), V((ROWS, TOK, 2 * BLK), BF16), V((ROWS, 3, 8, 16, TOK), BF16),
@@ -223,16 +230,19 @@
     )(pos, *in_hbm(*arrays))
 
 
-def grads_call(lin, lout, *arrays):
-    out = V((2, 3, ROWS, 16, W), BF16)
+GRADS = V((3, ROWS, 16, W), BF16)
+
+
+def grads_call(lin, lout, h0, h1, d0, act0, act1, d1):
     return pl.pallas_call(
         grads_kernel,
-        in_specs=[IN_SMEM] * 2 + [IN_VMEM] * 6,
-        out_specs=[IN_VMEM] * 2,
-        out_shape=[out, out],
-        compiler_params=pltpu.CompilerParams(vmem_limit_bytes=4 * 2**20),
-        cost_estimate=cost(12),
-    )(lin, lout, *in_vmem(*arrays))
+        in_specs=[IN_SMEM] * 2 + [IN_VMEM] * 5 + [ANYWHERE],
+        out_specs=[IN_VMEM] * 4,
+        out_shape=[GRADS] * 4,
+        scratch_shapes=[V((TOK, D), BF16), pltpu.SemaphoreType.DMA],
+        compiler_params=pltpu.CompilerParams(vmem_limit_bytes=6 * 2**20),
+        cost_estimate=pl.CostEstimate(flops=10**10, bytes_accessed=128 * 2**20, transcendentals=0),
+    )(lin, lout, *in_vmem(h0, h1, d0, act0, act1), d1)
 
 
 def finish_call(*arrays):
@@ -244,7 +254,7 @@
         out_shape=[out] * 3,
         scratch_shapes=[V((KB, ROWS * 16, BLK), F32)],
         compiler_params=pltpu.CompilerParams(vmem_limit_bytes=8 * 2**20),
-        cost_estimate=cost(6),
+        cost_estimate=pl.CostEstimate(flops=10**9, bytes_accessed=6 * 2**20, transcendentals=0),
     )(*in_vmem(*arrays))
 
 
@@ -262,26 +272,29 @@
     pos = jnp.stack([dp // 2, dp % 2, t // 4, t % 4]).astype(jnp.int32)
     h_other = send(h_in, "core")
     d_other = send(dout, "core")
-    keep, give, p_sent, p_kept, q_sent, q_kept, h_own, d_own = main_call(
+    keep, give, p_sent, p_own, q_sent, q_own, h_own, d_own = main_call(
         pos, in_layout, out_layout, h_in, dout, w_gate, w_up, w_down
     )
     taken = send(give, "core")
-    g_sent, g_kept = grads_call(in_layout, out_layout, h_own, h_other, d_own, d_other, keep, taken)
     p1, q1 = send(p_sent, "x", 0), send(q_sent, "y", 0)
-    g1 = send(g_sent, "z", 0)
-    p2 = send(add(p_kept[1], p1[1]), "x", 1)
-    q2 = send(add(q_kept[1], q1[1]), "y", 1)
-    p_mid = add(p_kept[0], p1[0], p2)
+    g_keeps, g_passes, g_own, g_next = grads_call(
+        in_layout, out_layout, h_own, h_other, d_own, keep, taken, d_other
+    )
+    g1 = send(g_passes, "z", 0)
+    g1k = send(g_keeps, "z", 0)
+    p2 = send(add(p_own[1], p1[1]), "x", 1)
+    q2 = send(add(q_own[1], q1[1]), "y", 1)
+    g2_in = add(g_next, g1)
+    g2 = send(g2_in, "z", 1)
+    p_mid = add(p_own[0], p1[0], after(p2, g2_in))
     p3 = send(p_mid[0:2], "y", 0)
-    g_half = add(g_kept[1], after(g1, p_mid)[1])
-    g2 = send(g_half, "z", 1)
-    q_mid = add(q_kept[0], q1[0], after(q2, g_half))
+    q_mid = add(q_own[0], q1[0], after(q2, p_mid))
     q3 = send(q_mid[0:2], "x", 0)
     p4 = send(add(p_mid[3], p3[1]), "y", 1)
-    q4 = send(add(q_mid[3], q3[1]), "x", 1)
-    g_gate, g_up, g_down = finish_call(g_kept, g1, g2)
-    out = add(p_mid[2], p3[0], after(p4, g_gate))
-    dh = add(q_mid[2], q3[0], after(q4, g_gate))
+    q4 = send(add(q_mid[3], after(q3, g1k)[1]), "x", 1)
+    g_gate, g_up, g_down = finish_call(g_own, g1k, g2)
+    out = add(p_mid[2], p3[0], after(p4, g_down))
+    dh = add(q_mid[2], q3[0], after(q4, g_down))
     return (out, dh, g_gate, g_up, g_down)
 
 

time: 57.8 us -> 56.6 us (0.979)
  waiting for transfers between devices: 13.7 us -> 16.5 us
  starting transfers between devices: 23.9 us -> 21.3 us
  Pallas kernels: 15.9 us -> 14.4 us
    ppermute x13 -> x14, waiting for transfers between devices: 13.7 us -> 16.5 us  [send(): return lax.ppermute(a, AXES, pairs(axis, step))]
    ppermute x13 -> x14, starting transfers between devices: 23.9 us -> 21.3 us  [send(): return lax.ppermute(a, AXES, pairs(axis, step))]
    pallas_call x1, Pallas kernels: 9.18 us -> 7.94 us  [main_call(): pl.pallas_call(main_kernel, in_specs=[IN_SMEM] + [ANYWHERE] * 7, out_spec...]
  transfers between devices with their start and end apart: 13 -> 14, of which waited for: 4 -> 5; matrix products, arithmetic and copies ran while one was open for 2% -> 2% of each run, Pallas kernels for 28% -> 26%
where the time goes in v4:
time: 56.6 us; the launch traced here: 55.5 us
  starting transfers between devices  21.3 us (38%)
  waiting for transfers between devices  16.5 us (29%)
  Pallas kernels  14.4 us (25%)
  other arithmetic  2.5 us (4%)
  between operations  0.74 us (1%)
    ppermute x14, starting transfers between devices, send(): return lax.ppermute(a, AXES, pairs(axis, step))  21.3 us
    ppermute x14, waiting for transfers between devices, send(): return lax.ppermute(a, AXES, pairs(axis, step))  16.5 us
    pallas_call x1, Pallas kernels, main_call(): pl.pallas_call(main_kernel, in_specs=[IN_SMEM] + [ANYWHERE] * 7, out_spec...  7.94 us
    pallas_call x1, Pallas kernels, grads_call(): pl.pallas_call(grads_kernel, in_specs=[IN_SMEM] * 2 + [IN_VMEM] * 5 + [AN...  4.7 us
    convert_element_type x9, other arithmetic, add(): return sum((t.astype(F32) for t in terms)).astype(BF16)  2.42 us
    pallas_call x1, Pallas kernels, finish_call(): pl.pallas_call(finish_kernel, in_specs=[IN_VMEM] * 3, out_specs=[IN_VMEM]...  1.8 us
  transfers between devices with their start and end apart: 14, of which 5 were waited for; matrix products, arithmetic and copies ran while one was open for 2% of the time, Pallas kernels for 26%

profile of v4, /device:TPU:0, one launch (start us, length us, event | category | flops | bytes accessed | tf_op | source)
XLA Modules:
  0.0 55.5 jit_solution(9568632461109820149)
XLA Ops:
  0.6 0.1 collective-permute-start.2
  0.7 0.5 collective-permute-start.4
  1.2 0.1 pad_add_fusion.pos
  1.3 7.9 %shard_map.110 = (bf16[3,14,4,16,128]{4,3,2,1,0:T(8,128)(2,1)S(1)}, bf16[3,14,4,16,128]{4,3,2,1,0:T(8,128)(2,1)S(1)}, bf16[2,4,128,512]{3,2,1,0:T(8,128)(2,1)S(1...) custom-call(s32[4]{0:T(128)S(1)} %pad_add_fusion.pos, ...), custom_call_target="tpu_custom_call" | custom-call | bytes 24576 | tf_op jit(solution)/shard_map/pallas_call | solution.py:218
  9.2 0.2 collective-permute-start.3
  9.4 1.6 %collective-permute-start = (bf16[2,4,128,512]{3,2,1,0:T(8,128)(2,1)S(1)}, bf16[2,4,128,512]{3,2,1,0:T(8,128)(2,1)S(1)}, u32[]{:S(2)}, u32[]{:S(2)}) collective-permute-start(bf16[2,4,128,512]{3,2,1,0:T(8,128)(2,1)S(1)} %get-tuple-element.26), channel_id=1, source_target_pairs={{0,1},{1,0},{2,3},{3,2},{4,5},{5,4},{6,7},{7,6},{8,9},{9,8},{10,11... | collective-permute-start | bytes 3145736 | tf_op jit(solution)/shard_map/ppermute | solution.py:41
  11.0 1.5 %collective-permute-start.10 = (bf16[2,4,128,512]{3,2,1,0:T(8,128)(2,1)S(1)}, bf16[2,4,128,512]{3,2,1,0:T(8,128)(2,1)S(1)}, u32[]{:S(2)}, u32[]{:S(2)}) collective-permute-start(bf16[2,4,128,512]{3,2,1,0:T(8,128)(2,1)S(1)} %get-tuple-element.39), channel_id=1, source_target_pairs={{0,4},{1,5},{2,6},{3,7},{4,0},{5,1},{6,2},{7,3},{8,12},{9,13},{10,... | collective-permute-start | bytes 3145736 | tf_op jit(solution)/shard_map/ppermute | solution.py:41
  12.6 0.0 collective-permute-done.2.h1
  12.6 0.0 collective-permute-done.4.d1_in
  12.6 4.7 %shard_map.111 = (bf16[3,14,16,512]{3,2,1,0:T(8,128)(2,1)S(1)}, bf16[3,14,16,512]{3,2,1,0:T(8,128)(2,1)S(1)}, bf16[3,14,16,512]{3,2,1,0:T(8,128)(2,1)S(1)}, bf16[3,14,16,512]{3,2,1,0:T(8,128)(2,1)S(1)}) custom-call(s32[4,14]{1,0:T(4,128)S(1)} %bitcast.31, s32[4,14]{1,0:T(4,128)S(1)} %bitcast.33, bf16[128,8192]{1,0:T(8,128)(2,1)S(1)} %get-tuple-element.27.h0, ...), custom_call_target="tpu_custom_call" | custom-call | flops 10000000000 | bytes 134217728 | tf_op jit(solution)/shard_map/pallas_call | solution.py:237
  17.3 2.0 %collective-permute-start.5 = (bf16[3,14,16,512]{3,2,1,0:T(8,128)(2,1)S(1)}, bf16[3,14,16,512]{3,2,1,0:T(8,128)(2,1)S(1)}, u32[]{:S(2)}, u32[]{:S(2)}) collective-permute-start(bf16[3,14,16,512]{3,2,1,0:T(8,128)(2,1)S(1)} %get-tuple-element.32), channel_id=1, source_target_pairs={{0,32},{1,33},{2,34},{3,35},{4,36},{5,37},{6,38},{7,39},{8,40},{9,... | collective-permute-start | bytes 2064392 | tf_op jit(solution)/shard_map/ppermute | solution.py:41
  19.3 4.9 %collective-permute-done = bf16[2,4,128,512]{3,2,1,0:T(8,128)(2,1)S(1)} collective-permute-done((bf16[2,4,128,512]{3,2,1,0:T(8,128)(2,1)S(1)}, bf16[2,4,128,512]{3,2,1,0:T(8,128)(2,1)S(1)}, u32[]{:S(2)}, u32[]{:S(2)}) %collective-permute-start) | collective-permute-done | bytes 1048608 | tf_op jit(solution)/shard_map/ppermute | solution.py:41
  24.2 0.1 fusion.2
  24.4 2.9 %collective-permute-start.1 = (bf16[4,128,512]{2,1,0:T(8,128)(2,1)S(1)}, bf16[4,128,512]{2,1,0:T(8,128)(2,1)S(1)}, u32[]{:S(2)}, u32[]{:S(2)}) collective-permute-start(bf16[4,128,512]{2,1,0:T(8,128)(2,1)S(1)} %fusion.2), channel_id=1, source_target_pairs={{0,3},{1,2},{2,1},{3,0},{4,7},{5,6},{6,5},{7,4},{8,11},{9,10},{10,... | collective-permute-start | bytes 1572872 | tf_op jit(solution)/shard_map/ppermute | solution.py:41
  27.3 0.1 fusion.3
  27.4 3.1 %collective-permute-start.11 = (bf16[4,128,512]{2,1,0:T(8,128)(2,1)S(1)}, bf16[4,128,512]{2,1,0:T(8,128)(2,1)S(1)}, u32[]{:S(2)}, u32[]{:S(2)}) collective-permute-start(bf16[4,128,512]{2,1,0:T(8,128)(2,1)S(1)} %fusion.3), channel_id=1, source_target_pairs={{0,12},{1,13},{2,14},{3,15},{4,8},{5,9},{6,10},{7,11},{8,4},{9,5},... | collective-permute-start | bytes 1572872 | tf_op jit(solution)/shard_map/ppermute | solution.py:41
  30.5 1.9 %collective-permute-start.8 = (bf16[3,14,16,512]{3,2,1,0:T(8,128)(2,1)S(1)}, bf16[3,14,16,512]{3,2,1,0:T(8,128)(2,1)S(1)}, u32[]{:S(2)}, u32[]{:S(2)}) collective-permute-start(bf16[3,14,16,512]{3,2,1,0:T(8,128)(2,1)S(1)} %get-tuple-element.35), channel_id=1, source_target_pairs={{0,32},{1,33},{2,34},{3,35},{4,36},{5,37},{6,38},{7,39},{8,40},{9,... | collective-permute-start | bytes 2064392 | tf_op jit(solution)/shard_map/ppermute | solution.py:41
  32.5 0.3 add_convert_fusion
  32.7 2.6 %collective-permute-start.9 = (bf16[3,14,16,512]{3,2,1,0:T(8,128)(2,1)S(1)}, bf16[3,14,16,512]{3,2,1,0:T(8,128)(2,1)S(1)}, u32[]{:S(2)}, u32[]{:S(2)}) collective-permute-start(bf16[3,14,16,512]{3,2,1,0:T(8,128)(2,1)S(1)} %add_convert_fusion), channel_id=1, source_target_pairs={{0,96},{1,97},{2,98},{3,99},{4,100},{5,101},{6,102},{7,103},{8,104... | collective-permute-start | bytes 2064392 | tf_op jit(solution)/shard_map/ppermute | solution.py:41
  35.3 0.2 fusion.1
  35.6 1.3 %collective-permute-start.6 = (bf16[2,128,512]{2,1,0:T(8,128)(2,1)S(1)}, bf16[2,128,512]{2,1,0:T(8,128)(2,1)S(1)}, u32[]{:S(2)}, u32[]{:S(2)}) collective-permute-start(bf16[2,128,512]{2,1,0:T(8,128)(2,1)S(1)} %slice.75), channel_id=1, source_target_pairs={{0,4},{1,5},{2,6},{3,7},{4,0},{5,1},{6,2},{7,3},{8,12},{9,13},{10,... | collective-permute-start | bytes 786440 | tf_op jit(solution)/shard_map/ppermute | solution.py:41
  36.8 1.4 %collective-permute-done.11 = bf16[4,128,512]{2,1,0:T(8,128)(2,1)S(1)} collective-permute-done((bf16[4,128,512]{2,1,0:T(8,128)(2,1)S(1)}, bf16[4,128,512]{2,1,0:T(8,128)(2,1)S(1)}, u32[]{:S(2)}, u32[]{:S(2)}) %collective-permute-start.11) | collective-permute-done | bytes 524320 | tf_op jit(solution)/shard_map/ppermute | solution.py:41
  38.2 0.2 fusion
  38.5 0.1 collective-permute-start.12
  38.6 3.4 %collective-permute-done.6 = bf16[2,128,512]{2,1,0:T(8,128)(2,1)S(1)} collective-permute-done((bf16[2,128,512]{2,1,0:T(8,128)(2,1)S(1)}, bf16[2,128,512]{2,1,0:T(8,128)(2,1)S(1)}, u32[]{:S(2)}, u32[]{:S(2)}) %collective-permute-start.6) | collective-permute-done | bytes 262176 | tf_op jit(solution)/shard_map/ppermute | solution.py:41
  42.0 2.7 %collective-permute-start.7 = (bf16[128,512]{1,0:T(8,128)(2,1)S(1)}, bf16[128,512]{1,0:T(8,128)(2,1)S(1)}, u32[]{:S(2)}, u32[]{:S(2)}) collective-permute-start(bf16[128,512]{1,0:T(8,128)(2,1)S(1)} %fusion.6), channel_id=1, source_target_pairs={{0,12},{1,13},{2,14},{3,15},{4,8},{5,9},{6,10},{7,11},{8,4},{9,5},... | collective-permute-start | bytes 393224 | tf_op jit(solution)/shard_map/ppermute | solution.py:41
  44.7 3.1 %collective-permute-done.8.r1 = bf16[3,14,16,512]{3,2,1,0:T(8,128)(2,1)S(1)} collective-permute-done((bf16[3,14,16,512]{3,2,1,0:T(8,128)(2,1)S(1)}, bf16[3,14,16,512]{3,2,1,0:T(8,128)(2,1)S(1)}, u32[]{:S(2)}, u32[]{:S(2)}) %collective-permute-start.8) | collective-permute-done | bytes 688160 | tf_op jit(solution)/shard_map/ppermute | solution.py:41
  47.9 0.8 %collective-permute-start.13 = (bf16[128,512]{1,0:T(8,128)(2,1)S(1)}, bf16[128,512]{1,0:T(8,128)(2,1)S(1)}, u32[]{:S(2)}, u32[]{:S(2)}) collective-permute-start(bf16[128,512]{1,0:T(8,128)(2,1)S(1)} %fusion.7), channel_id=1, source_target_pairs={{0,3},{1,2},{2,1},{3,0},{4,7},{5,6},{6,5},{7,4},{8,11},{9,10},{10,... | collective-permute-start | bytes 393224 | tf_op jit(solution)/shard_map/ppermute | solution.py:41
  48.7 1.8 %shard_map.112 = (f32[14,8192]{1,0:T(8,128)}, f32[14,8192]{1,0:T(8,128)}, f32[14,8192]{1,0:T(8,128)}) custom-call(bf16[3,14,16,512]{3,2,1,0:T(8,128)(2,1)S(1)} %get-tuple-element.34.own, bf16[3,14,16,512]{3,2,1,0:T(8,128)(2,1)S(1)} %collective-permute-done.8.r1, bf16[3,14,16,512]{3,2,1,0:T(8,128)(2,1)S(1)} %collective-permute-done.9.r2), custom_call_target="tpu_custom_call" | custom-call | flops 1000000000 | bytes 6291456 | tf_op jit(solution)/shard_map/pallas_call | solution.py:250
  50.5 3.6 %collective-permute-done.13 = bf16[128,512]{1,0:T(8,128)(2,1)S(1)} collective-permute-done((bf16[128,512]{1,0:T(8,128)(2,1)S(1)}, bf16[128,512]{1,0:T(8,128)(2,1)S(1)}, u32[]{:S(2)}, u32[]{:S(2)}) %collective-permute-start.13) | collective-permute-done | bytes 131104 | tf_op jit(solution)/shard_map/ppermute | solution.py:41
  54.1 0.7 %fusion.5 = bf16[128,512]{1,0:T(8,128)(2,1)} fusion(bf16[128,512]{1,0:T(8,128)(2,1)S(1)} %collective-permute-done.7, bf16[2,128,512]{2,1,0:T(8,128)(2,1)S(1)} %collective-permute-done.6, bf16[4,128,512]{2,1,0:T(8,128)(2,1)S(1)} %fusion.1), kind=kLoop, calls=%fused_computation.12 | loop fusion | flops 393216 | bytes 524288 | tf_op jit(solution)/shard_map/convert_element_type | solution.py:262
  54.8 0.7 %fusion.4 = bf16[128,512]{1,0:T(8,128)(2,1)} fusion(bf16[128,512]{1,0:T(8,128)(2,1)S(1)} %collective-permute-done.13, bf16[2,128,512]{2,1,0:T(8,128)(2,1)S(1)} %collective-permute-done.12, bf16[4,128,512]{2,1,0:T(8,128)(2,1)S(1)} %fusion), kind=kLoop, calls=%fused_computation.10 | loop fusion | flops 393216 | bytes 524288 | tf_op jit(solution)/shard_map/convert_element_type | solution.py:262
  (15 shorter events, 0.1 us)
Async XLA Ops:
  0.6 11.9 %collective-permute-start.2 = (bf16[128,8192]{1,0:T(8,128)(2,1)}, bf16[128,8192]{1,0:T(8,128)(2,1)S(1)}, u32[]{:S(2)}, u32[]{:S(2)}) collective-permute-start(bf16[128,8192]{1,0:T(8,128)(2,1)} %h_hbm.1), channel_id=1, source_target_pairs={{0,16},{1,17},{2,18},{3,19},{4,20},{5,21},{6,22},{7,23},{8,24},{9,... | collective-permute-start | bytes 6291464 | tf_op jit(solution)/shard_map/ppermute | solution.py:41
  0.7 11.9 %collective-permute-start.4 = (bf16[128,8192]{1,0:T(8,128)(2,1)}, bf16[128,8192]{1,0:T(8,128)(2,1)}, u32[]{:S(2)}, u32[]{:S(2)}) collective-permute-start(bf16[128,8192]{1,0:T(8,128)(2,1)} %d_hbm.1), channel_id=1, source_target_pairs={{0,16},{1,17},{2,18},{3,19},{4,20},{5,21},{6,22},{7,23},{8,24},{9,... | collective-permute-start | bytes 6291464 | tf_op jit(solution)/shard_map/ppermute | solution.py:41
  1.3 11.3 %copy-start = (s32[14,4]{0,1:T(4,128)S(1)}, s32[14,4]{0,1:T(4,128)}, u32[]{:S(2)}) copy-start(s32[14,4]{0,1:T(4,128)} %param.12) | copy-start | bytes 676
  1.3 11.3 %copy-start.1 = (s32[14,4]{0,1:T(4,128)S(1)}, s32[14,4]{0,1:T(4,128)}, u32[]{:S(2)}) copy-start(s32[14,4]{0,1:T(4,128)} %param.13) | copy-start | bytes 676
  9.2 3.3 %collective-permute-start.3 = (bf16[3,14,4,16,128]{4,3,2,1,0:T(8,128)(2,1)S(1)}, bf16[3,14,4,16,128]{4,3,2,1,0:T(8,128)(2,1)S(1)}, u32[]{:S(2)}, u32[]{:S(2)}) collective-permute-start(bf16[3,14,4,16,128]{4,3,2,1,0:T(8,128)(2,1)S(1)} %get-tuple-element.30), channel_id=1, source_target_pairs={{0,16},{1,17},{2,18},{3,19},{4,20},{5,21},{6,22},{7,23},{8,24},{9,... | collective-permute-start | bytes 2064392 | tf_op jit(solution)/shard_map/ppermute | solution.py:41
  9.4 14.8 %collective-permute-start = (bf16[2,4,128,512]{3,2,1,0:T(8,128)(2,1)S(1)}, bf16[2,4,128,512]{3,2,1,0:T(8,128)(2,1)S(1)}, u32[]{:S(2)}, u32[]{:S(2)}) collective-permute-start(bf16[2,4,128,512]{3,2,1,0:T(8,128)(2,1)S(1)} %get-tuple-element.26), channel_id=1, source_target_pairs={{0,1},{1,0},{2,3},{3,2},{4,5},{5,4},{6,7},{7,6},{8,9},{9,8},{10,11... | collective-permute-start | bytes 3145736 | tf_op jit(solution)/shard_map/ppermute | solution.py:41
  11.0 16.3 %collective-permute-start.10 = (bf16[2,4,128,512]{3,2,1,0:T(8,128)(2,1)S(1)}, bf16[2,4,128,512]{3,2,1,0:T(8,128)(2,1)S(1)}, u32[]{:S(2)}, u32[]{:S(2)}) collective-permute-start(bf16[2,4,128,512]{3,2,1,0:T(8,128)(2,1)S(1)} %get-tuple-element.39), channel_id=1, source_target_pairs={{0,4},{1,5},{2,6},{3,7},{4,0},{5,1},{6,2},{7,3},{8,12},{9,13},{10,... | collective-permute-start | bytes 3145736 | tf_op jit(solution)/shard_map/ppermute | solution.py:41
  17.3 15.1 %collective-permute-start.5 = (bf16[3,14,16,512]{3,2,1,0:T(8,128)(2,1)S(1)}, bf16[3,14,16,512]{3,2,1,0:T(8,128)(2,1)S(1)}, u32[]{:S(2)}, u32[]{:S(2)}) collective-permute-start(bf16[3,14,16,512]{3,2,1,0:T(8,128)(2,1)S(1)} %get-tuple-element.32), channel_id=1, source_target_pairs={{0,32},{1,33},{2,34},{3,35},{4,36},{5,37},{6,38},{7,39},{8,40},{9,... | collective-permute-start | bytes 2064392 | tf_op jit(solution)/shard_map/ppermute | solution.py:41
  24.4 11.0 %collective-permute-start.1 = (bf16[4,128,512]{2,1,0:T(8,128)(2,1)S(1)}, bf16[4,128,512]{2,1,0:T(8,128)(2,1)S(1)}, u32[]{:S(2)}, u32[]{:S(2)}) collective-permute-start(bf16[4,128,512]{2,1,0:T(8,128)(2,1)S(1)} %fusion.2), channel_id=1, source_target_pairs={{0,3},{1,2},{2,1},{3,0},{4,7},{5,6},{6,5},{7,4},{8,11},{9,10},{10,... | collective-permute-start | bytes 1572872 | tf_op jit(solution)/shard_map/ppermute | solution.py:41
  27.4 10.8 %collective-permute-start.11 = (bf16[4,128,512]{2,1,0:T(8,128)(2,1)S(1)}, bf16[4,128,512]{2,1,0:T(8,128)(2,1)S(1)}, u32[]{:S(2)}, u32[]{:S(2)}) collective-permute-start(bf16[4,128,512]{2,1,0:T(8,128)(2,1)S(1)} %fusion.3), channel_id=1, source_target_pairs={{0,12},{1,13},{2,14},{3,15},{4,8},{5,9},{6,10},{7,11},{8,4},{9,5},... | collective-permute-start | bytes 1572872 | tf_op jit(solution)/shard_map/ppermute | solution.py:41
  30.5 17.3 %collective-permute-start.8 = (bf16[3,14,16,512]{3,2,1,0:T(8,128)(2,1)S(1)}, bf16[3,14,16,512]{3,2,1,0:T(8,128)(2,1)S(1)}, u32[]{:S(2)}, u32[]{:S(2)}) collective-permute-start(bf16[3,14,16,512]{3,2,1,0:T(8,128)(2,1)S(1)} %get-tuple-element.35), channel_id=1, source_target_pairs={{0,32},{1,33},{2,34},{3,35},{4,36},{5,37},{6,38},{7,39},{8,40},{9,... | collective-permute-start | bytes 2064392 | tf_op jit(solution)/shard_map/ppermute | solution.py:41
  32.7 16.0 %collective-permute-start.9 = (bf16[3,14,16,512]{3,2,1,0:T(8,128)(2,1)S(1)}, bf16[3,14,16,512]{3,2,1,0:T(8,128)(2,1)S(1)}, u32[]{:S(2)}, u32[]{:S(2)}) collective-permute-start(bf16[3,14,16,512]{3,2,1,0:T(8,128)(2,1)S(1)} %add_convert_fusion), channel_id=1, source_target_pairs={{0,96},{1,97},{2,98},{3,99},{4,100},{5,101},{6,102},{7,103},{8,104... | collective-permute-start | bytes 2064392 | tf_op jit(solution)/shard_map/ppermute | solution.py:41
  35.6 6.5 %collective-permute-start.6 = (bf16[2,128,512]{2,1,0:T(8,128)(2,1)S(1)}, bf16[2,128,512]{2,1,0:T(8,128)(2,1)S(1)}, u32[]{:S(2)}, u32[]{:S(2)}) collective-permute-start(bf16[2,128,512]{2,1,0:T(8,128)(2,1)S(1)} %slice.75), channel_id=1, source_target_pairs={{0,4},{1,5},{2,6},{3,7},{4,0},{5,1},{6,2},{7,3},{8,12},{9,13},{10,... | collective-permute-start | bytes 786440 | tf_op jit(solution)/shard_map/ppermute | solution.py:41
  38.5 9.4 %collective-permute-start.12 = (bf16[2,128,512]{2,1,0:T(8,128)(2,1)S(1)}, bf16[2,128,512]{2,1,0:T(8,128)(2,1)S(1)}, u32[]{:S(2)}, u32[]{:S(2)}) collective-permute-start(bf16[2,128,512]{2,1,0:T(8,128)(2,1)S(1)} %slice.82), channel_id=1, source_target_pairs={{0,1},{1,0},{2,3},{3,2},{4,5},{5,4},{6,7},{7,6},{8,9},{9,8},{10,11... | collective-permute-start | bytes 786440 | tf_op jit(solution)/shard_map/ppermute | solution.py:41
  42.0 8.4 %collective-permute-start.7 = (bf16[128,512]{1,0:T(8,128)(2,1)S(1)}, bf16[128,512]{1,0:T(8,128)(2,1)S(1)}, u32[]{:S(2)}, u32[]{:S(2)}) collective-permute-start(bf16[128,512]{1,0:T(8,128)(2,1)S(1)} %fusion.6), channel_id=1, source_target_pairs={{0,12},{1,13},{2,14},{3,15},{4,8},{5,9},{6,10},{7,11},{8,4},{9,5},... | collective-permute-start | bytes 393224 | tf_op jit(solution)/shard_map/ppermute | solution.py:41
  47.9 6.3 %collective-permute-start.13 = (bf16[128,512]{1,0:T(8,128)(2,1)S(1)}, bf16[128,512]{1,0:T(8,128)(2,1)S(1)}, u32[]{:S(2)}, u32[]{:S(2)}) collective-permute-start(bf16[128,512]{1,0:T(8,128)(2,1)S(1)} %fusion.7), channel_id=1, source_target_pairs={{0,3},{1,2},{2,1},{3,0},{4,7},{5,6},{6,5},{7,4},{8,11},{9,10},{10,... | collective-permute-start | bytes 393224 | tf_op jit(solution)/shard_map/ppermute | solution.py:41

commit v5 on v4

--- a/solution.py
+++ b/solution.py
@@ -58,19 +58,18 @@
     )
 
 
-def emit_chunks(acc, outer, inner, transposed, sent, stay):
-    for p in range(4):
-        dst = sent if p < 2 else stay
+def emit_chunks(acc, outer, inner, transposed, outs):
+    for p, dst in enumerate(outs):
         for q in range(4):
             y, x = (inner[q], outer[p]) if transposed else (outer[p], inner[q])
             base = (y * 4 + x) * 4
             for j in range(4):
-                dst[p % 2, q, :, j * BLK : (j + 1) * BLK] = acc[base + j].astype(BF16)
+                dst[q, :, j * BLK : (j + 1) * BLK] = acc[base + j].astype(BF16)
 
 
 def main_kernel(
     pos, lin_hbm, lout_hbm, h_hbm, d_hbm, wg_hbm, wu_hbm, wd_hbm,
-    keep, give, p_sent, p_stay, q_sent, q_stay, h, d,
+    keep, give, p0, p1, p2, p3, q0, q1, q2, q3, h, d,
     wg, wu, wd, acc_p, acc_q, hid, dgu, turned, lin, lout, sem, w_sem,
 ):
     small = [
@@ -143,8 +142,8 @@
         units(s)
     features(ROWS // UNROLL - 1)
     xs, ys = ring_order(pos[3], core), ring_order(pos[2], core)
-    emit_chunks(acc_p, xs, ys, True, p_sent, p_stay)
-    emit_chunks(acc_q, ys, xs, False, q_sent, q_stay)
+    emit_chunks(acc_p, xs, ys, True, (p0, p1, p2, p3))
+    emit_chunks(acc_q, ys, xs, False, (q0, q1, q2, q3))
 
 
 def pair_rows(a, b):
@@ -211,15 +210,15 @@
 
 def main_call(pos, *arrays):
     act = V((3, ROWS, 4, 16, TOK), BF16)
-    chunks = V((2, 4, TOK, W), BF16)
+    chunks = V((4, TOK, W), BF16)
     weight = V((ROWS * BLK, W), BF16)
     total = V((NBLK, TOK, BLK), F32)
     layout = pltpu.SMEM((KB, ROWS), jnp.int32)
     return pl.pallas_call(
         main_kernel,
         in_specs=[IN_SMEM] + [ANYWHERE] * 7,
-        out_specs=[IN_VMEM] * 8,
-        out_shape=[act, act] + [chunks] * 4 + [V((TOK, D), BF16)] * 2,
+        out_specs=[IN_VMEM] * 12,
+        out_shape=[act, act] + [chunks] * 8 + [V((TOK, D), BF16)] * 2,
         scratch_shapes=[
             weight, weight, weight, total, total,
             V((ROWS, TOK, BLK), BF16), V((ROWS, TOK, 2 * BLK), BF16), V((ROWS, 3, 8, 16, TOK), BF16),
@@ -272,23 +271,24 @@
     pos = jnp.stack([dp // 2, dp % 2, t // 4, t % 4]).astype(jnp.int32)
     h_other = send(h_in, "core")
     d_other = send(dout, "core")
-    keep, give, p_sent, p_own, q_sent, q_own, h_own, d_own = main_call(
-        pos, in_layout, out_layout, h_in, dout, w_gate, w_up, w_down
+    keep, give, p_keeps, p_passes, p_own, p_next, q_keeps, q_passes, q_own, q_next, h_own, d_own = (
+        main_call(pos, in_layout, out_layout, h_in, dout, w_gate, w_up, w_down)
     )
     taken = send(give, "core")
-    p1, q1 = send(p_sent, "x", 0), send(q_sent, "y", 0)
+    p1, q1 = send(p_passes, "x", 0), send(q_passes, "y", 0)
+    p1k, q1k = send(p_keeps, "x", 0), send(q_keeps, "y", 0)
     g_keeps, g_passes, g_own, g_next = grads_call(
         in_layout, out_layout, h_own, h_other, d_own, keep, taken, d_other
     )
     g1 = send(g_passes, "z", 0)
     g1k = send(g_keeps, "z", 0)
-    p2 = send(add(p_own[1], p1[1]), "x", 1)
-    q2 = send(add(q_own[1], q1[1]), "y", 1)
+    p2 = send(add(p_next, p1), "x", 1)
+    q2 = send(add(q_next, q1), "y", 1)
     g2_in = add(g_next, g1)
     g2 = send(g2_in, "z", 1)
-    p_mid = add(p_own[0], p1[0], after(p2, g2_in))
+    p_mid = add(p_own, p1k, after(p2, g2_in))
     p3 = send(p_mid[0:2], "y", 0)
-    q_mid = add(q_own[0], q1[0], after(q2, p_mid))
+    q_mid = add(q_own, q1k, after(q2, p_mid))
     q3 = send(q_mid[0:2], "x", 0)
     p4 = send(add(p_mid[3], p3[1]), "y", 1)
     q4 = send(add(q_mid[3], after(q3, g1k)[1]), "x", 1)

time: 56.6 us -> 55.3 us (0.977); the launches traced: 55.5 us -> 54.9 us
  starting transfers between devices: 21.3 us -> 18.8 us
  waiting for transfers between devices: 16.5 us -> 18.4 us
    ppermute x14 -> x16, starting transfers between devices: 21.3 us -> 18.8 us  [send(): return lax.ppermute(a, AXES, pairs(axis, step))]
    ppermute x14 -> x16, waiting for transfers between devices: 16.5 us -> 18.4 us  [send(): return lax.ppermute(a, AXES, pairs(axis, step))]
  transfers between devices with their start and end apart: 14 -> 16, of which waited for: 5 -> 5; matrix products, arithmetic and copies ran while one was open for 2% -> 2% of each run, Pallas kernels for 26% -> 26%
where the time goes in v5:
time: 55.3 us; the launch traced here: 54.9 us
  starting transfers between devices  18.8 us (34%)
  waiting for transfers between devices  18.4 us (33%)
  Pallas kernels  14.4 us (26%)
  other arithmetic  2.52 us (5%)
  between operations  0.75 us (1%)
    ppermute x16, starting transfers between devices, send(): return lax.ppermute(a, AXES, pairs(axis, step))  18.8 us
    ppermute x16, waiting for transfers between devices, send(): return lax.ppermute(a, AXES, pairs(axis, step))  18.4 us
    pallas_call x1, Pallas kernels, main_call(): pl.pallas_call(main_kernel, in_specs=[IN_SMEM] + [ANYWHERE] * 7, out_spec...  7.92 us
    pallas_call x1, Pallas kernels, grads_call(): pl.pallas_call(grads_kernel, in_specs=[IN_SMEM] * 2 + [IN_VMEM] * 5 + [AN...  4.69 us
    convert_element_type x9, other arithmetic, add(): return sum((t.astype(F32) for t in terms)).astype(BF16)  2.44 us
    pallas_call x1, Pallas kernels, finish_call(): pl.pallas_call(finish_kernel, in_specs=[IN_VMEM] * 3, out_specs=[IN_VMEM]...  1.8 us
  transfers between devices with their start and end apart: 16, of which 5 were waited for; matrix products, arithmetic and copies ran while one was open for 2% of the time, Pallas kernels for 26%

profile of v5, /device:TPU:0, one launch (start us, length us, event | category | flops | bytes accessed | tf_op | source)
XLA Modules:
  0.0 54.9 jit_solution(1552603537273776157)
XLA Ops:
  0.6 0.1 collective-permute-start.3
  0.7 0.5 collective-permute-start.5
  1.2 0.1 pad_add_fusion.pos
  1.3 7.9 %shard_map.110 = (bf16[3,14,4,16,128]{4,3,2,1,0:T(8,128)(2,1)S(1)}, bf16[3,14,4,16,128]{4,3,2,1,0:T(8,128)(2,1)S(1)}, bf16[4,128,512]{2,1,0:T(8,128)(2,1)S(1)}, ...) custom-call(s32[4]{0:T(128)S(1)} %pad_add_fusion.pos, ...), custom_call_target="tpu_custom_call" | custom-call | bytes 24576 | tf_op jit(solution)/shard_map/pallas_call | solution.py:217
  9.2 0.2 collective-permute-start.4
  9.4 1.6 %collective-permute-start.1 = (bf16[4,128,512]{2,1,0:T(8,128)(2,1)S(1)}, bf16[4,128,512]{2,1,0:T(8,128)(2,1)S(1)}, u32[]{:S(2)}, u32[]{:S(2)}) collective-permute-start(bf16[4,128,512]{2,1,0:T(8,128)(2,1)S(1)} %get-tuple-element.32), channel_id=1, source_target_pairs={{0,1},{1,0},{2,3},{3,2},{4,5},{5,4},{6,7},{7,6},{8,9},{9,8},{10,11... | collective-permute-start | bytes 1572872 | tf_op jit(solution)/shard_map/ppermute | solution.py:41
  11.0 1.6 %collective-permute-start.12 = (bf16[4,128,512]{2,1,0:T(8,128)(2,1)S(1)}, bf16[4,128,512]{2,1,0:T(8,128)(2,1)S(1)}, u32[]{:S(2)}, u32[]{:S(2)}) collective-permute-start(bf16[4,128,512]{2,1,0:T(8,128)(2,1)S(1)} %get-tuple-element.47), channel_id=1, source_target_pairs={{0,4},{1,5},{2,6},{3,7},{4,0},{5,1},{6,2},{7,3},{8,12},{9,13},{10,... | collective-permute-start | bytes 1572872 | tf_op jit(solution)/shard_map/ppermute | solution.py:41
  12.6 4.7 %shard_map.111 = (bf16[3,14,16,512]{3,2,1,0:T(8,128)(2,1)S(1)}, bf16[3,14,16,512]{3,2,1,0:T(8,128)(2,1)S(1)}, bf16[3,14,16,512]{3,2,1,0:T(8,128)(2,1)S(1)}, bf16[3,14,16,512]{3,2,1,0:T(8,128)(2,1)S(1)}) custom-call(s32[4,14]{1,0:T(4,128)S(1)} %bitcast.19, s32[4,14]{1,0:T(4,128)S(1)} %bitcast.21, bf16[128,8192]{1,0:T(8,128)(2,1)S(1)} %get-tuple-element.33.h0, ...), custom_call_target="tpu_custom_call" | custom-call | flops 10000000000 | bytes 134217728 | tf_op jit(solution)/shard_map/pallas_call | solution.py:236
  17.3 2.0 %collective-permute-start.6 = (bf16[3,14,16,512]{3,2,1,0:T(8,128)(2,1)S(1)}, bf16[3,14,16,512]{3,2,1,0:T(8,128)(2,1)S(1)}, u32[]{:S(2)}, u32[]{:S(2)}) collective-permute-start(bf16[3,14,16,512]{3,2,1,0:T(8,128)(2,1)S(1)} %get-tuple-element.38), channel_id=1, source_target_pairs={{0,32},{1,33},{2,34},{3,35},{4,36},{5,37},{6,38},{7,39},{8,40},{9,... | collective-permute-start | bytes 2064392 | tf_op jit(solution)/shard_map/ppermute | solution.py:41
  19.3 0.6 %collective-permute-start = (bf16[4,128,512]{2,1,0:T(8,128)(2,1)S(1)}, bf16[4,128,512]{2,1,0:T(8,128)(2,1)S(1)}, u32[]{:S(2)}, u32[]{:S(2)}) collective-permute-start(bf16[4,128,512]{2,1,0:T(8,128)(2,1)S(1)} %get-tuple-element.30), channel_id=1, source_target_pairs={{0,1},{1,0},{2,3},{3,2},{4,5},{5,4},{6,7},{7,6},{8,9},{9,8},{10,11... | collective-permute-start | bytes 1572872 | tf_op jit(solution)/shard_map/ppermute | solution.py:41
  19.9 1.5 %collective-permute-start.11 = (bf16[4,128,512]{2,1,0:T(8,128)(2,1)S(1)}, bf16[4,128,512]{2,1,0:T(8,128)(2,1)S(1)}, u32[]{:S(2)}, u32[]{:S(2)}) collective-permute-start(bf16[4,128,512]{2,1,0:T(8,128)(2,1)S(1)} %get-tuple-element.45), channel_id=1, source_target_pairs={{0,4},{1,5},{2,6},{3,7},{4,0},{5,1},{6,2},{7,3},{8,12},{9,13},{10,... | collective-permute-start | bytes 1572872 | tf_op jit(solution)/shard_map/ppermute | solution.py:41
  21.3 0.1 add_convert_fusion.4
  21.5 2.2 %collective-permute-start.2 = (bf16[4,128,512]{2,1,0:T(8,128)(2,1)S(1)}, bf16[4,128,512]{2,1,0:T(8,128)(2,1)S(1)}, u32[]{:S(2)}, u32[]{:S(2)}) collective-permute-start(bf16[4,128,512]{2,1,0:T(8,128)(2,1)S(1)} %add_convert_fusion.4), channel_id=1, source_target_pairs={{0,3},{1,2},{2,1},{3,0},{4,7},{5,6},{6,5},{7,4},{8,11},{9,10},{10,... | collective-permute-start | bytes 1572872 | tf_op jit(solution)/shard_map/ppermute | solution.py:41
  23.7 0.1 add_convert_fusion.2
  23.8 2.7 %collective-permute-start.13 = (bf16[4,128,512]{2,1,0:T(8,128)(2,1)S(1)}, bf16[4,128,512]{2,1,0:T(8,128)(2,1)S(1)}, u32[]{:S(2)}, u32[]{:S(2)}) collective-permute-start(bf16[4,128,512]{2,1,0:T(8,128)(2,1)S(1)} %add_convert_fusion.2), channel_id=1, source_target_pairs={{0,12},{1,13},{2,14},{3,15},{4,8},{5,9},{6,10},{7,11},{8,4},{9,5},... | collective-permute-start | bytes 1572872 | tf_op jit(solution)/shard_map/ppermute | solution.py:41
  26.5 1.8 %collective-permute-done.6 = bf16[3,14,16,512]{3,2,1,0:T(8,128)(2,1)S(1)} collective-permute-done((bf16[3,14,16,512]{3,2,1,0:T(8,128)(2,1)S(1)}, bf16[3,14,16,512]{3,2,1,0:T(8,128)(2,1)S(1)}, u32[]{:S(2)}, u32[]{:S(2)}) %collective-permute-start.6) | collective-permute-done | bytes 688160 | tf_op jit(solution)/shard_map/ppermute | solution.py:41
  28.3 1.9 %collective-permute-start.9 = (bf16[3,14,16,512]{3,2,1,0:T(8,128)(2,1)S(1)}, bf16[3,14,16,512]{3,2,1,0:T(8,128)(2,1)S(1)}, u32[]{:S(2)}, u32[]{:S(2)}) collective-permute-start(bf16[3,14,16,512]{3,2,1,0:T(8,128)(2,1)S(1)} %get-tuple-element.41), channel_id=1, source_target_pairs={{0,32},{1,33},{2,34},{3,35},{4,36},{5,37},{6,38},{7,39},{8,40},{9,... | collective-permute-start | bytes 2064392 | tf_op jit(solution)/shard_map/ppermute | solution.py:41
  30.2 0.3 add_convert_fusion
  30.5 5.9 %collective-permute-done.2 = bf16[4,128,512]{2,1,0:T(8,128)(2,1)S(1)} collective-permute-done((bf16[4,128,512]{2,1,0:T(8,128)(2,1)S(1)}, bf16[4,128,512]{2,1,0:T(8,128)(2,1)S(1)}, u32[]{:S(2)}, u32[]{:S(2)}) %collective-permute-start.2) | collective-permute-done | bytes 524320 | tf_op jit(solution)/shard_map/ppermute | solution.py:41
  36.4 0.2 add_convert_fusion.3
  36.6 2.3 %collective-permute-done.13 = bf16[4,128,512]{2,1,0:T(8,128)(2,1)S(1)} collective-permute-done((bf16[4,128,512]{2,1,0:T(8,128)(2,1)S(1)}, bf16[4,128,512]{2,1,0:T(8,128)(2,1)S(1)}, u32[]{:S(2)}, u32[]{:S(2)}) %collective-permute-start.13) | collective-permute-done | bytes 524320 | tf_op jit(solution)/shard_map/ppermute | solution.py:41
  38.9 0.2 add_convert_fusion.1
  39.2 0.4 collective-permute-start.14
  39.6 0.4 collective-permute-start.10
  40.0 0.1 collective-permute-start.7
  40.1 5.6 %collective-permute-done.14 = bf16[2,128,512]{2,1,0:T(8,128)(2,1)S(1)} collective-permute-done((bf16[2,128,512]{2,1,0:T(8,128)(2,1)S(1)}, bf16[2,128,512]{2,1,0:T(8,128)(2,1)S(1)}, u32[]{:S(2)}, u32[]{:S(2)}) %collective-permute-start.14) | collective-permute-done | bytes 262176 | tf_op jit(solution)/shard_map/ppermute | solution.py:41
  45.7 1.6 %collective-permute-start.15 = (bf16[128,512]{1,0:T(8,128)(2,1)S(1)}, bf16[128,512]{1,0:T(8,128)(2,1)S(1)}, u32[]{:S(2)}, u32[]{:S(2)}) collective-permute-start(bf16[128,512]{1,0:T(8,128)(2,1)S(1)} %fusion.3), channel_id=1, source_target_pairs={{0,3},{1,2},{2,1},{3,0},{4,7},{5,6},{6,5},{7,4},{8,11},{9,10},{10,... | collective-permute-start | bytes 393224 | tf_op jit(solution)/shard_map/ppermute | solution.py:41
  47.3 1.7 %collective-permute-start.8 = (bf16[128,512]{1,0:T(8,128)(2,1)S(1)}, bf16[128,512]{1,0:T(8,128)(2,1)S(1)}, u32[]{:S(2)}, u32[]{:S(2)}) collective-permute-start(bf16[128,512]{1,0:T(8,128)(2,1)S(1)} %fusion.2), channel_id=1, source_target_pairs={{0,12},{1,13},{2,14},{3,15},{4,8},{5,9},{6,10},{7,11},{8,4},{9,5},... | collective-permute-start | bytes 393224 | tf_op jit(solution)/shard_map/ppermute | solution.py:41
  48.9 2.8 %collective-permute-done.10.r2 = bf16[3,14,16,512]{3,2,1,0:T(8,128)(2,1)S(1)} collective-permute-done((bf16[3,14,16,512]{3,2,1,0:T(8,128)(2,1)S(1)}, bf16[3,14,16,512]{3,2,1,0:T(8,128)(2,1)S(1)}, u32[]{:S(2)}, u32[]{:S(2)}) %collective-permute-start.10) | collective-permute-done | bytes 688160 | tf_op jit(solution)/shard_map/ppermute | solution.py:41
  51.7 1.8 %shard_map.112 = (f32[14,8192]{1,0:T(8,128)}, f32[14,8192]{1,0:T(8,128)}, f32[14,8192]{1,0:T(8,128)}) custom-call(bf16[3,14,16,512]{3,2,1,0:T(8,128)(2,1)S(1)} %get-tuple-element.40.own, bf16[3,14,16,512]{3,2,1,0:T(8,128)(2,1)S(1)} %collective-permute-done.9.r1, bf16[3,14,16,512]{3,2,1,0:T(8,128)(2,1)S(1)} %collective-permute-done.10.r2), custom_call_target="tpu_custom_call" | custom-call | flops 1000000000 | bytes 6291456 | tf_op jit(solution)/shard_map/pallas_call | solution.py:249
  53.5 0.7 %fusion = bf16[128,512]{1,0:T(8,128)(2,1)} fusion(bf16[128,512]{1,0:T(8,128)(2,1)S(1)} %collective-permute-done.15, bf16[2,128,512]{2,1,0:T(8,128)(2,1)S(1)} %collective-permute-done.14, bf16[4,128,512]{2,1,0:T(8,128)(2,1)S(1)} %add_convert_fusion.1), kind=kLoop, calls=%fused_computation.6 | loop fusion | flops 393216 | bytes 524288 | tf_op jit(solution)/shard_map/convert_element_type | solution.py:261
  54.2 0.7 %fusion.1 = bf16[128,512]{1,0:T(8,128)(2,1)} fusion(bf16[128,512]{1,0:T(8,128)(2,1)S(1)} %collective-permute-done.8, bf16[2,128,512]{2,1,0:T(8,128)(2,1)S(1)} %collective-permute-done.7, bf16[4,128,512]{2,1,0:T(8,128)(2,1)S(1)} %add_convert_fusion.3), kind=kLoop, calls=%fused_computation.8 | loop fusion | flops 393216 | bytes 524288 | tf_op jit(solution)/shard_map/convert_element_type | solution.py:261
  (19 shorter events, 0.1 us)
Async XLA Ops:
  0.6 11.9 %collective-permute-start.3 = (bf16[128,8192]{1,0:T(8,128)(2,1)}, bf16[128,8192]{1,0:T(8,128)(2,1)S(1)}, u32[]{:S(2)}, u32[]{:S(2)}) collective-permute-start(bf16[128,8192]{1,0:T(8,128)(2,1)} %h_hbm.1), channel_id=1, source_target_pairs={{0,16},{1,17},{2,18},{3,19},{4,20},{5,21},{6,22},{7,23},{8,24},{9,... | collective-permute-start | bytes 6291464 | tf_op jit(solution)/shard_map/ppermute | solution.py:41
  0.7 11.8 %collective-permute-start.5 = (bf16[128,8192]{1,0:T(8,128)(2,1)}, bf16[128,8192]{1,0:T(8,128)(2,1)}, u32[]{:S(2)}, u32[]{:S(2)}) collective-permute-start(bf16[128,8192]{1,0:T(8,128)(2,1)} %d_hbm.1), channel_id=1, source_target_pairs={{0,16},{1,17},{2,18},{3,19},{4,20},{5,21},{6,22},{7,23},{8,24},{9,... | collective-permute-start | bytes 6291464 | tf_op jit(solution)/shard_map/ppermute | solution.py:41
  1.3 11.3 %copy-start = (s32[14,4]{0,1:T(4,128)S(1)}, s32[14,4]{0,1:T(4,128)}, u32[]{:S(2)}) copy-start(s32[14,4]{0,1:T(4,128)} %param.12) | copy-start | bytes 676
  1.3 11.3 %copy-start.1 = (s32[14,4]{0,1:T(4,128)S(1)}, s32[14,4]{0,1:T(4,128)}, u32[]{:S(2)}) copy-start(s32[14,4]{0,1:T(4,128)} %param.13) | copy-start | bytes 676
  9.2 3.3 %collective-permute-start.4 = (bf16[3,14,4,16,128]{4,3,2,1,0:T(8,128)(2,1)S(1)}, bf16[3,14,4,16,128]{4,3,2,1,0:T(8,128)(2,1)S(1)}, u32[]{:S(2)}, u32[]{:S(2)}) collective-permute-start(bf16[3,14,4,16,128]{4,3,2,1,0:T(8,128)(2,1)S(1)} %get-tuple-element.36), channel_id=1, source_target_pairs={{0,16},{1,17},{2,18},{3,19},{4,20},{5,21},{6,22},{7,23},{8,24},{9,... | collective-permute-start | bytes 2064392 | tf_op jit(solution)/shard_map/ppermute | solution.py:41
  9.4 11.9 %collective-permute-start.1 = (bf16[4,128,512]{2,1,0:T(8,128)(2,1)S(1)}, bf16[4,128,512]{2,1,0:T(8,128)(2,1)S(1)}, u32[]{:S(2)}, u32[]{:S(2)}) collective-permute-start(bf16[4,128,512]{2,1,0:T(8,128)(2,1)S(1)} %get-tuple-element.32), channel_id=1, source_target_pairs={{0,1},{1,0},{2,3},{3,2},{4,5},{5,4},{6,7},{7,6},{8,9},{9,8},{10,11... | collective-permute-start | bytes 1572872 | tf_op jit(solution)/shard_map/ppermute | solution.py:41
  11.0 12.7 %collective-permute-start.12 = (bf16[4,128,512]{2,1,0:T(8,128)(2,1)S(1)}, bf16[4,128,512]{2,1,0:T(8,128)(2,1)S(1)}, u32[]{:S(2)}, u32[]{:S(2)}) collective-permute-start(bf16[4,128,512]{2,1,0:T(8,128)(2,1)S(1)} %get-tuple-element.47), channel_id=1, source_target_pairs={{0,4},{1,5},{2,6},{3,7},{4,0},{5,1},{6,2},{7,3},{8,12},{9,13},{10,... | collective-permute-start | bytes 1572872 | tf_op jit(solution)/shard_map/ppermute | solution.py:41
  17.3 11.0 %collective-permute-start.6 = (bf16[3,14,16,512]{3,2,1,0:T(8,128)(2,1)S(1)}, bf16[3,14,16,512]{3,2,1,0:T(8,128)(2,1)S(1)}, u32[]{:S(2)}, u32[]{:S(2)}) collective-permute-start(bf16[3,14,16,512]{3,2,1,0:T(8,128)(2,1)S(1)} %get-tuple-element.38), channel_id=1, source_target_pairs={{0,32},{1,33},{2,34},{3,35},{4,36},{5,37},{6,38},{7,39},{8,40},{9,... | collective-permute-start | bytes 2064392 | tf_op jit(solution)/shard_map/ppermute | solution.py:41
  19.3 17.1 %collective-permute-start = (bf16[4,128,512]{2,1,0:T(8,128)(2,1)S(1)}, bf16[4,128,512]{2,1,0:T(8,128)(2,1)S(1)}, u32[]{:S(2)}, u32[]{:S(2)}) collective-permute-start(bf16[4,128,512]{2,1,0:T(8,128)(2,1)S(1)} %get-tuple-element.30), channel_id=1, source_target_pairs={{0,1},{1,0},{2,3},{3,2},{4,5},{5,4},{6,7},{7,6},{8,9},{9,8},{10,11... | collective-permute-start | bytes 1572872 | tf_op jit(solution)/shard_map/ppermute | solution.py:41
  19.9 19.1 %collective-permute-start.11 = (bf16[4,128,512]{2,1,0:T(8,128)(2,1)S(1)}, bf16[4,128,512]{2,1,0:T(8,128)(2,1)S(1)}, u32[]{:S(2)}, u32[]{:S(2)}) collective-permute-start(bf16[4,128,512]{2,1,0:T(8,128)(2,1)S(1)} %get-tuple-element.45), channel_id=1, source_target_pairs={{0,4},{1,5},{2,6},{3,7},{4,0},{5,1},{6,2},{7,3},{8,12},{9,13},{10,... | collective-permute-start | bytes 1572872 | tf_op jit(solution)/shard_map/ppermute | solution.py:41
  21.5 14.9 %collective-permute-start.2 = (bf16[4,128,512]{2,1,0:T(8,128)(2,1)S(1)}, bf16[4,128,512]{2,1,0:T(8,128)(2,1)S(1)}, u32[]{:S(2)}, u32[]{:S(2)}) collective-permute-start(bf16[4,128,512]{2,1,0:T(8,128)(2,1)S(1)} %add_convert_fusion.4), channel_id=1, source_target_pairs={{0,3},{1,2},{2,1},{3,0},{4,7},{5,6},{6,5},{7,4},{8,11},{9,10},{10,... | collective-permute-start | bytes 1572872 | tf_op jit(solution)/shard_map/ppermute | solution.py:41
  23.8 15.1 %collective-permute-start.13 = (bf16[4,128,512]{2,1,0:T(8,128)(2,1)S(1)}, bf16[4,128,512]{2,1,0:T(8,128)(2,1)S(1)}, u32[]{:S(2)}, u32[]{:S(2)}) collective-permute-start(bf16[4,128,512]{2,1,0:T(8,128)(2,1)S(1)} %add_convert_fusion.2), channel_id=1, source_target_pairs={{0,12},{1,13},{2,14},{3,15},{4,8},{5,9},{6,10},{7,11},{8,4},{9,5},... | collective-permute-start | bytes 1572872 | tf_op jit(solution)/shard_map/ppermute | solution.py:41
  28.3 11.8 %collective-permute-start.9 = (bf16[3,14,16,512]{3,2,1,0:T(8,128)(2,1)S(1)}, bf16[3,14,16,512]{3,2,1,0:T(8,128)(2,1)S(1)}, u32[]{:S(2)}, u32[]{:S(2)}) collective-permute-start(bf16[3,14,16,512]{3,2,1,0:T(8,128)(2,1)S(1)} %get-tuple-element.41), channel_id=1, source_target_pairs={{0,32},{1,33},{2,34},{3,35},{4,36},{5,37},{6,38},{7,39},{8,40},{9,... | collective-permute-start | bytes 2064392 | tf_op jit(solution)/shard_map/ppermute | solution.py:41
  39.2 6.5 %collective-permute-start.14 = (bf16[2,128,512]{2,1,0:T(8,128)(2,1)S(1)}, bf16[2,128,512]{2,1,0:T(8,128)(2,1)S(1)}, u32[]{:S(2)}, u32[]{:S(2)}) collective-permute-start(bf16[2,128,512]{2,1,0:T(8,128)(2,1)S(1)} %slice.46), channel_id=1, source_target_pairs={{0,1},{1,0},{2,3},{3,2},{4,5},{5,4},{6,7},{7,6},{8,9},{9,8},{10,11... | collective-permute-start | bytes 786440 | tf_op jit(solution)/shard_map/ppermute | solution.py:41
  39.6 12.1 %collective-permute-start.10 = (bf16[3,14,16,512]{3,2,1,0:T(8,128)(2,1)S(1)}, bf16[3,14,16,512]{3,2,1,0:T(8,128)(2,1)S(1)}, u32[]{:S(2)}, u32[]{:S(2)}) collective-permute-start(bf16[3,14,16,512]{3,2,1,0:T(8,128)(2,1)S(1)} %add_convert_fusion), channel_id=1, source_target_pairs={{0,96},{1,97},{2,98},{3,99},{4,100},{5,101},{6,102},{7,103},{8,104... | collective-permute-start | bytes 2064392 | tf_op jit(solution)/shard_map/ppermute | solution.py:41
  40.0 7.3 %collective-permute-start.7 = (bf16[2,128,512]{2,1,0:T(8,128)(2,1)S(1)}, bf16[2,128,512]{2,1,0:T(8,128)(2,1)S(1)}, u32[]{:S(2)}, u32[]{:S(2)}) collective-permute-start(bf16[2,128,512]{2,1,0:T(8,128)(2,1)S(1)} %slice.41), channel_id=1, source_target_pairs={{0,4},{1,5},{2,6},{3,7},{4,0},{5,1},{6,2},{7,3},{8,12},{9,13},{10,... | collective-permute-start | bytes 786440 | tf_op jit(solution)/shard_map/ppermute | solution.py:41
  45.7 7.9 %collective-permute-start.15 = (bf16[128,512]{1,0:T(8,128)(2,1)S(1)}, bf16[128,512]{1,0:T(8,128)(2,1)S(1)}, u32[]{:S(2)}, u32[]{:S(2)}) collective-permute-start(bf16[128,512]{1,0:T(8,128)(2,1)S(1)} %fusion.3), channel_id=1, source_target_pairs={{0,3},{1,2},{2,1},{3,0},{4,7},{5,6},{6,5},{7,4},{8,11},{9,10},{10,... | collective-permute-start | bytes 393224 | tf_op jit(solution)/shard_map/ppermute | solution.py:41
  47.3 6.3 %collective-permute-start.8 = (bf16[128,512]{1,0:T(8,128)(2,1)S(1)}, bf16[128,512]{1,0:T(8,128)(2,1)S(1)}, u32[]{:S(2)}, u32[]{:S(2)}) collective-permute-start(bf16[128,512]{1,0:T(8,128)(2,1)S(1)} %fusion.2), channel_id=1, source_target_pairs={{0,12},{1,13},{2,14},{3,15},{4,8},{5,9},{6,10},{7,11},{8,4},{9,5},... | collective-permute-start | bytes 393224 | tf_op jit(solution)/shard_map/ppermute | solution.py:41

commit v6 on v5

--- a/solution.py
+++ b/solution.py
@@ -154,10 +154,7 @@
     return jnp.concatenate([act0[a, r].reshape(64, TOK), act1[a, r].reshape(64, TOK)], axis=1)
 
 
-def grads_kernel(lin, lout, h0, h1, d0, act0, act1, d1_in, keeps, passes, own, after_next, d1, sem):
-    copy = pltpu.make_async_copy(d1_in, d1, sem)
-    copy.start()
-
+def grads_kernel(lin, lout, h0, h1, d0, d1, act0, act1, keeps, passes, own, after_next):
     def put(g, r, rows):
         for q, dst in enumerate((keeps, passes, own, after_next)):
             dst[g, r] = rows[q * 16 : (q + 1) * 16]
@@ -168,8 +165,6 @@
         g = dot(dgu, hx).astype(BF16)
         put(0, r, g[:64])
         put(1, r, g[64:])
-
-    copy.wait()
 
     for r in range(ROWS):
         dob = pair_rows(gather_cols(d0, lout, r), gather_cols(d1, lout, r))
@@ -232,16 +227,15 @@
 GRADS = V((3, ROWS, 16, W), BF16)
 
 
-def grads_call(lin, lout, h0, h1, d0, act0, act1, d1):
+def grads_call(lin, lout, *arrays):
     return pl.pallas_call(
         grads_kernel,
-        in_specs=[IN_SMEM] * 2 + [IN_VMEM] * 5 + [ANYWHERE],
+        in_specs=[IN_SMEM] * 2 + [IN_VMEM] * 6,
         out_specs=[IN_VMEM] * 4,
         out_shape=[GRADS] * 4,
-        scratch_shapes=[V((TOK, D), BF16), pltpu.SemaphoreType.DMA],
-        compiler_params=pltpu.CompilerParams(vmem_limit_bytes=6 * 2**20),
+        compiler_params=pltpu.CompilerParams(vmem_limit_bytes=4 * 2**20),
         cost_estimate=pl.CostEstimate(flops=10**10, bytes_accessed=128 * 2**20, transcendentals=0),
-    )(lin, lout, *in_vmem(h0, h1, d0, act0, act1), d1)
+    )(lin, lout, *in_vmem(*arrays))
 
 
 def finish_call(*arrays):
@@ -278,7 +272,7 @@
     p1, q1 = send(p_passes, "x", 0), send(q_passes, "y", 0)
     p1k, q1k = send(p_keeps, "x", 0), send(q_keeps, "y", 0)
     g_keeps, g_passes, g_own, g_next = grads_call(
-        in_layout, out_layout, h_own, h_other, d_own, keep, taken, d_other
+        in_layout, out_layout, h_own, h_other, d_own, d_other, keep, taken
     )
     g1 = send(g_passes, "z", 0)
     g1k = send(g_keeps, "z", 0)

time: 55.3 us -> 54.7 us (0.989)
  no operation moved by 1% of the time
where the time goes in v6:
time: 54.7 us; the launch traced here: 54.4 us
  starting transfers between devices  18.7 us (34%)
  waiting for transfers between devices  18.5 us (34%)
  Pallas kernels  13.9 us (25%)
  other arithmetic  2.52 us (5%)
  between operations  0.74 us (1%)
    ppermute x16, starting transfers between devices, send(): return lax.ppermute(a, AXES, pairs(axis, step))  18.7 us
    ppermute x16, waiting for transfers between devices, send(): return lax.ppermute(a, AXES, pairs(axis, step))  18.5 us
    pallas_call x1, Pallas kernels, main_call(): pl.pallas_call(main_kernel, in_specs=[IN_SMEM] + [ANYWHERE] * 7, out_spec...  7.96 us
    pallas_call x1, Pallas kernels, grads_call(): pl.pallas_call(grads_kernel, in_specs=[IN_SMEM] * 2 + [IN_VMEM] * 6, out_...  4.18 us
    convert_element_type x9, other arithmetic, add(): return sum((t.astype(F32) for t in terms)).astype(BF16)  2.44 us
    pallas_call x1, Pallas kernels, finish_call(): pl.pallas_call(finish_kernel, in_specs=[IN_VMEM] * 3, out_specs=[IN_VMEM]...  1.8 us
  transfers between devices with their start and end apart: 16, of which 5 were waited for; matrix products, arithmetic and copies ran while one was open for 2% of the time, Pallas kernels for 26%

profile of v6, /device:TPU:0, one launch (start us, length us, event | category | flops | bytes accessed | tf_op | source)
XLA Modules:
  0.0 54.4 jit_solution(7083138743350422029)
XLA Ops:
  0.6 0.1 collective-permute-start.3
  0.7 0.5 collective-permute-start.4
  1.2 0.1 pad_add_fusion.pos
  1.3 8.0 %shard_map.110 = (bf16[3,14,4,16,128]{4,3,2,1,0:T(8,128)(2,1)S(1)}, bf16[3,14,4,16,128]{4,3,2,1,0:T(8,128)(2,1)S(1)}, bf16[4,128,512]{2,1,0:T(8,128)(2,1)S(1)}, ...) custom-call(s32[4]{0:T(128)S(1)} %pad_add_fusion.pos, ...), custom_call_target="tpu_custom_call" | custom-call | bytes 24576 | tf_op jit(solution)/shard_map/pallas_call | solution.py:212
  9.3 0.2 collective-permute-start.5
  9.4 1.6 %collective-permute-start.1 = (bf16[4,128,512]{2,1,0:T(8,128)(2,1)S(1)}, bf16[4,128,512]{2,1,0:T(8,128)(2,1)S(1)}, u32[]{:S(2)}, u32[]{:S(2)}) collective-permute-start(bf16[4,128,512]{2,1,0:T(8,128)(2,1)S(1)} %get-tuple-element.32), channel_id=1, source_target_pairs={{0,1},{1,0},{2,3},{3,2},{4,5},{5,4},{6,7},{7,6},{8,9},{9,8},{10,11... | collective-permute-start | bytes 1572872 | tf_op jit(solution)/shard_map/ppermute | solution.py:41
  11.0 1.6 %collective-permute-start.12 = (bf16[4,128,512]{2,1,0:T(8,128)(2,1)S(1)}, bf16[4,128,512]{2,1,0:T(8,128)(2,1)S(1)}, u32[]{:S(2)}, u32[]{:S(2)}) collective-permute-start(bf16[4,128,512]{2,1,0:T(8,128)(2,1)S(1)} %get-tuple-element.47), channel_id=1, source_target_pairs={{0,4},{1,5},{2,6},{3,7},{4,0},{5,1},{6,2},{7,3},{8,12},{9,13},{10,... | collective-permute-start | bytes 1572872 | tf_op jit(solution)/shard_map/ppermute | solution.py:41
  12.6 4.2 %shard_map.111 = (bf16[3,14,16,512]{3,2,1,0:T(8,128)(2,1)S(1)}, bf16[3,14,16,512]{3,2,1,0:T(8,128)(2,1)S(1)}, bf16[3,14,16,512]{3,2,1,0:T(8,128)(2,1)S(1)}, bf16[3,14,16,512]{3,2,1,0:T(8,128)(2,1)S(1)}) custom-call(s32[4,14]{1,0:T(4,128)S(1)} %bitcast.19, s32[4,14]{1,0:T(4,128)S(1)} %bitcast.21, bf16[128,8192]{1,0:T(8,128)(2,1)S(1)} %get-tuple-element.33.h0, ...), custom_call_target="tpu_custom_call" | custom-call | flops 10000000000 | bytes 134217728 | tf_op jit(solution)/shard_map/pallas_call | solution.py:231
  16.8 2.0 %collective-permute-start.6 = (bf16[3,14,16,512]{3,2,1,0:T(8,128)(2,1)S(1)}, bf16[3,14,16,512]{3,2,1,0:T(8,128)(2,1)S(1)}, u32[]{:S(2)}, u32[]{:S(2)}) collective-permute-start(bf16[3,14,16,512]{3,2,1,0:T(8,128)(2,1)S(1)} %get-tuple-element.38), channel_id=1, source_target_pairs={{0,32},{1,33},{2,34},{3,35},{4,36},{5,37},{6,38},{7,39},{8,40},{9,... | collective-permute-start | bytes 2064392 | tf_op jit(solution)/shard_map/ppermute | solution.py:41
  18.8 0.5 collective-permute-start
  19.3 1.5 %collective-permute-start.11 = (bf16[4,128,512]{2,1,0:T(8,128)(2,1)S(1)}, bf16[4,128,512]{2,1,0:T(8,128)(2,1)S(1)}, u32[]{:S(2)}, u32[]{:S(2)}) collective-permute-start(bf16[4,128,512]{2,1,0:T(8,128)(2,1)S(1)} %get-tuple-element.45), channel_id=1, source_target_pairs={{0,4},{1,5},{2,6},{3,7},{4,0},{5,1},{6,2},{7,3},{8,12},{9,13},{10,... | collective-permute-start | bytes 1572872 | tf_op jit(solution)/shard_map/ppermute | solution.py:41
  20.8 0.1 add_convert_fusion.4
  21.0 2.2 %collective-permute-start.2 = (bf16[4,128,512]{2,1,0:T(8,128)(2,1)S(1)}, bf16[4,128,512]{2,1,0:T(8,128)(2,1)S(1)}, u32[]{:S(2)}, u32[]{:S(2)}) collective-permute-start(bf16[4,128,512]{2,1,0:T(8,128)(2,1)S(1)} %add_convert_fusion.4), channel_id=1, source_target_pairs={{0,3},{1,2},{2,1},{3,0},{4,7},{5,6},{6,5},{7,4},{8,11},{9,10},{10,... | collective-permute-start | bytes 1572872 | tf_op jit(solution)/shard_map/ppermute | solution.py:41
  23.1 0.1 add_convert_fusion.2
  23.3 2.7 %collective-permute-start.13 = (bf16[4,128,512]{2,1,0:T(8,128)(2,1)S(1)}, bf16[4,128,512]{2,1,0:T(8,128)(2,1)S(1)}, u32[]{:S(2)}, u32[]{:S(2)}) collective-permute-start(bf16[4,128,512]{2,1,0:T(8,128)(2,1)S(1)} %add_convert_fusion.2), channel_id=1, source_target_pairs={{0,12},{1,13},{2,14},{3,15},{4,8},{5,9},{6,10},{7,11},{8,4},{9,5},... | collective-permute-start | bytes 1572872 | tf_op jit(solution)/shard_map/ppermute | solution.py:41
  26.0 1.8 %collective-permute-done.6 = bf16[3,14,16,512]{3,2,1,0:T(8,128)(2,1)S(1)} collective-permute-done((bf16[3,14,16,512]{3,2,1,0:T(8,128)(2,1)S(1)}, bf16[3,14,16,512]{3,2,1,0:T(8,128)(2,1)S(1)}, u32[]{:S(2)}, u32[]{:S(2)}) %collective-permute-start.6) | collective-permute-done | bytes 688160 | tf_op jit(solution)/shard_map/ppermute | solution.py:41
  27.8 1.9 %collective-permute-start.9 = (bf16[3,14,16,512]{3,2,1,0:T(8,128)(2,1)S(1)}, bf16[3,14,16,512]{3,2,1,0:T(8,128)(2,1)S(1)}, u32[]{:S(2)}, u32[]{:S(2)}) collective-permute-start(bf16[3,14,16,512]{3,2,1,0:T(8,128)(2,1)S(1)} %get-tuple-element.41), channel_id=1, source_target_pairs={{0,32},{1,33},{2,34},{3,35},{4,36},{5,37},{6,38},{7,39},{8,40},{9,... | collective-permute-start | bytes 2064392 | tf_op jit(solution)/shard_map/ppermute | solution.py:41
  29.7 0.3 add_convert_fusion
  30.0 5.9 %collective-permute-done.2 = bf16[4,128,512]{2,1,0:T(8,128)(2,1)S(1)} collective-permute-done((bf16[4,128,512]{2,1,0:T(8,128)(2,1)S(1)}, bf16[4,128,512]{2,1,0:T(8,128)(2,1)S(1)}, u32[]{:S(2)}, u32[]{:S(2)}) %collective-permute-start.2) | collective-permute-done | bytes 524320 | tf_op jit(solution)/shard_map/ppermute | solution.py:41
  35.9 0.2 add_convert_fusion.3
  36.1 2.3 %collective-permute-done.13 = bf16[4,128,512]{2,1,0:T(8,128)(2,1)S(1)} collective-permute-done((bf16[4,128,512]{2,1,0:T(8,128)(2,1)S(1)}, bf16[4,128,512]{2,1,0:T(8,128)(2,1)S(1)}, u32[]{:S(2)}, u32[]{:S(2)}) %collective-permute-start.13) | collective-permute-done | bytes 524320 | tf_op jit(solution)/shard_map/ppermute | solution.py:41
  38.4 0.2 add_convert_fusion.1
  38.7 0.4 collective-permute-start.14
  39.0 0.4 collective-permute-start.10
  39.4 0.1 collective-permute-start.7
  39.5 5.6 %collective-permute-done.14 = bf16[2,128,512]{2,1,0:T(8,128)(2,1)S(1)} collective-permute-done((bf16[2,128,512]{2,1,0:T(8,128)(2,1)S(1)}, bf16[2,128,512]{2,1,0:T(8,128)(2,1)S(1)}, u32[]{:S(2)}, u32[]{:S(2)}) %collective-permute-start.14) | collective-permute-done | bytes 262176 | tf_op jit(solution)/shard_map/ppermute | solution.py:41
  45.2 1.6 %collective-permute-start.15 = (bf16[128,512]{1,0:T(8,128)(2,1)S(1)}, bf16[128,512]{1,0:T(8,128)(2,1)S(1)}, u32[]{:S(2)}, u32[]{:S(2)}) collective-permute-start(bf16[128,512]{1,0:T(8,128)(2,1)S(1)} %fusion.3), channel_id=1, source_target_pairs={{0,3},{1,2},{2,1},{3,0},{4,7},{5,6},{6,5},{7,4},{8,11},{9,10},{10,... | collective-permute-start | bytes 393224 | tf_op jit(solution)/shard_map/ppermute | solution.py:41
  46.8 1.6 %collective-permute-start.8 = (bf16[128,512]{1,0:T(8,128)(2,1)S(1)}, bf16[128,512]{1,0:T(8,128)(2,1)S(1)}, u32[]{:S(2)}, u32[]{:S(2)}) collective-permute-start(bf16[128,512]{1,0:T(8,128)(2,1)S(1)} %fusion.2), channel_id=1, source_target_pairs={{0,12},{1,13},{2,14},{3,15},{4,8},{5,9},{6,10},{7,11},{8,4},{9,5},... | collective-permute-start | bytes 393224 | tf_op jit(solution)/shard_map/ppermute | solution.py:41
  48.4 2.8 %collective-permute-done.10.r2 = bf16[3,14,16,512]{3,2,1,0:T(8,128)(2,1)S(1)} collective-permute-done((bf16[3,14,16,512]{3,2,1,0:T(8,128)(2,1)S(1)}, bf16[3,14,16,512]{3,2,1,0:T(8,128)(2,1)S(1)}, u32[]{:S(2)}, u32[]{:S(2)}) %collective-permute-start.10) | collective-permute-done | bytes 688160 | tf_op jit(solution)/shard_map/ppermute | solution.py:41
  51.2 1.8 %shard_map.112 = (f32[14,8192]{1,0:T(8,128)}, f32[14,8192]{1,0:T(8,128)}, f32[14,8192]{1,0:T(8,128)}) custom-call(bf16[3,14,16,512]{3,2,1,0:T(8,128)(2,1)S(1)} %get-tuple-element.40.own, bf16[3,14,16,512]{3,2,1,0:T(8,128)(2,1)S(1)} %collective-permute-done.9.r1, bf16[3,14,16,512]{3,2,1,0:T(8,128)(2,1)S(1)} %collective-permute-done.10.r2), custom_call_target="tpu_custom_call" | custom-call | flops 1000000000 | bytes 6291456 | tf_op jit(solution)/shard_map/pallas_call | solution.py:243
  53.0 0.7 %fusion = bf16[128,512]{1,0:T(8,128)(2,1)} fusion(bf16[128,512]{1,0:T(8,128)(2,1)S(1)} %collective-permute-done.15, bf16[2,128,512]{2,1,0:T(8,128)(2,1)S(1)} %collective-permute-done.14, bf16[4,128,512]{2,1,0:T(8,128)(2,1)S(1)} %add_convert_fusion.1), kind=kLoop, calls=%fused_computation.6 | loop fusion | flops 393216 | bytes 524288 | tf_op jit(solution)/shard_map/convert_element_type | solution.py:255
  53.7 0.7 %fusion.1 = bf16[128,512]{1,0:T(8,128)(2,1)} fusion(bf16[128,512]{1,0:T(8,128)(2,1)S(1)} %collective-permute-done.8, bf16[2,128,512]{2,1,0:T(8,128)(2,1)S(1)} %collective-permute-done.7, bf16[4,128,512]{2,1,0:T(8,128)(2,1)S(1)} %add_convert_fusion.3), kind=kLoop, calls=%fused_computation.8 | loop fusion | flops 393216 | bytes 524288 | tf_op jit(solution)/shard_map/convert_element_type | solution.py:255
  (19 shorter events, 0.2 us)
Async XLA Ops:
  0.6 12.0 %collective-permute-start.3 = (bf16[128,8192]{1,0:T(8,128)(2,1)}, bf16[128,8192]{1,0:T(8,128)(2,1)S(1)}, u32[]{:S(2)}, u32[]{:S(2)}) collective-permute-start(bf16[128,8192]{1,0:T(8,128)(2,1)} %h_hbm.1), channel_id=1, source_target_pairs={{0,16},{1,17},{2,18},{3,19},{4,20},{5,21},{6,22},{7,23},{8,24},{9,... | collective-permute-start | bytes 6291464 | tf_op jit(solution)/shard_map/ppermute | solution.py:41
  0.7 11.9 %collective-permute-start.4 = (bf16[128,8192]{1,0:T(8,128)(2,1)}, bf16[128,8192]{1,0:T(8,128)(2,1)}, u32[]{:S(2)}, u32[]{:S(2)}) collective-permute-start(bf16[128,8192]{1,0:T(8,128)(2,1)} %d_hbm.1), channel_id=1, source_target_pairs={{0,16},{1,17},{2,18},{3,19},{4,20},{5,21},{6,22},{7,23},{8,24},{9,... | collective-permute-start | bytes 6291464 | tf_op jit(solution)/shard_map/ppermute | solution.py:41
  1.3 11.3 %copy-start = (s32[14,4]{0,1:T(4,128)S(1)}, s32[14,4]{0,1:T(4,128)}, u32[]{:S(2)}) copy-start(s32[14,4]{0,1:T(4,128)} %param.12) | copy-start | bytes 676
  1.3 11.3 %copy-start.1 = (s32[14,4]{0,1:T(4,128)S(1)}, s32[14,4]{0,1:T(4,128)}, u32[]{:S(2)}) copy-start(s32[14,4]{0,1:T(4,128)} %param.13) | copy-start | bytes 676
  9.3 3.3 %collective-permute-start.5 = (bf16[3,14,4,16,128]{4,3,2,1,0:T(8,128)(2,1)S(1)}, bf16[3,14,4,16,128]{4,3,2,1,0:T(8,128)(2,1)S(1)}, u32[]{:S(2)}, u32[]{:S(2)}) collective-permute-start(bf16[3,14,4,16,128]{4,3,2,1,0:T(8,128)(2,1)S(1)} %get-tuple-element.36), channel_id=1, source_target_pairs={{0,16},{1,17},{2,18},{3,19},{4,20},{5,21},{6,22},{7,23},{8,24},{9,... | collective-permute-start | bytes 2064392 | tf_op jit(solution)/shard_map/ppermute | solution.py:41
  9.4 11.4 %collective-permute-start.1 = (bf16[4,128,512]{2,1,0:T(8,128)(2,1)S(1)}, bf16[4,128,512]{2,1,0:T(8,128)(2,1)S(1)}, u32[]{:S(2)}, u32[]{:S(2)}) collective-permute-start(bf16[4,128,512]{2,1,0:T(8,128)(2,1)S(1)} %get-tuple-element.32), channel_id=1, source_target_pairs={{0,1},{1,0},{2,3},{3,2},{4,5},{5,4},{6,7},{7,6},{8,9},{9,8},{10,11... | collective-permute-start | bytes 1572872 | tf_op jit(solution)/shard_map/ppermute | solution.py:41
  11.0 12.1 %collective-permute-start.12 = (bf16[4,128,512]{2,1,0:T(8,128)(2,1)S(1)}, bf16[4,128,512]{2,1,0:T(8,128)(2,1)S(1)}, u32[]{:S(2)}, u32[]{:S(2)}) collective-permute-start(bf16[4,128,512]{2,1,0:T(8,128)(2,1)S(1)} %get-tuple-element.47), channel_id=1, source_target_pairs={{0,4},{1,5},{2,6},{3,7},{4,0},{5,1},{6,2},{7,3},{8,12},{9,13},{10,... | collective-permute-start | bytes 1572872 | tf_op jit(solution)/shard_map/ppermute | solution.py:41
  16.8 11.0 %collective-permute-start.6 = (bf16[3,14,16,512]{3,2,1,0:T(8,128)(2,1)S(1)}, bf16[3,14,16,512]{3,2,1,0:T(8,128)(2,1)S(1)}, u32[]{:S(2)}, u32[]{:S(2)}) collective-permute-start(bf16[3,14,16,512]{3,2,1,0:T(8,128)(2,1)S(1)} %get-tuple-element.38), channel_id=1, source_target_pairs={{0,32},{1,33},{2,34},{3,35},{4,36},{5,37},{6,38},{7,39},{8,40},{9,... | collective-permute-start | bytes 2064392 | tf_op jit(solution)/shard_map/ppermute | solution.py:41
  18.8 17.1 %collective-permute-start = (bf16[4,128,512]{2,1,0:T(8,128)(2,1)S(1)}, bf16[4,128,512]{2,1,0:T(8,128)(2,1)S(1)}, u32[]{:S(2)}, u32[]{:S(2)}) collective-permute-start(bf16[4,128,512]{2,1,0:T(8,128)(2,1)S(1)} %get-tuple-element.30), channel_id=1, source_target_pairs={{0,1},{1,0},{2,3},{3,2},{4,5},{5,4},{6,7},{7,6},{8,9},{9,8},{10,11... | collective-permute-start | bytes 1572872 | tf_op jit(solution)/shard_map/ppermute | solution.py:41
  19.3 19.1 %collective-permute-start.11 = (bf16[4,128,512]{2,1,0:T(8,128)(2,1)S(1)}, bf16[4,128,512]{2,1,0:T(8,128)(2,1)S(1)}, u32[]{:S(2)}, u32[]{:S(2)}) collective-permute-start(bf16[4,128,512]{2,1,0:T(8,128)(2,1)S(1)} %get-tuple-element.45), channel_id=1, source_target_pairs={{0,4},{1,5},{2,6},{3,7},{4,0},{5,1},{6,2},{7,3},{8,12},{9,13},{10,... | collective-permute-start | bytes 1572872 | tf_op jit(solution)/shard_map/ppermute | solution.py:41
  21.0 14.9 %collective-permute-start.2 = (bf16[4,128,512]{2,1,0:T(8,128)(2,1)S(1)}, bf16[4,128,512]{2,1,0:T(8,128)(2,1)S(1)}, u32[]{:S(2)}, u32[]{:S(2)}) collective-permute-start(bf16[4,128,512]{2,1,0:T(8,128)(2,1)S(1)} %add_convert_fusion.4), channel_id=1, source_target_pairs={{0,3},{1,2},{2,1},{3,0},{4,7},{5,6},{6,5},{7,4},{8,11},{9,10},{10,... | collective-permute-start | bytes 1572872 | tf_op jit(solution)/shard_map/ppermute | solution.py:41
  23.3 15.1 %collective-permute-start.13 = (bf16[4,128,512]{2,1,0:T(8,128)(2,1)S(1)}, bf16[4,128,512]{2,1,0:T(8,128)(2,1)S(1)}, u32[]{:S(2)}, u32[]{:S(2)}) collective-permute-start(bf16[4,128,512]{2,1,0:T(8,128)(2,1)S(1)} %add_convert_fusion.2), channel_id=1, source_target_pairs={{0,12},{1,13},{2,14},{3,15},{4,8},{5,9},{6,10},{7,11},{8,4},{9,5},... | collective-permute-start | bytes 1572872 | tf_op jit(solution)/shard_map/ppermute | solution.py:41
  27.8 11.7 %collective-permute-start.9 = (bf16[3,14,16,512]{3,2,1,0:T(8,128)(2,1)S(1)}, bf16[3,14,16,512]{3,2,1,0:T(8,128)(2,1)S(1)}, u32[]{:S(2)}, u32[]{:S(2)}) collective-permute-start(bf16[3,14,16,512]{3,2,1,0:T(8,128)(2,1)S(1)} %get-tuple-element.41), channel_id=1, source_target_pairs={{0,32},{1,33},{2,34},{3,35},{4,36},{5,37},{6,38},{7,39},{8,40},{9,... | collective-permute-start | bytes 2064392 | tf_op jit(solution)/shard_map/ppermute | solution.py:41
  38.7 6.5 %collective-permute-start.14 = (bf16[2,128,512]{2,1,0:T(8,128)(2,1)S(1)}, bf16[2,128,512]{2,1,0:T(8,128)(2,1)S(1)}, u32[]{:S(2)}, u32[]{:S(2)}) collective-permute-start(bf16[2,128,512]{2,1,0:T(8,128)(2,1)S(1)} %slice.46), channel_id=1, source_target_pairs={{0,1},{1,0},{2,3},{3,2},{4,5},{5,4},{6,7},{7,6},{8,9},{9,8},{10,11... | collective-permute-start | bytes 786440 | tf_op jit(solution)/shard_map/ppermute | solution.py:41
  39.0 12.1 %collective-permute-start.10 = (bf16[3,14,16,512]{3,2,1,0:T(8,128)(2,1)S(1)}, bf16[3,14,16,512]{3,2,1,0:T(8,128)(2,1)S(1)}, u32[]{:S(2)}, u32[]{:S(2)}) collective-permute-start(bf16[3,14,16,512]{3,2,1,0:T(8,128)(2,1)S(1)} %add_convert_fusion), channel_id=1, source_target_pairs={{0,96},{1,97},{2,98},{3,99},{4,100},{5,101},{6,102},{7,103},{8,104... | collective-permute-start | bytes 2064392 | tf_op jit(solution)/shard_map/ppermute | solution.py:41
  39.4 7.3 %collective-permute-start.7 = (bf16[2,128,512]{2,1,0:T(8,128)(2,1)S(1)}, bf16[2,128,512]{2,1,0:T(8,128)(2,1)S(1)}, u32[]{:S(2)}, u32[]{:S(2)}) collective-permute-start(bf16[2,128,512]{2,1,0:T(8,128)(2,1)S(1)} %slice.41), channel_id=1, source_target_pairs={{0,4},{1,5},{2,6},{3,7},{4,0},{5,1},{6,2},{7,3},{8,12},{9,13},{10,... | collective-permute-start | bytes 786440 | tf_op jit(solution)/shard_map/ppermute | solution.py:41
  45.2 7.8 %collective-permute-start.15 = (bf16[128,512]{1,0:T(8,128)(2,1)S(1)}, bf16[128,512]{1,0:T(8,128)(2,1)S(1)}, u32[]{:S(2)}, u32[]{:S(2)}) collective-permute-start(bf16[128,512]{1,0:T(8,128)(2,1)S(1)} %fusion.3), channel_id=1, source_target_pairs={{0,3},{1,2},{2,1},{3,0},{4,7},{5,6},{6,5},{7,4},{8,11},{9,10},{10,... | collective-permute-start | bytes 393224 | tf_op jit(solution)/shard_map/ppermute | solution.py:41
  46.8 6.3 %collective-permute-start.8 = (bf16[128,512]{1,0:T(8,128)(2,1)S(1)}, bf16[128,512]{1,0:T(8,128)(2,1)S(1)}, u32[]{:S(2)}, u32[]{:S(2)}) collective-permute-start(bf16[128,512]{1,0:T(8,128)(2,1)S(1)} %fusion.2), channel_id=1, source_target_pairs={{0,12},{1,13},{2,14},{3,15},{4,8},{5,9},{6,10},{7,11},{8,4},{9,5},... | collective-permute-start | bytes 393224 | tf_op jit(solution)/shard_map/ppermute | solution.py:41

commit v7 on v6

--- a/solution.py
+++ b/solution.py
@@ -248,6 +248,23 @@
         scratch_shapes=[V((KB, ROWS * 16, BLK), F32)],
         compiler_params=pltpu.CompilerParams(vmem_limit_bytes=8 * 2**20),
         cost_estimate=pl.CostEstimate(flops=10**9, bytes_accessed=6 * 2**20, transcendentals=0),
+    )(*in_vmem(*arrays))
+
+
+def last_kernel(p_mid, p3, p4, q_mid, q3, q4, out, dh):
+    out[...] = add(p_mid[2], p3[0], p4[...])
+    dh[...] = add(q_mid[2], q3[0], q4[...])
+
+
+def last_call(*arrays):
+    out = jax.ShapeDtypeStruct((TOK, W), BF16)
+    return pl.pallas_call(
+        last_kernel,
+        in_specs=[IN_VMEM] * 6,
+        out_specs=[IN_VMEM] * 2,
+        out_shape=[out] * 2,
+        compiler_params=pltpu.CompilerParams(vmem_limit_bytes=4 * 2**20),
+        cost_estimate=cost(1),
     )(*in_vmem(*arrays))
 
 
@@ -287,8 +304,7 @@
     p4 = send(add(p_mid[3], p3[1]), "y", 1)
     q4 = send(add(q_mid[3], after(q3, g1k)[1]), "x", 1)
     g_gate, g_up, g_down = finish_call(g_own, g1k, g2)
-    out = add(p_mid[2], p3[0], after(p4, g_down))
-    dh = add(q_mid[2], q3[0], after(q4, g_down))
+    out, dh = last_call(p_mid, p3, after(p4, g_down), q_mid, q3, q4)
     return (out, dh, g_gate, g_up, g_down)
 
 

time: 54.7 us -> 53.9 us (0.985)
  starting transfers between devices: 18.7 us -> 20.5 us
  waiting for transfers between devices: 18.5 us -> 16.8 us
  other arithmetic: 2.52 us -> 1.1 us
  Pallas kernels: 13.9 us -> 14.7 us
    ppermute x16, starting transfers between devices: 18.7 us -> 20.5 us  [send(): return lax.ppermute(a, AXES, pairs(axis, step))]
    ppermute x16, waiting for transfers between devices: 18.5 us -> 16.8 us  [send(): return lax.ppermute(a, AXES, pairs(axis, step))]
    convert_element_type x9 -> x7, other arithmetic: 2.44 us -> 1.03 us  [add(): return sum((t.astype(F32) for t in terms)).astype(BF16)]
    pallas_call x0 -> x1, Pallas kernels: none -> 0.76 us  [last_call(): pl.pallas_call(last_kernel, in_specs=[IN_VMEM] * 6, out_specs=[IN_VMEM] *...]
where the time goes in v7:
time: 53.9 us; the launch traced here: 53.8 us
  starting transfers between devices  20.5 us (38%)
  waiting for transfers between devices  16.8 us (31%)
  Pallas kernels  14.7 us (27%)
  other arithmetic  1.1 us (2%)
  between operations  0.75 us (1%)
    ppermute x16, starting transfers between devices, send(): return lax.ppermute(a, AXES, pairs(axis, step))  20.5 us
    ppermute x16, waiting for transfers between devices, send(): return lax.ppermute(a, AXES, pairs(axis, step))  16.8 us
    pallas_call x1, Pallas kernels, main_call(): pl.pallas_call(main_kernel, in_specs=[IN_SMEM] + [ANYWHERE] * 7, out_spec...  7.94 us
    pallas_call x1, Pallas kernels, grads_call(): pl.pallas_call(grads_kernel, in_specs=[IN_SMEM] * 2 + [IN_VMEM] * 6, out_...  4.17 us
    pallas_call x1, Pallas kernels, finish_call(): pl.pallas_call(finish_kernel, in_specs=[IN_VMEM] * 3, out_specs=[IN_VMEM]...  1.79 us
  transfers between devices with their start and end apart: 16, of which 5 were waited for; matrix products, arithmetic and copies ran while one was open for 2% of the time, Pallas kernels for 26%

profile of v7, /device:TPU:0, one launch (start us, length us, event | category | flops | bytes accessed | tf_op | source)
XLA Modules:
  0.0 53.8 jit_solution(2932302807600319004)
XLA Ops:
  0.6 0.1 collective-permute-start.3
  0.7 0.5 collective-permute-start.4
  1.2 0.1 pad_add_fusion.pos
  1.3 7.9 %shard_map.110 = (bf16[3,14,4,16,128]{4,3,2,1,0:T(8,128)(2,1)S(1)}, bf16[3,14,4,16,128]{4,3,2,1,0:T(8,128)(2,1)S(1)}, bf16[4,128,512]{2,1,0:T(8,128)(2,1)S(1)}, ...) custom-call(s32[4]{0:T(128)S(1)} %pad_add_fusion.pos, ...), custom_call_target="tpu_custom_call" | custom-call | bytes 24576 | tf_op jit(solution)/shard_map/pallas_call | solution.py:212
  9.2 0.2 collective-permute-start.5
  9.4 1.6 %collective-permute-start.1 = (bf16[4,128,512]{2,1,0:T(8,128)(2,1)S(1)}, bf16[4,128,512]{2,1,0:T(8,128)(2,1)S(1)}, u32[]{:S(2)}, u32[]{:S(2)}) collective-permute-start(bf16[4,128,512]{2,1,0:T(8,128)(2,1)S(1)} %get-tuple-element.33), channel_id=1, source_target_pairs={{0,1},{1,0},{2,3},{3,2},{4,5},{5,4},{6,7},{7,6},{8,9},{9,8},{10,11... | collective-permute-start | bytes 1572872 | tf_op jit(solution)/shard_map/ppermute | solution.py:41
  11.0 1.6 %collective-permute-start.12 = (bf16[4,128,512]{2,1,0:T(8,128)(2,1)S(1)}, bf16[4,128,512]{2,1,0:T(8,128)(2,1)S(1)}, u32[]{:S(2)}, u32[]{:S(2)}) collective-permute-start(bf16[4,128,512]{2,1,0:T(8,128)(2,1)S(1)} %get-tuple-element.48), channel_id=1, source_target_pairs={{0,4},{1,5},{2,6},{3,7},{4,0},{5,1},{6,2},{7,3},{8,12},{9,13},{10,... | collective-permute-start | bytes 1572872 | tf_op jit(solution)/shard_map/ppermute | solution.py:41
  12.6 4.2 %shard_map.111 = (bf16[3,14,16,512]{3,2,1,0:T(8,128)(2,1)S(1)}, bf16[3,14,16,512]{3,2,1,0:T(8,128)(2,1)S(1)}, bf16[3,14,16,512]{3,2,1,0:T(8,128)(2,1)S(1)}, bf16[3,14,16,512]{3,2,1,0:T(8,128)(2,1)S(1)}) custom-call(s32[4,14]{1,0:T(4,128)S(1)} %bitcast.11, s32[4,14]{1,0:T(4,128)S(1)} %bitcast.13, bf16[128,8192]{1,0:T(8,128)(2,1)S(1)} %get-tuple-element.34.h0, ...), custom_call_target="tpu_custom_call" | custom-call | flops 10000000000 | bytes 134217728 | tf_op jit(solution)/shard_map/pallas_call | solution.py:231
  16.8 2.0 %collective-permute-start.6 = (bf16[3,14,16,512]{3,2,1,0:T(8,128)(2,1)S(1)}, bf16[3,14,16,512]{3,2,1,0:T(8,128)(2,1)S(1)}, u32[]{:S(2)}, u32[]{:S(2)}) collective-permute-start(bf16[3,14,16,512]{3,2,1,0:T(8,128)(2,1)S(1)} %get-tuple-element.39), channel_id=1, source_target_pairs={{0,32},{1,33},{2,34},{3,35},{4,36},{5,37},{6,38},{7,39},{8,40},{9,... | collective-permute-start | bytes 2064392 | tf_op jit(solution)/shard_map/ppermute | solution.py:41
  18.8 0.6 %collective-permute-start = (bf16[4,128,512]{2,1,0:T(8,128)(2,1)S(1)}, bf16[4,128,512]{2,1,0:T(8,128)(2,1)S(1)}, u32[]{:S(2)}, u32[]{:S(2)}) collective-permute-start(bf16[4,128,512]{2,1,0:T(8,128)(2,1)S(1)} %get-tuple-element.31), channel_id=1, source_target_pairs={{0,1},{1,0},{2,3},{3,2},{4,5},{5,4},{6,7},{7,6},{8,9},{9,8},{10,11... | collective-permute-start | bytes 1572872 | tf_op jit(solution)/shard_map/ppermute | solution.py:41
  19.3 1.5 %collective-permute-start.11 = (bf16[4,128,512]{2,1,0:T(8,128)(2,1)S(1)}, bf16[4,128,512]{2,1,0:T(8,128)(2,1)S(1)}, u32[]{:S(2)}, u32[]{:S(2)}) collective-permute-start(bf16[4,128,512]{2,1,0:T(8,128)(2,1)S(1)} %get-tuple-element.46), channel_id=1, source_target_pairs={{0,4},{1,5},{2,6},{3,7},{4,0},{5,1},{6,2},{7,3},{8,12},{9,13},{10,... | collective-permute-start | bytes 1572872 | tf_op jit(solution)/shard_map/ppermute | solution.py:41
  20.8 0.0 collective-permute-done.1
  20.8 0.1 add_convert_fusion.4
  21.0 2.2 %collective-permute-start.2 = (bf16[4,128,512]{2,1,0:T(8,128)(2,1)S(1)}, bf16[4,128,512]{2,1,0:T(8,128)(2,1)S(1)}, u32[]{:S(2)}, u32[]{:S(2)}) collective-permute-start(bf16[4,128,512]{2,1,0:T(8,128)(2,1)S(1)} %add_convert_fusion.4), channel_id=1, source_target_pairs={{0,3},{1,2},{2,1},{3,0},{4,7},{5,6},{6,5},{7,4},{8,11},{9,10},{10,... | collective-permute-start | bytes 1572872 | tf_op jit(solution)/shard_map/ppermute | solution.py:41
  23.1 0.1 add_convert_fusion.2
  23.3 2.7 %collective-permute-start.13 = (bf16[4,128,512]{2,1,0:T(8,128)(2,1)S(1)}, bf16[4,128,512]{2,1,0:T(8,128)(2,1)S(1)}, u32[]{:S(2)}, u32[]{:S(2)}) collective-permute-start(bf16[4,128,512]{2,1,0:T(8,128)(2,1)S(1)} %add_convert_fusion.2), channel_id=1, source_target_pairs={{0,12},{1,13},{2,14},{3,15},{4,8},{5,9},{6,10},{7,11},{8,4},{9,5},... | collective-permute-start | bytes 1572872 | tf_op jit(solution)/shard_map/ppermute | solution.py:41
  26.0 1.8 %collective-permute-done.6 = bf16[3,14,16,512]{3,2,1,0:T(8,128)(2,1)S(1)} collective-permute-done((bf16[3,14,16,512]{3,2,1,0:T(8,128)(2,1)S(1)}, bf16[3,14,16,512]{3,2,1,0:T(8,128)(2,1)S(1)}, u32[]{:S(2)}, u32[]{:S(2)}) %collective-permute-start.6) | collective-permute-done | bytes 688160 | tf_op jit(solution)/shard_map/ppermute | solution.py:41
  27.8 1.9 %collective-permute-start.9 = (bf16[3,14,16,512]{3,2,1,0:T(8,128)(2,1)S(1)}, bf16[3,14,16,512]{3,2,1,0:T(8,128)(2,1)S(1)}, u32[]{:S(2)}, u32[]{:S(2)}) collective-permute-start(bf16[3,14,16,512]{3,2,1,0:T(8,128)(2,1)S(1)} %get-tuple-element.42), channel_id=1, source_target_pairs={{0,32},{1,33},{2,34},{3,35},{4,36},{5,37},{6,38},{7,39},{8,40},{9,... | collective-permute-start | bytes 2064392 | tf_op jit(solution)/shard_map/ppermute | solution.py:41
  29.7 0.3 add_convert_fusion
  30.0 5.9 %collective-permute-done.2 = bf16[4,128,512]{2,1,0:T(8,128)(2,1)S(1)} collective-permute-done((bf16[4,128,512]{2,1,0:T(8,128)(2,1)S(1)}, bf16[4,128,512]{2,1,0:T(8,128)(2,1)S(1)}, u32[]{:S(2)}, u32[]{:S(2)}) %collective-permute-start.2) | collective-permute-done | bytes 524320 | tf_op jit(solution)/shard_map/ppermute | solution.py:41
  35.9 2.7 %collective-permute-start.10 = (bf16[3,14,16,512]{3,2,1,0:T(8,128)(2,1)S(1)}, bf16[3,14,16,512]{3,2,1,0:T(8,128)(2,1)S(1)}, u32[]{:S(2)}, u32[]{:S(2)}) collective-permute-start(bf16[3,14,16,512]{3,2,1,0:T(8,128)(2,1)S(1)} %add_convert_fusion), channel_id=1, source_target_pairs={{0,96},{1,97},{2,98},{3,99},{4,100},{5,101},{6,102},{7,103},{8,104... | collective-permute-start | bytes 2064392 | tf_op jit(solution)/shard_map/ppermute | solution.py:41
  38.6 0.2 add_convert_fusion.3.p_mid
  38.8 0.2 collective-permute-start.7
  39.1 0.2 add_convert_fusion.1.q_mid
  39.3 0.1 collective-permute-start.14
  39.4 5.9 %collective-permute-done.7.p3 = bf16[2,128,512]{2,1,0:T(8,128)(2,1)S(1)} collective-permute-done((bf16[2,128,512]{2,1,0:T(8,128)(2,1)S(1)}, bf16[2,128,512]{2,1,0:T(8,128)(2,1)S(1)}, u32[]{:S(2)}, u32[]{:S(2)}) %collective-permute-start.7) | collective-permute-done | bytes 262176 | tf_op jit(solution)/shard_map/ppermute | solution.py:41
  45.3 1.4 %collective-permute-start.8 = (bf16[128,512]{1,0:T(8,128)(2,1)S(1)}, bf16[128,512]{1,0:T(8,128)(2,1)S(1)}, u32[]{:S(2)}, u32[]{:S(2)}) collective-permute-start(bf16[128,512]{1,0:T(8,128)(2,1)S(1)} %fusion), channel_id=1, source_target_pairs={{0,12},{1,13},{2,14},{3,15},{4,8},{5,9},{6,10},{7,11},{8,4},{9,5},... | collective-permute-start | bytes 393224 | tf_op jit(solution)/shard_map/ppermute | solution.py:41
  46.8 1.3 %collective-permute-start.15 = (bf16[128,512]{1,0:T(8,128)(2,1)S(1)}, bf16[128,512]{1,0:T(8,128)(2,1)S(1)}, u32[]{:S(2)}, u32[]{:S(2)}) collective-permute-start(bf16[128,512]{1,0:T(8,128)(2,1)S(1)} %fusion.1), channel_id=1, source_target_pairs={{0,3},{1,2},{2,1},{3,0},{4,7},{5,6},{6,5},{7,4},{8,11},{9,10},{10,... | collective-permute-start | bytes 393224 | tf_op jit(solution)/shard_map/ppermute | solution.py:41
  48.1 2.3 %collective-permute-done.10.r2 = bf16[3,14,16,512]{3,2,1,0:T(8,128)(2,1)S(1)} collective-permute-done((bf16[3,14,16,512]{3,2,1,0:T(8,128)(2,1)S(1)}, bf16[3,14,16,512]{3,2,1,0:T(8,128)(2,1)S(1)}, u32[]{:S(2)}, u32[]{:S(2)}) %collective-permute-start.10) | collective-permute-done | bytes 688160 | tf_op jit(solution)/shard_map/ppermute | solution.py:41
  50.3 1.8 %shard_map.112 = (f32[14,8192]{1,0:T(8,128)}, f32[14,8192]{1,0:T(8,128)}, f32[14,8192]{1,0:T(8,128)}) custom-call(bf16[3,14,16,512]{3,2,1,0:T(8,128)(2,1)S(1)} %get-tuple-element.41.own, bf16[3,14,16,512]{3,2,1,0:T(8,128)(2,1)S(1)} %collective-permute-done.9.r1, bf16[3,14,16,512]{3,2,1,0:T(8,128)(2,1)S(1)} %collective-permute-done.10.r2), custom_call_target="tpu_custom_call" | custom-call | flops 1000000000 | bytes 6291456 | tf_op jit(solution)/shard_map/pallas_call | solution.py:243
  52.1 0.9 %collective-permute-done.15.q4 = bf16[128,512]{1,0:T(8,128)(2,1)S(1)} collective-permute-done((bf16[128,512]{1,0:T(8,128)(2,1)S(1)}, bf16[128,512]{1,0:T(8,128)(2,1)S(1)}, u32[]{:S(2)}, u32[]{:S(2)}) %collective-permute-start.15) | collective-permute-done | bytes 131104 | tf_op jit(solution)/shard_map/ppermute | solution.py:41
  53.0 0.8 %shard_map.113 = (bf16[128,512]{1,0:T(8,128)(2,1)}, bf16[128,512]{1,0:T(8,128)(2,1)}) custom-call(bf16[4,128,512]{2,1,0:T(8,128)(2,1)S(1)} %add_convert_fusion.3.p_mid, bf16[2,128,512]{2,1,0:T(8,128)(2,1)S(1)} %collective-permute-done.7.p3, bf16[128,512]{1,0:T(8,128)(2,1)S(1)} %collective-permute-done.8.p4, ...), custom_call_target="tpu_custom_call" | custom-call | bytes 1024 | tf_op jit(solution)/shard_map/pallas_call | solution.py:261
  (18 shorter events, 0.1 us)
Async XLA Ops:
  0.6 11.9 %collective-permute-start.3 = (bf16[128,8192]{1,0:T(8,128)(2,1)}, bf16[128,8192]{1,0:T(8,128)(2,1)S(1)}, u32[]{:S(2)}, u32[]{:S(2)}) collective-permute-start(bf16[128,8192]{1,0:T(8,128)(2,1)} %h_hbm.1), channel_id=1, source_target_pairs={{0,16},{1,17},{2,18},{3,19},{4,20},{5,21},{6,22},{7,23},{8,24},{9,... | collective-permute-start | bytes 6291464 | tf_op jit(solution)/shard_map/ppermute | solution.py:41
  0.7 11.9 %collective-permute-start.4 = (bf16[128,8192]{1,0:T(8,128)(2,1)}, bf16[128,8192]{1,0:T(8,128)(2,1)}, u32[]{:S(2)}, u32[]{:S(2)}) collective-permute-start(bf16[128,8192]{1,0:T(8,128)(2,1)} %d_hbm.1), channel_id=1, source_target_pairs={{0,16},{1,17},{2,18},{3,19},{4,20},{5,21},{6,22},{7,23},{8,24},{9,... | collective-permute-start | bytes 6291464 | tf_op jit(solution)/shard_map/ppermute | solution.py:41
  1.3 11.3 %copy-start = (s32[14,4]{0,1:T(4,128)S(1)}, s32[14,4]{0,1:T(4,128)}, u32[]{:S(2)}) copy-start(s32[14,4]{0,1:T(4,128)} %param.12) | copy-start | bytes 676
  1.3 11.3 %copy-start.1 = (s32[14,4]{0,1:T(4,128)S(1)}, s32[14,4]{0,1:T(4,128)}, u32[]{:S(2)}) copy-start(s32[14,4]{0,1:T(4,128)} %param.13) | copy-start | bytes 676
  9.2 3.3 %collective-permute-start.5 = (bf16[3,14,4,16,128]{4,3,2,1,0:T(8,128)(2,1)S(1)}, bf16[3,14,4,16,128]{4,3,2,1,0:T(8,128)(2,1)S(1)}, u32[]{:S(2)}, u32[]{:S(2)}) collective-permute-start(bf16[3,14,4,16,128]{4,3,2,1,0:T(8,128)(2,1)S(1)} %get-tuple-element.37), channel_id=1, source_target_pairs={{0,16},{1,17},{2,18},{3,19},{4,20},{5,21},{6,22},{7,23},{8,24},{9,... | collective-permute-start | bytes 2064392 | tf_op jit(solution)/shard_map/ppermute | solution.py:41
  9.4 11.4 %collective-permute-start.1 = (bf16[4,128,512]{2,1,0:T(8,128)(2,1)S(1)}, bf16[4,128,512]{2,1,0:T(8,128)(2,1)S(1)}, u32[]{:S(2)}, u32[]{:S(2)}) collective-permute-start(bf16[4,128,512]{2,1,0:T(8,128)(2,1)S(1)} %get-tuple-element.33), channel_id=1, source_target_pairs={{0,1},{1,0},{2,3},{3,2},{4,5},{5,4},{6,7},{7,6},{8,9},{9,8},{10,11... | collective-permute-start | bytes 1572872 | tf_op jit(solution)/shard_map/ppermute | solution.py:41
  11.0 12.1 %collective-permute-start.12 = (bf16[4,128,512]{2,1,0:T(8,128)(2,1)S(1)}, bf16[4,128,512]{2,1,0:T(8,128)(2,1)S(1)}, u32[]{:S(2)}, u32[]{:S(2)}) collective-permute-start(bf16[4,128,512]{2,1,0:T(8,128)(2,1)S(1)} %get-tuple-element.48), channel_id=1, source_target_pairs={{0,4},{1,5},{2,6},{3,7},{4,0},{5,1},{6,2},{7,3},{8,12},{9,13},{10,... | collective-permute-start | bytes 1572872 | tf_op jit(solution)/shard_map/ppermute | solution.py:41
  16.8 11.0 %collective-permute-start.6 = (bf16[3,14,16,512]{3,2,1,0:T(8,128)(2,1)S(1)}, bf16[3,14,16,512]{3,2,1,0:T(8,128)(2,1)S(1)}, u32[]{:S(2)}, u32[]{:S(2)}) collective-permute-start(bf16[3,14,16,512]{3,2,1,0:T(8,128)(2,1)S(1)} %get-tuple-element.39), channel_id=1, source_target_pairs={{0,32},{1,33},{2,34},{3,35},{4,36},{5,37},{6,38},{7,39},{8,40},{9,... | collective-permute-start | bytes 2064392 | tf_op jit(solution)/shard_map/ppermute | solution.py:41
  18.8 19.8 %collective-permute-start = (bf16[4,128,512]{2,1,0:T(8,128)(2,1)S(1)}, bf16[4,128,512]{2,1,0:T(8,128)(2,1)S(1)}, u32[]{:S(2)}, u32[]{:S(2)}) collective-permute-start(bf16[4,128,512]{2,1,0:T(8,128)(2,1)S(1)} %get-tuple-element.31), channel_id=1, source_target_pairs={{0,1},{1,0},{2,3},{3,2},{4,5},{5,4},{6,7},{7,6},{8,9},{9,8},{10,11... | collective-permute-start | bytes 1572872 | tf_op jit(solution)/shard_map/ppermute | solution.py:41
  19.3 19.7 %collective-permute-start.11 = (bf16[4,128,512]{2,1,0:T(8,128)(2,1)S(1)}, bf16[4,128,512]{2,1,0:T(8,128)(2,1)S(1)}, u32[]{:S(2)}, u32[]{:S(2)}) collective-permute-start(bf16[4,128,512]{2,1,0:T(8,128)(2,1)S(1)} %get-tuple-element.46), channel_id=1, source_target_pairs={{0,4},{1,5},{2,6},{3,7},{4,0},{5,1},{6,2},{7,3},{8,12},{9,13},{10,... | collective-permute-start | bytes 1572872 | tf_op jit(solution)/shard_map/ppermute | solution.py:41
  21.0 14.9 %collective-permute-start.2 = (bf16[4,128,512]{2,1,0:T(8,128)(2,1)S(1)}, bf16[4,128,512]{2,1,0:T(8,128)(2,1)S(1)}, u32[]{:S(2)}, u32[]{:S(2)}) collective-permute-start(bf16[4,128,512]{2,1,0:T(8,128)(2,1)S(1)} %add_convert_fusion.4), channel_id=1, source_target_pairs={{0,3},{1,2},{2,1},{3,0},{4,7},{5,6},{6,5},{7,4},{8,11},{9,10},{10,... | collective-permute-start | bytes 1572872 | tf_op jit(solution)/shard_map/ppermute | solution.py:41
  23.3 15.5 %collective-permute-start.13 = (bf16[4,128,512]{2,1,0:T(8,128)(2,1)S(1)}, bf16[4,128,512]{2,1,0:T(8,128)(2,1)S(1)}, u32[]{:S(2)}, u32[]{:S(2)}) collective-permute-start(bf16[4,128,512]{2,1,0:T(8,128)(2,1)S(1)} %add_convert_fusion.2), channel_id=1, source_target_pairs={{0,12},{1,13},{2,14},{3,15},{4,8},{5,9},{6,10},{7,11},{8,4},{9,5},... | collective-permute-start | bytes 1572872 | tf_op jit(solution)/shard_map/ppermute | solution.py:41
  27.8 19.0 %collective-permute-start.9 = (bf16[3,14,16,512]{3,2,1,0:T(8,128)(2,1)S(1)}, bf16[3,14,16,512]{3,2,1,0:T(8,128)(2,1)S(1)}, u32[]{:S(2)}, u32[]{:S(2)}) collective-permute-start(bf16[3,14,16,512]{3,2,1,0:T(8,128)(2,1)S(1)} %get-tuple-element.42), channel_id=1, source_target_pairs={{0,32},{1,33},{2,34},{3,35},{4,36},{5,37},{6,38},{7,39},{8,40},{9,... | collective-permute-start | bytes 2064392 | tf_op jit(solution)/shard_map/ppermute | solution.py:41
  35.9 14.5 %collective-permute-start.10 = (bf16[3,14,16,512]{3,2,1,0:T(8,128)(2,1)S(1)}, bf16[3,14,16,512]{3,2,1,0:T(8,128)(2,1)S(1)}, u32[]{:S(2)}, u32[]{:S(2)}) collective-permute-start(bf16[3,14,16,512]{3,2,1,0:T(8,128)(2,1)S(1)} %add_convert_fusion), channel_id=1, source_target_pairs={{0,96},{1,97},{2,98},{3,99},{4,100},{5,101},{6,102},{7,103},{8,104... | collective-permute-start | bytes 2064392 | tf_op jit(solution)/shard_map/ppermute | solution.py:41
  38.8 6.5 %collective-permute-start.7 = (bf16[2,128,512]{2,1,0:T(8,128)(2,1)S(1)}, bf16[2,128,512]{2,1,0:T(8,128)(2,1)S(1)}, u32[]{:S(2)}, u32[]{:S(2)}) collective-permute-start(bf16[2,128,512]{2,1,0:T(8,128)(2,1)S(1)} %slice.24), channel_id=1, source_target_pairs={{0,4},{1,5},{2,6},{3,7},{4,0},{5,1},{6,2},{7,3},{8,12},{9,13},{10,... | collective-permute-start | bytes 786440 | tf_op jit(solution)/shard_map/ppermute | solution.py:41
  39.3 7.4 %collective-permute-start.14 = (bf16[2,128,512]{2,1,0:T(8,128)(2,1)S(1)}, bf16[2,128,512]{2,1,0:T(8,128)(2,1)S(1)}, u32[]{:S(2)}, u32[]{:S(2)}) collective-permute-start(bf16[2,128,512]{2,1,0:T(8,128)(2,1)S(1)} %slice.27), channel_id=1, source_target_pairs={{0,1},{1,0},{2,3},{3,2},{4,5},{5,4},{6,7},{7,6},{8,9},{9,8},{10,11... | collective-permute-start | bytes 786440 | tf_op jit(solution)/shard_map/ppermute | solution.py:41
  45.3 6.8 %collective-permute-start.8 = (bf16[128,512]{1,0:T(8,128)(2,1)S(1)}, bf16[128,512]{1,0:T(8,128)(2,1)S(1)}, u32[]{:S(2)}, u32[]{:S(2)}) collective-permute-start(bf16[128,512]{1,0:T(8,128)(2,1)S(1)} %fusion), channel_id=1, source_target_pairs={{0,12},{1,13},{2,14},{3,15},{4,8},{5,9},{6,10},{7,11},{8,4},{9,5},... | collective-permute-start | bytes 393224 | tf_op jit(solution)/shard_map/ppermute | solution.py:41
  46.8 6.3 %collective-permute-start.15 = (bf16[128,512]{1,0:T(8,128)(2,1)S(1)}, bf16[128,512]{1,0:T(8,128)(2,1)S(1)}, u32[]{:S(2)}, u32[]{:S(2)}) collective-permute-start(bf16[128,512]{1,0:T(8,128)(2,1)S(1)} %fusion.1), channel_id=1, source_target_pairs={{0,3},{1,2},{2,1},{3,0},{4,7},{5,6},{6,5},{7,4},{8,11},{9,10},{10,... | collective-permute-start | bytes 393224 | tf_op jit(solution)/shard_map/ppermute | solution.py:41
